TPU v7x, 512 devices: a whole 4x4x16 slice. The times are simulated.
512 devices in a mesh: dp: 64 (over z, y), corpus: 8 (over x, core).
Axes of the slice: x: 4, y: 4, z: 16, core: 2. Of those that a mesh axis runs over, the one named last changes fastest.
Arguments:
- queries: bfloat16 [65536, 1024], P(('dp', 'corpus')), may hold values from -6 to 6
- passages: bfloat16 [196608, 1024], P(('dp', 'corpus')), may hold values from -6 to 6
- weight: bfloat16 [1024, 1024], replicated, may hold values from -0.1875 to 0.1875
- pairs: int32 [512, 8], P(('dp', 'corpus')), may hold values from 0 to 23, as said below
- positive: int32 [65536], P(('dp', 'corpus')), may hold values from 0 to 1023
Outputs:
- losses: float32 [65536], P(('dp', 'corpus'))
- query_grad: bfloat16 [65536, 1024], P(('dp', 'corpus'))
- passage_grad: bfloat16 [196608, 1024], P(('dp', 'corpus'))
- weight_grad: float32 [1024, 1024], P('dp')
Inputs may be any that keep to these rules, and one draw needn't show every extreme that they name: `pairs`: each row lists 8 distinct blocks of its own data-parallel group; block b of a group sits on corpus shard b // 3 of that group as its block b % 3. No shard holds more than 2 of a row's blocks, and in every row some shard holds exactly 2 of them. `positive`: index into the tile's 8 * 128 candidate passages, in the order of the tile's row of pairs.
All inputs are finite; a program needn't handle non-finite values.
Results may differ from a plain program's by a relative error of at most 0.0057.
Values may be sent and summed in bfloat16 or wider, within the bound.
No kernel may reach another device: no remote copies, remote signals or barrier semaphores. Data moves between devices by JAX's collectives and lax.ppermute only.
A program may use at most 64 MiB of HBM per device.

v0:
```python
import jax
import jax.numpy as jnp
from jax import lax
from jax.sharding import PartitionSpec as P

CAP = 2


score_scale = 50.0
epsilon = 1e-06


def normalize(proj):
    return proj * lax.rsqrt(jnp.sum(proj * proj, axis=-1, keepdims=True) + epsilon)


def project_back(proj_back, weight):
    return lax.dot_general(
        proj_back, weight, (((1,), (1,)), ((), ())), preferred_element_type=jnp.float32
    ).astype(jnp.bfloat16)


def body(queries, passages, weight, pairs, positive):
    tile_rows = queries.shape[0]
    feature_width = queries.shape[1]
    shards = lax.axis_size("corpus")
    blocks_dev = passages.shape[0] // tile_rows
    block_count = pairs.shape[1]
    slot_total = shards * CAP
    query_proj = jnp.dot(queries, weight, preferred_element_type=jnp.float32)
    passage_proj = jnp.dot(passages, weight, preferred_element_type=jnp.float32)
    query_emb = normalize(query_proj).astype(jnp.bfloat16)
    passage_emb = normalize(passage_proj).astype(jnp.bfloat16)
    named_blocks = pairs[0]
    owner_shard = named_blocks // blocks_dev
    local_block = named_blocks % blocks_dev
    positions = jnp.arange(block_count, dtype=jnp.int32)
    earlier_same = (owner_shard[None, :] == owner_shard[:, None]) & (
        positions[None, :] < positions[:, None]
    )
    slot_rank = jnp.sum(earlier_same.astype(jnp.int32), axis=1)
    slot_index = owner_shard * CAP + slot_rank
    slot_match = slot_index[:, None] == jnp.arange(slot_total, dtype=jnp.int32)[None, :]
    wanted = jnp.sum(jnp.where(slot_match, local_block[:, None] + 1, 0), axis=0) - 1
    served = lax.all_to_all(
        wanted.reshape(shards, CAP), "corpus", split_axis=0, concat_axis=0, tiled=True
    )
    own_blocks = passage_emb.reshape(blocks_dev, tile_rows, feature_width)
    served_valid = served >= 0
    outgoing = jnp.where(
        served_valid[:, :, None, None],
        own_blocks[jnp.maximum(served, 0)],
        jnp.zeros((), jnp.bfloat16),
    )
    arrived = lax.all_to_all(outgoing, "corpus", split_axis=0, concat_axis=0, tiled=True)
    candidates = arrived.reshape(slot_total, tile_rows, feature_width)[slot_index].reshape(
        block_count * tile_rows, feature_width
    )
    scores = (
        lax.dot_general(
            query_emb, candidates, (((1,), (1,)), ((), ())), preferred_element_type=jnp.float32
        )
        * score_scale
    )
    exponent = jnp.exp(scores)
    exp_total = jnp.sum(exponent, axis=1)
    picked = jnp.take_along_axis(scores, positive[:, None], axis=1)[:, 0]
    losses = jnp.log(exp_total) - picked
    column = jnp.arange(block_count * tile_rows, dtype=jnp.int32)
    target = (column[None, :] == positive[:, None]).astype(jnp.float32)
    dscore = (exponent / exp_total[:, None] - target).astype(jnp.bfloat16)
    query_grad = jnp.dot(dscore, candidates, preferred_element_type=jnp.float32) * score_scale
    served_hit = (
        served[:, :, None] == jnp.arange(blocks_dev, dtype=jnp.int32)[None, None, :]
    ).astype(jnp.bfloat16)
    served_hit = served_hit.reshape(slot_total, blocks_dev)
    block_term = (
        lax.dot_general(
            dscore, query_emb, (((0,), (0,)), ((), ())), preferred_element_type=jnp.float32
        )
        * score_scale
    )
    block_term = block_term.astype(jnp.bfloat16).reshape(block_count, tile_rows * feature_width)
    placed = lax.dot_general(
        slot_match.astype(jnp.bfloat16),
        block_term,
        (((0,), (0,)), ((), ())),
        preferred_element_type=jnp.float32,
    ).astype(jnp.bfloat16)
    returned = lax.all_to_all(
        placed.reshape(shards, CAP, tile_rows, feature_width),
        "corpus",
        split_axis=0,
        concat_axis=0,
        tiled=True,
    )
    block_terms = returned.reshape(slot_total, tile_rows * feature_width)
    passage_emb_grad = lax.dot_general(
        served_hit, block_terms, (((0,), (0,)), ((), ())), preferred_element_type=jnp.float32
    )
    passage_emb_grad = passage_emb_grad.reshape(blocks_dev * tile_rows, feature_width)
    query_back = jax.vjp(normalize, query_proj)[1](query_grad)[0].astype(jnp.bfloat16)
    passage_back = jax.vjp(normalize, passage_proj)[1](passage_emb_grad)[0].astype(jnp.bfloat16)
    query_hidden = project_back(query_back, weight)
    passage_hidden = project_back(passage_back, weight)
    weight_term = lax.dot_general(
        queries, query_back, (((0,), (0,)), ((), ())), preferred_element_type=jnp.float32
    )
    weight_term = weight_term + lax.dot_general(
        passages, passage_back, (((0,), (0,)), ((), ())), preferred_element_type=jnp.float32
    )
    row_sums = lax.psum_scatter(weight_term, "dp", scatter_dimension=0, tiled=True)
    weight_sum = lax.psum(row_sums, "corpus")
    tile_total = lax.axis_size("dp") * lax.axis_size("corpus")
    return (losses, query_hidden, passage_hidden, weight_sum / float(tile_total))


def solution(mesh):
    placed = (
        P(("dp", "corpus"), None),
        P(("dp", "corpus"), None),
        P(),
        P(("dp", "corpus"), None),
        P(("dp", "corpus")),
    )
    return jax.shard_map(
        body,
        mesh=mesh,
        in_specs=placed,
        out_specs=(
            P(("dp", "corpus")),
            P(("dp", "corpus"), None),
            P(("dp", "corpus"), None),
            P("dp", None),
        ),
        check_vma=False,
    )
```

profile of v0, /device:TPU:1, one launch (start us, length us, event | category | flops | bytes accessed | tf_op | source)
XLA Modules:
  0.0 966.5 jit_solution(11538083506561642701)
XLA Ops:
  7.2 0.8 fusion.6
  8.0 0.7 fusion.7
  8.7 0.2 convert_reduce_fusion
  8.9 0.1 select_reduce_fusion
  9.0 0.7 sub.22
  9.6 10.1 %all-to-all-start = ((s32[8,1,2]{2,1,0:T(1,128)}), s32[8,1,2]{2,1,0:T(1,128)S(1)}, u32[]{:S(2)}, u32[]{:S(2)}) async-start(s32[8,1,2]{2,1,0:T(1,128)} %bitcast.4), calls=%async_computation | async-start | bytes 8192 | tf_op jit(solution)/shard_map/all_to_all | solution.py:45
  19.7 2.2 multiply_reduce_fusion.1
  21.9 1.1 copy-done.2
  23.1 0.1 multiply_convert_fusion.1
  23.2 1.0 all-to-all-done
  24.2 0.5 broadcast.296
  24.8 0.7 fusion.15
  25.4 0.1 reshape.233
  25.5 0.1 copy.20
  25.6 0.1 copy.21
  25.7 2.8 gather_fusion
  28.6 4.6 broadcast_select_fusion
  33.1 5.3 all-to-all-start.1
  38.4 0.5 multiply_reduce_fusion.3
  39.0 48.3 %all-to-all-done.1 = bf16[8,2,128,1024]{3,2,1,0:T(8,128)(2,1)} async-done(((bf16[8,2,128,1024]{3,2,1,0:T(8,128)(2,1)}), bf16[8,2,128,1024]{3,2,1,0:T(8,128)(2,1)}, u32[]{:S(2)}, u32[]{:S(2)}) %all-to-all-start.1) | async-done | bytes 4194336 | tf_op jit(solution)/shard_map/all_to_all | solution.py:55
  87.3 4.2 gather_fusion.1
  91.5 2.5 exponential_reduce_fusion
  94.1 2.2 multiply_convert_fusion
  96.2 3.9 reshape.227
  100.1 2.9 convolution_convert_fusion
  103.0 4.4 copy.25
  107.5 5.3 all-to-all-start.2
  112.8 0.1 eq.69
  112.8 2.2 multiply_reduce_fusion.2
  115.1 0.2 fusion.1
  115.2 2.7 fusion.16
  118.0 43.7 %all-to-all-done.2 = bf16[8,2,128,1024]{3,2,1,0:T(8,128)(2,1)} async-done(((bf16[8,2,128,1024]{3,2,1,0:T(8,128)(2,1)}), bf16[8,2,128,1024]{3,2,1,0:T(8,128)(2,1)}, u32[]{:S(2)}, u32[]{:S(2)}) %all-to-all-start.2) | async-done | bytes 4194336 | tf_op jit(solution)/shard_map/all_to_all | solution.py:90
  161.7 4.5 copy.26
  166.2 2.2 fusion.2
  168.4 4.0 reshape.230
  172.4 2.3 multiply_reduce_fusion
  174.7 2.3 fusion
  176.9 3.3 add_bitcast_fusion
  180.3 5.3 copy.23
  185.7 2.1 gather_fusion.2
  187.9 0.5 fusion.9
  188.4 1.6 convolution_convert_fusion.2
  190.0 682.7 %reduce-scatter.4.cloned.1.call-done = f32[16,1024]{1,0:T(8,128)} async-done(((f32[1024,1024]{1,0:T(8,128)}), f32[16,1024]{1,0:T(8,128)}) %reduce-scatter.4.cloned.1.call-update) | async-done | bytes 65552
  872.6 1.8 copy.24
  874.5 1.9 convolution_convert_fusion.1
  876.4 81.4 %all-reduce.2.cloned.1.call-done = f32[16,1024]{0,1:T(8,128)} async-done(((f32[16,1024]{0,1:T(8,128)}), f32[16,1024]{0,1:T(8,128)}) %all-reduce.2.cloned.1.call-update) | async-done | bytes 65552 | tf_op jit(solution)/shard_map/psum | solution.py:113
  957.8 1.1 broadcast_multiply_fusion
  958.9 0.8 copy.22
  (33 shorter events, 0.2 us)
Async XLA Ops:
  7.2 12.6 %copy-start = (bf16[1024,1024]{1,0:T(8,128)(2,1)S(1)}, bf16[1024,1024]{1,0:T(8,128)(2,1)}, u32[]{:S(2)}) copy-start(bf16[1024,1024]{1,0:T(8,128)(2,1)} %param.7) | copy-start | bytes 6291460
  9.6 14.6 %all-to-all-start = ((s32[8,1,2]{2,1,0:T(1,128)}), s32[8,1,2]{2,1,0:T(1,128)S(1)}, u32[]{:S(2)}, u32[]{:S(2)}) async-start(s32[8,1,2]{2,1,0:T(1,128)} %bitcast.4), calls=%async_computation | async-start | bytes 8192 | tf_op jit(solution)/shard_map/all_to_all | solution.py:45
  21.9 1.2 copy-start.2
  33.1 5.3 copy-start.6
  33.1 5.3 copy-start.4
  33.1 54.2 %all-to-all-start.1 = ((bf16[8,2,128,1024]{3,2,1,0:T(8,128)(2,1)}), bf16[8,2,128,1024]{3,2,1,0:T(8,128)(2,1)}, u32[]{:S(2)}, u32[]{:S(2)}) async-start(bf16[8,2,128,1024]{3,2,1,0:T(8,128)(2,1)} %broadcast_select_fusion), calls=%async_computation.1 | async-start | bytes 8388608 | tf_op jit(solution)/shard_map/all_to_all | solution.py:55
  91.5 2.5 copy-start.7
  94.0 18.8 %copy-start.3 = (f32[128,1024]{1,0:T(8,128)}, f32[128,1024]{1,0:T(8,128)S(1)}, u32[]{:S(2)}) copy-start(f32[128,1024]{1,0:T(8,128)S(1)} %get-tuple-element.32) | copy-start | bytes 1572868
  107.5 54.2 %all-to-all-start.2 = ((bf16[8,2,128,1024]{3,2,1,0:T(8,128)(2,1)}), bf16[8,2,128,1024]{3,2,1,0:T(8,128)(2,1)}, u32[]{:S(2)}, u32[]{:S(2)}) async-start(bf16[8,2,128,1024]{3,2,1,0:T(8,128)(2,1)} %bitcast.68), calls=%async_computation.2 | async-start | bytes 8388608 | tf_op jit(solution)/shard_map/all_to_all | solution.py:90
  112.8 759.9 %reduce-scatter.4.cloned.1.call-start = ((), (), s32[]{:S(2)}) async-start(), calls=%async_computation.5 | async-start | bytes 4259840
  172.4 4.5 copy-start.1
  174.6 2.3 copy-start.5
  185.6 772.2 %all-reduce.2.cloned.1.call-start = ((), (), s32[]{:S(2)}) async-start(), calls=%async_computation.4 | async-start | bytes 1048576 | tf_op jit(solution)/shard_map/psum | solution.py:113
Sparse Core Ops, SparseCore 0:
  185.8 686.8 reduce-scatter.3
  875.1 82.7 all-reduce.1
where the time goes:
time: 968 us; the launch traced here: 967 us
  waiting for transfers between devices  857 us (89%)
  local copies, waits for them, and re-layouts  36.6 us (4%)
  matrix products  24.4 us (3%)
  starting transfers between devices  20.7 us (2%)
  between operations  14.2 us (1%)
  other arithmetic  13.5 us (1%)
    unnamed x3, waiting for transfers between devices  683 us
    psum x1, waiting for transfers between devices, body(): weight_sum = lax.psum(row_sums, 'corpus')  81.4 us
    all_to_all x1, waiting for transfers between devices, body(): lax.all_to_all(outgoing, 'corpus', split_axis=0, concat_axis=0, tiled=True)  48.3 us
    all_to_all x1, waiting for transfers between devices, body(): lax.all_to_all(placed.reshape(shards, CAP, tile_rows, feature_width), 'co...  43.7 us
  transfers between devices with their start and end apart: 5, of which 5 were waited for; matrix products, arithmetic and copies ran while one was open for 1% of the time, Pallas kernels for 0%

commit v1 on v0

v1 whole, which is shorter than its diff:
```python
import jax
import jax.numpy as jnp
from jax import lax
from jax.sharding import Mesh, PartitionSpec as P

score_scale = 50.0
epsilon = 1e-06

X, C, Y, Z = 4, 2, 4, 16
SWAP = ((0, 1), (1, 0))


def exchange(value, axis):
    return lax.all_to_all(value, axis, split_axis=0, concat_axis=0, tiled=True)


def gather(value, axis, size):
    return exchange(jnp.broadcast_to(value[None], (size,) + value.shape), axis)


def matmul(a, b):
    return jnp.dot(a, b, preferred_element_type=jnp.float32)


def matmul_tn(a, b):
    return lax.dot_general(a, b, (((0,), (0,)), ((), ())), preferred_element_type=jnp.float32)


def matmul_nt(a, b):
    return lax.dot_general(a, b, (((1,), (1,)), ((), ())), preferred_element_type=jnp.float32)


def inverse_norm(proj):
    return lax.rsqrt(jnp.sum(proj * proj, axis=-1, keepdims=True) + epsilon)


def back_of(proj, r, grad):
    inner = jnp.sum(proj * grad, axis=-1, keepdims=True)
    return (r * grad - (r * r * r * inner) * proj).astype(jnp.bfloat16)


def body(queries, passages, weight, pairs, positive):
    rows, width = queries.shape
    own_p = passages.shape[0]
    blocks = own_p // rows
    chip_blocks = blocks * C
    names = pairs.shape[1]
    x = lax.axis_index("x")
    c = lax.axis_index("c")

    tiles = gather(queries, "x", X)
    index = jnp.concatenate([positive, pairs[0], jnp.zeros((rows - names,), jnp.int32)])
    index = gather(index.reshape(2, rows), "x", X)
    sibling = lax.ppermute(passages, "c", SWAP)

    chip_passages = jnp.concatenate([passages, sibling], axis=0)
    p_proj = matmul(chip_passages, weight)
    p_r = inverse_norm(p_proj)
    p_emb = (p_proj * p_r).astype(jnp.bfloat16)

    tile_positive = index[:, 0]
    tile_pairs = index[:, 1, :names]
    local = tile_pairs - x * chip_blocks
    slot = jnp.where((local >= 0) & (local < chip_blocks), (local + blocks * c) % chip_blocks, -1)
    named = jnp.any(slot[:, :, None] == jnp.arange(chip_blocks)[None, None, :], axis=1)
    pos_name = tile_positive // rows
    pos_slot = jnp.sum(
        jnp.where(pos_name[:, :, None] == jnp.arange(names)[None, None, :], slot[:, None, :], 0), axis=2
    )
    pos_column = jnp.where(pos_slot >= 0, pos_slot * rows + tile_positive % rows, -1).reshape(-1, 1)
    column = jnp.arange(chip_blocks * rows, dtype=jnp.int32)[None, :]
    target = column == pos_column
    mask = jnp.repeat(jnp.repeat(named, rows, axis=1), rows, axis=0)

    chip_queries = tiles.reshape(X * rows, width)
    q_proj = matmul(chip_queries, weight)
    q_r = inverse_norm(q_proj)
    q_emb = (q_proj * q_r).astype(jnp.bfloat16)
    scores = matmul_nt(q_emb, p_emb) * score_scale
    exponent = jnp.where(mask, jnp.exp(scores), 0.0)
    part_total = jnp.sum(exponent, axis=1)
    part_picked = jnp.sum(jnp.where(target, scores, 0.0), axis=1)
    outgoing = jnp.concatenate(
        [
            jnp.broadcast_to(part_total.reshape(1, X, rows), (X, X, rows)),
            part_picked.reshape(X, 1, rows),
        ],
        axis=1,
    )
    sums = jnp.sum(exchange(outgoing, "x"), axis=0)
    total = sums[:X]
    own_total = jnp.sum(jnp.where((jnp.arange(X) == x)[:, None], total, 0.0), axis=0)
    losses = jnp.log(own_total) - sums[X]
    dscore = (exponent / total.reshape(-1, 1) - target.astype(jnp.float32)).astype(jnp.bfloat16)

    q_grad = matmul(dscore, p_emb) * score_scale
    p_grad = matmul_tn(dscore, q_emb) * score_scale
    q_back = back_of(q_proj, q_r, q_grad)
    p_back = back_of(p_proj, p_r, p_grad)

    half = width // C
    backs = jnp.concatenate([q_back, p_back], axis=0)
    hidden = jnp.concatenate([chip_queries, chip_passages], axis=0)
    backs_there = lax.dynamic_slice_in_dim(backs, (1 - c) * half, half, axis=1)
    backs_here = lax.dynamic_slice_in_dim(backs, c * half, half, axis=1)
    w_there = lax.ppermute(matmul_tn(hidden, backs_there).astype(jnp.bfloat16), "c", SWAP)
    w_here = matmul_tn(hidden, backs_here) + w_there.astype(jnp.float32)
    own_rows = width // (Z * Y)
    w = w_here.astype(jnp.bfloat16).reshape(Z, Y, own_rows, half).transpose(1, 0, 2, 3)
    w = jnp.sum(exchange(w, "y").astype(jnp.float32), axis=0)
    w = w.astype(jnp.bfloat16).reshape(Z, own_rows, X, half // X).transpose(2, 0, 1, 3)
    w = jnp.sum(exchange(w, "x").astype(jnp.float32), axis=0)
    w = jnp.sum(exchange(w.astype(jnp.bfloat16), "z").astype(jnp.float32), axis=0)
    w = gather(w * (1.0 / (Z * Y * X * C)), ("x", "c"), X * C)
    weight_grad = w.reshape(X, C, own_rows, half // X).transpose(2, 1, 0, 3).reshape(own_rows, width)

    q_sum = jnp.sum(
        exchange(q_grad.astype(jnp.bfloat16).reshape(X, rows, width), "x").astype(jnp.float32), axis=0
    )
    own_proj = lax.dynamic_slice_in_dim(q_proj, x * rows, rows, axis=0)
    own_r = lax.dynamic_slice_in_dim(q_r, x * rows, rows, axis=0)
    query_grad = matmul_nt(back_of(own_proj, own_r, q_sum), weight).astype(jnp.bfloat16)

    p_sum = p_grad[:own_p] + lax.ppermute(p_grad[own_p:].astype(jnp.bfloat16), "c", SWAP).astype(jnp.float32)
    passage_grad = matmul_nt(back_of(p_proj[:own_p], p_r[:own_p], p_sum), weight).astype(jnp.bfloat16)
    return losses, query_grad, passage_grad, weight_grad


def solution(mesh):
    torus = Mesh(mesh.devices.reshape(Z, Y, X, C), ("z", "y", "x", "c"))
    every = ("z", "y", "x", "c")
    return jax.shard_map(
        body,
        mesh=torus,
        in_specs=(P(every, None), P(every, None), P(), P(every, None), P(every)),
        out_specs=(P(every), P(every, None), P(every, None), P(("z", "y"), None)),
        check_vma=False,
    )
```

time: 968 us -> 162 us (0.17)
  waiting for transfers between devices: 857 us -> 48.4 us
  starting transfers between devices: 20.7 us -> 58.6 us
  local copies, waits for them, and re-layouts: 36.6 us -> 11.3 us
  between operations: 14.2 us -> 0.94 us
    unnamed x3 -> x0, waiting for transfers between devices: 683 us -> none
    psum x1 -> x0, waiting for transfers between devices: 81.4 us -> none  [body(): weight_sum = lax.psum(row_sums, 'corpus')]
    all_to_all x3 -> x8, waiting for transfers between devices: 93.1 us -> 45.8 us  [exchange(): return lax.all_to_all(value, axis, split_axis=0, concat_axis=0, tiled=True)]
    all_to_all x3 -> x8, starting transfers between devices: 20.7 us -> 42.5 us  [exchange(): return lax.all_to_all(value, axis, split_axis=0, concat_axis=0, tiled=True)]
    unnamed x22 -> x24, local copies, waits for them, and re-layouts: 18.1 us -> 1.2 us
    ppermute x0 -> x3, starting transfers between devices: none -> 16.1 us  [the longest x1 7.2 us: body(): sibling = lax.ppermute(passages, 'c', SWAP)]
    dot_general x11 -> x9, matrix products: 24.4 us -> 26.4 us  [the longest x3 9.13 us: matmul_nt(): lax.dot_general(a, b, (((1,), (1,)), ((), ())), preferred_element_type=jn...]
  transfers between devices with their start and end apart: 5 -> 11, of which waited for: 5 -> 7; matrix products, arithmetic and copies ran while one was open for 1% -> 14% of each run, Pallas kernels for 0% -> 0%
where the time goes in v1:
time: 162 us; the launch traced here: 161 us
  starting transfers between devices  58.6 us (36%)
  waiting for transfers between devices  48.4 us (30%)
  matrix products  26.4 us (16%)
  other arithmetic  15.4 us (10%)
  local copies, waits for them, and re-layouts  11.3 us (7%)
    all_to_all x8, waiting for transfers between devices, exchange(): return lax.all_to_all(value, axis, split_axis=0, concat_axis=0, tiled=True)  45.8 us
    all_to_all x8, starting transfers between devices, exchange(): return lax.all_to_all(value, axis, split_axis=0, concat_axis=0, tiled=True)  42.5 us
    dot_general x3, matrix products, matmul_nt(): lax.dot_general(a, b, (((1,), (1,)), ((), ())), preferred_element_type=jn...  9.13 us
    dot_general x3, matrix products, matmul_tn(): lax.dot_general(a, b, (((0,), (0,)), ((), ())), preferred_element_type=jn...  9.09 us
    dot_general x3, matrix products, matmul(): return jnp.dot(a, b, preferred_element_type=jnp.float32)  8.15 us
    ppermute x1, starting transfers between devices, body(): sibling = lax.ppermute(passages, 'c', SWAP)  7.2 us
    ppermute x1, starting transfers between devices, body(): lax.ppermute(matmul_tn(hidden, backs_there).astype(jnp.bfloat16), 'c', SWAP)  6.59 us
    convert_element_type x2, other arithmetic, back_of(): return (r * grad - r * r * r * inner * proj).astype(jnp.bfloat16)  3.64 us
  transfers between devices with their start and end apart: 11, of which 7 were waited for; matrix products, arithmetic and copies ran while one was open for 14% of the time, Pallas kernels for 0%

profile of v1, /device:TPU:1, one launch (start us, length us, event | category | flops | bytes accessed | tf_op | source)
XLA Modules:
  0.0 161.1 jit_solution(17916410353905067770)
XLA Ops:
  0.7 0.9 add_bitcast_fusion
  1.6 0.6 broadcast_in_dim.96
  2.1 4.8 %all-to-all-start = ((s32[4,2,128]{2,1,0:T(2,128)}), s32[4,2,128]{2,1,0:T(2,128)S(1)}, u32[]{:S(2)}, u32[]{:S(2)}) async-start(s32[4,2,128]{2,1,0:T(2,128)} %broadcast_in_dim.96), calls=%async_computation | async-start | bytes 8192 | tf_op jit(solution)/shard_map/all_to_all | solution.py:14
  7.0 7.2 %collective-permute-start = (bf16[384,1024]{1,0:T(8,128)(2,1)}, bf16[384,1024]{1,0:T(8,128)(2,1)}, u32[]{:S(2)}, u32[]{:S(2)}) collective-permute-start(bf16[384,1024]{1,0:T(8,128)(2,1)} %param.6), channel_id=1, source_target_pairs={{0,1},{1,0},{2,3},{3,2},{4,5},{5,4},{6,7},{7,6},{8,9},{9,8},{10,11... | collective-permute-start | bytes 2359304 | tf_op jit(solution)/shard_map/ppermute | solution.py:54
  14.2 2.1 %broadcast_in_dim.100 = bf16[4,128,1024]{2,1,0:T(8,128)(2,1)} broadcast(bf16[128,1024]{1,0:T(8,128)(2,1)} %param.5), dimensions={1,2} | broadcast | bytes 1310720 | tf_op jit(solution)/shard_map/broadcast_in_dim | solution.py:18
  16.3 4.5 %all-to-all-start.1 = ((bf16[4,128,1024]{2,1,0:T(8,128)(2,1)}), bf16[4,128,1024]{2,1,0:T(8,128)(2,1)S(1)}, u32[]{:S(2)}, u32[]{:S(2)}) async-start(bf16[4,128,1024]{2,1,0:T(8,128)(2,1)} %broadcast_in_dim.100), calls=%async_computation.1 | async-start | bytes 2097152 | tf_op jit(solution)/shard_map/all_to_all | solution.py:14
  20.8 0.2 fusion.13
  21.3 11.9 %all-to-all-done.1 = bf16[4,128,1024]{2,1,0:T(8,128)(2,1)S(1)} async-done(((bf16[4,128,1024]{2,1,0:T(8,128)(2,1)}), bf16[4,128,1024]{2,1,0:T(8,128)(2,1)S(1)}, u32[]{:S(2)}, u32[]{:S(2)}) %all-to-all-start.1) | async-done | bytes 1048608 | tf_op jit(solution)/shard_map/all_to_all | solution.py:14
  33.3 1.3 multiply_reduce_fusion.3
  34.6 3.6 %multiply_reduce_fusion.1 = (f32[768]{0:T(1024)S(1)}, f32[768,1024]{1,0:T(8,128)S(1)}) fusion(bf16[1024,1024]{1,0:T(8,128)(2,1)S(1)} %copy-done, bf16[384,1024]{1,0:T(8,128)(2,1)} %collective-permute-done, bf16[384,1024]{1,0:T(8,128)(2,1)S(1)} %copy-done.9), kind=kOutput, calls=%fused_computation.3 | convolution fusion | flops 1615330560 | bytes 6818816 | tf_op jit(solution)/shard_map/dot_general | solution.py:22
  38.3 2.5 %fusion.4 = (f32[512]{0:T(512)S(1)}, f32[512]{0:T(512)S(1)}, f32[512,768]{1,0:T(8,128)}) fusion(pred[4,768]{1,0:T(4,128)(4,1)S(1)} %bitcast.68, s32[512]{0:T(512)S(1)} %fusion.20, f32[768,1024]{1,0:T(8,128)S(1)} %get-tuple-element.24, f32[768]{0:T(1024)S(1)} %add_rsqrt_fusion, f32[512,1024]{1,0:T(8,128)S(1)} %get-tuple-element.22, f32[512]{0:T(512)S(1)} %add_rsqrt_fusion.1), kind=kOutput, calls=%fused_computation.32 | convolution fusion | flops 810286080 | bytes 6830080 | tf_op jit(solution)/shard_map/dot_general | solution.py:30
  40.8 0.6 pad_maximum_fusion.3
  41.4 3.3 %all-to-all-start.2 = ((f32[4,5,128]{2,1,0:T(8,128)}), f32[4,5,128]{2,1,0:T(8,128)S(1)}, u32[]{:S(2)}, u32[]{:S(2)}) async-start(f32[4,5,128]{2,1,0:T(8,128)} %pad_maximum_fusion.3), calls=%async_computation.2 | async-start | bytes 32768 | tf_op jit(solution)/shard_map/all_to_all | solution.py:14
  44.7 4.2 %all-to-all-done.2 = f32[4,5,128]{2,1,0:T(8,128)S(1)} async-done(((f32[4,5,128]{2,1,0:T(8,128)}), f32[4,5,128]{2,1,0:T(8,128)S(1)}, u32[]{:S(2)}, u32[]{:S(2)}) %all-to-all-start.2) | async-done | bytes 10272 | tf_op jit(solution)/shard_map/all_to_all | solution.py:14
  48.9 2.0 %subtract_convert_fusion.3 = bf16[512,768]{1,0:T(8,128)(2,1)S(1)} fusion(f32[512,768]{1,0:T(8,128)} %get-tuple-element.25, f32[512]{0:T(512)S(1)} %get-tuple-element.17, s32[512]{0:T(512)S(1)} %fusion.20, pred[4,768]{1,0:T(4,128)(4,1)S(1)} %bitcast.69), kind=kLoop, calls=%fused_computation.25 | loop fusion | flops 2359296 | bytes 2366464 | tf_op jit(solution)/shard_map/convert_element_type | solution.py:94
  51.0 3.2 %multiply_reduce_fusion.2 = (f32[512]{0:T(512)S(1)}, f32[512,1024]{1,0:T(8,128)S(1)}) fusion(f32[512,1024]{1,0:T(8,128)S(1)} %copy-done.4, bf16[512,768]{1,0:T(8,128)(2,1)S(1)} %subtract_convert_fusion.3, f32[768,1024]{1,0:T(8,128)} %copy-done.1, f32[768]{0:T(1024)S(1)} %add_rsqrt_fusion), kind=kOutput, calls=%fused_computation.11 | convolution fusion | flops 808451584 | bytes 8131584 | tf_op jit(solution)/shard_map/dot_general | solution.py:22
  54.2 1.2 multiply_reduce_fusion
  55.4 1.4 subtract_convert_fusion.1
  56.8 2.2 %subtract_convert_fusion = (bf16[768,1024]{1,0:T(8,128)(2,1)S(1)}, f32[768,1024]{1,0:T(8,128)}) fusion(f32[768,1024]{1,0:T(8,128)S(1)} %copy-done.2, f32[768,1024]{1,0:T(8,128)S(1)} %get-tuple-element.29, f32[768]{0:T(1024)S(1)} %get-tuple-element.16, f32[768]{0:T(1024)S(1)} %get-tuple-element.15), kind=kLoop, calls=%fused_computation | loop fusion | flops 3932160 | bytes 11016192 | tf_op jit(solution)/shard_map/convert_element_type | solution.py:39
  59.1 4.3 %convolution_convert_fusion = bf16[1024,512]{1,0:T(8,128)(2,1)} fusion(s32[]{:T(128)S(6)} %select_n.90, bf16[768,1024]{1,0:T(8,128)(2,1)S(1)} %get-tuple-element.11, bf16[512,1024]{1,0:T(8,128)(2,1)S(1)} %get-tuple-element.13, bf16[384,1024]{1,0:T(8,128)(2,1)} %collective-permute-done, bf16[384,1024]{1,0:T(8,128)(2,1)S(1)} %copy-done.10, ...), kind=kOutput, calls=%fused_computation.29 | convolution fusion | flops 1353187328 | bytes 6291460 | tf_op jit(solution)/shard_map/dot_general | solution.py:26
  63.3 6.6 %collective-permute-start.2 = (bf16[1024,512]{1,0:T(8,128)(2,1)}, bf16[1024,512]{1,0:T(8,128)(2,1)}, u32[]{:S(2)}, u32[]{:S(2)}) collective-permute-start(bf16[1024,512]{1,0:T(8,128)(2,1)} %convolution_convert_fusion), channel_id=1, source_target_pairs={{0,1},{1,0},{2,3},{3,2},{4,5},{5,4},{6,7},{7,6},{8,9},{9,8},{10,11... | collective-permute-start | bytes 3145736 | tf_op jit(solution)/shard_map/ppermute | solution.py:106
  69.9 2.6 %collective-permute-done.2 = bf16[1024,512]{1,0:T(8,128)(2,1)} collective-permute-done((bf16[1024,512]{1,0:T(8,128)(2,1)}, bf16[1024,512]{1,0:T(8,128)(2,1)}, u32[]{:S(2)}, u32[]{:S(2)}) %collective-permute-start.2) | collective-permute-done | bytes 1048608 | tf_op jit(solution)/shard_map/ppermute | solution.py:106
  72.5 3.6 %add_convert_fusion = bf16[1024,512]{1,0:T(8,128)(2,1)S(1)} fusion(bf16[1024,512]{1,0:T(8,128)(2,1)} %collective-permute-done.2, s32[]{:T(128)S(6)} %select_n.89, bf16[768,1024]{1,0:T(8,128)(2,1)} %copy-done.7, bf16[512,1024]{1,0:T(8,128)(2,1)} %copy-done.8, bf16[384,1024]{1,0:T(8,128)(2,1)} %collective-permute-done, bf16[384,1024]{1,0:T(8,128)(2,1)} %param.6, ...), kind=kOutput, calls=%fused_computation.9 | convolution fusion | flops 1354235904 | bytes 7340036 | tf_op jit(solution)/shard_map/dot_general | solution.py:26
  76.2 1.1 copy.35
  77.3 3.5 %all-to-all-start.4 = ((bf16[4,16,16,512]{3,2,1,0:T(8,128)(2,1)}), bf16[4,16,16,512]{3,2,1,0:T(8,128)(2,1)S(1)}, u32[]{:S(2)}, u32[]{:S(2)}) async-start(bf16[4,16,16,512]{3,2,1,0:T(8,128)(2,1)} %bitcast.60), calls=%async_computation.4 | async-start | bytes 2097152 | tf_op jit(solution)/shard_map/all_to_all | solution.py:14
  80.8 2.4 %slice.63 = bf16[384,1024]{1,0:T(8,128)(2,1)} slice(f32[768,1024]{1,0:T(8,128)} %get-tuple-element.12), slice={[384:768], [0:1024]} | slice | bytes 1572864 | tf_op jit(solution)/shard_map/slice | solution.py:124
  83.2 2.3 %collective-permute-start.1 = (bf16[384,1024]{1,0:T(8,128)(2,1)}, bf16[384,1024]{1,0:T(8,128)(2,1)}, u32[]{:S(2)}, u32[]{:S(2)}) collective-permute-start(bf16[384,1024]{1,0:T(8,128)(2,1)} %slice.63), channel_id=1, source_target_pairs={{0,1},{1,0},{2,3},{3,2},{4,5},{5,4},{6,7},{7,6},{8,9},{9,8},{10,11... | collective-permute-start | bytes 2359304 | tf_op jit(solution)/shard_map/ppermute | solution.py:124
  85.5 10.1 %all-to-all-done.4 = bf16[4,16,16,512]{3,2,1,0:T(8,128)(2,1)S(1)} async-done(((bf16[4,16,16,512]{3,2,1,0:T(8,128)(2,1)}), bf16[4,16,16,512]{3,2,1,0:T(8,128)(2,1)S(1)}, u32[]{:S(2)}, u32[]{:S(2)}) %all-to-all-start.4) | async-done | bytes 1048608 | tf_op jit(solution)/shard_map/all_to_all | solution.py:14
  95.6 1.1 copy-done.6
  96.7 3.5 %all-to-all-start.3 = ((bf16[4,128,1024]{2,1,0:T(8,128)(2,1)}), bf16[4,128,1024]{2,1,0:T(8,128)(2,1)S(1)}, u32[]{:S(2)}, u32[]{:S(2)}) async-start(bf16[4,128,1024]{2,1,0:T(8,128)(2,1)} %bitcast.61), calls=%async_computation.3 | async-start | bytes 2097152 | tf_op jit(solution)/shard_map/all_to_all | solution.py:14
  100.2 0.5 bitcast_subtract_fusion
  100.8 2.4 %multiply_reduce_fusion.4 = f32[384]{0:T(512)S(1)} fusion(f32[768,1024]{1,0:T(8,128)} %copy-done.1, bf16[384,1024]{1,0:T(8,128)(2,1)} %collective-permute-done.1, f32[768,1024]{1,0:T(8,128)} %get-tuple-element.12), kind=kLoop, calls=%fused_computation.23 | loop fusion | flops 1572480 | bytes 3933696 | tf_op jit(solution)/shard_map/reduce_sum | solution.py:38
  103.2 1.4 reduce_sum.153
  104.6 0.8 reshape.200
  105.4 1.7 %copy.24 = bf16[4,16,16,128]{3,2,1,0:T(8,128)(2,1)} copy(bf16[4,16,16,128]{3,0,2,1:T(4,128)(2,1)} %bitcast.66) | data formatting | bytes 524288 | tf_op jit(solution)/shard_map/transpose | solution.py:111
  107.1 7.0 %all-to-all-done.3 = bf16[4,128,1024]{2,1,0:T(8,128)(2,1)S(1)} async-done(((bf16[4,128,1024]{2,1,0:T(8,128)(2,1)}), bf16[4,128,1024]{2,1,0:T(8,128)(2,1)S(1)}, u32[]{:S(2)}, u32[]{:S(2)}) %all-to-all-start.3) | async-done | bytes 1048608 | tf_op jit(solution)/shard_map/all_to_all | solution.py:14
  114.1 3.4 %all-to-all-start.5 = ((bf16[4,16,16,128]{3,2,1,0:T(8,128)(2,1)}), bf16[4,16,16,128]{3,2,1,0:T(8,128)(2,1)S(1)}, u32[]{:S(2)}, u32[]{:S(2)}) async-start(bf16[4,16,16,128]{3,2,1,0:T(8,128)(2,1)} %copy.24), calls=%async_computation.5 | async-start | bytes 524288 | tf_op jit(solution)/shard_map/all_to_all | solution.py:14
  117.5 4.0 %convolution_convert_fusion.1 = bf16[384,1024]{1,0:T(8,128)(2,1)} fusion(bf16[1024,1024]{1,0:T(8,128)(2,1)S(1)} %copy-done, f32[768,1024]{1,0:T(8,128)} %copy-done.1, bf16[384,1024]{1,0:T(8,128)(2,1)} %collective-permute-done.1, f32[768,1024]{1,0:T(8,128)} %get-tuple-element.12, f32[384]{0:T(512)S(1)} %fusion.24, f32[384]{0:T(512)S(1)} %slice.32), kind=kOutput, calls=%fused_computation.31 | convolution fusion | flops 808058880 | bytes 6818816 | tf_op jit(solution)/shard_map/dot_general | solution.py:30
  121.6 1.5 convert_reduce_fusion
  123.1 0.7 reduce_sum.154
  123.7 10.9 %all-to-all-start.6 = ((bf16[16,16,128]{2,1,0:T(8,128)(2,1)}), bf16[16,16,128]{2,1,0:T(8,128)(2,1)S(1)}, u32[]{:S(2)}, u32[]{:S(2)}) async-start(bf16[16,16,128]{2,1,0:T(8,128)(2,1)} %reduce_sum.154), calls=%async_computation.6 | async-start | bytes 131072 | tf_op jit(solution)/shard_map/all_to_all | solution.py:14
  134.6 1.2 multiply_reduce_fusion.5
  135.9 10.3 %all-to-all-done.6 = bf16[16,16,128]{2,1,0:T(8,128)(2,1)S(1)} async-done(((bf16[16,16,128]{2,1,0:T(8,128)(2,1)}), bf16[16,16,128]{2,1,0:T(8,128)(2,1)S(1)}, u32[]{:S(2)}, u32[]{:S(2)}) %all-to-all-start.6) | async-done | bytes 65568 | tf_op jit(solution)/shard_map/all_to_all | solution.py:14
  146.2 0.6 broadcast_in_dim.112
  146.9 8.7 %all-to-all-start.7 = ((f32[8,16,128]{2,1,0:T(8,128)}), f32[8,16,128]{2,1,0:T(8,128)S(1)}, u32[]{:S(2)}, u32[]{:S(2)}) async-start(f32[8,16,128]{2,1,0:T(8,128)} %broadcast_in_dim.112), calls=%async_computation.7 | async-start | bytes 131072 | tf_op jit(solution)/shard_map/all_to_all | solution.py:14
  155.5 2.6 %convolution_convert_fusion.2 = bf16[128,1024]{1,0:T(8,128)(2,1)} fusion(bf16[1024,1024]{1,0:T(8,128)(2,1)S(1)} %copy-done, f32[128,1024]{1,0:T(8,128)S(1)} %convert_reduce_fusion, f32[512,1024]{1,0:T(8,128)} %copy-done.3, s32[]{:T(128)S(6)} %select_n.88, f32[128]{0:T(128)S(1)} %get-tuple-element.6, f32[128]{0:T(128)S(1)} %get-tuple-element.7), kind=kOutput, calls=%fused_computation.35 | convolution fusion | flops 269090816 | bytes 3408900 | tf_op jit(solution)/shard_map/dot_general | solution.py:30
  158.1 2.3 %all-to-all-done.7 = f32[8,16,128]{2,1,0:T(8,128)S(1)} async-done(((f32[8,16,128]{2,1,0:T(8,128)}), f32[8,16,128]{2,1,0:T(8,128)S(1)}, u32[]{:S(2)}, u32[]{:S(2)}) %all-to-all-start.7) | async-done | bytes 65568 | tf_op jit(solution)/shard_map/all_to_all | solution.py:14
  160.4 0.7 reshape.202
  (49 shorter events, 0.7 us)
Async XLA Ops:
  0.6 32.6 %copy-start = (bf16[1024,1024]{1,0:T(8,128)(2,1)S(1)}, bf16[1024,1024]{1,0:T(8,128)(2,1)}, u32[]{:S(2)}) copy-start(bf16[1024,1024]{1,0:T(8,128)(2,1)} %param.7) | copy-start | bytes 6291460
  2.1 12.1 %all-to-all-start = ((s32[4,2,128]{2,1,0:T(2,128)}), s32[4,2,128]{2,1,0:T(2,128)S(1)}, u32[]{:S(2)}, u32[]{:S(2)}) async-start(s32[4,2,128]{2,1,0:T(2,128)} %broadcast_in_dim.96), calls=%async_computation | async-start | bytes 8192 | tf_op jit(solution)/shard_map/all_to_all | solution.py:14
  7.0 27.6 %collective-permute-start = (bf16[384,1024]{1,0:T(8,128)(2,1)}, bf16[384,1024]{1,0:T(8,128)(2,1)}, u32[]{:S(2)}, u32[]{:S(2)}) collective-permute-start(bf16[384,1024]{1,0:T(8,128)(2,1)} %param.6), channel_id=1, source_target_pairs={{0,1},{1,0},{2,3},{3,2},{4,5},{5,4},{6,7},{7,6},{8,9},{9,8},{10,11... | collective-permute-start | bytes 2359304 | tf_op jit(solution)/shard_map/ppermute | solution.py:54
  16.3 17.0 %all-to-all-start.1 = ((bf16[4,128,1024]{2,1,0:T(8,128)(2,1)}), bf16[4,128,1024]{2,1,0:T(8,128)(2,1)S(1)}, u32[]{:S(2)}, u32[]{:S(2)}) async-start(bf16[4,128,1024]{2,1,0:T(8,128)(2,1)} %broadcast_in_dim.100), calls=%async_computation.1 | async-start | bytes 2097152 | tf_op jit(solution)/shard_map/all_to_all | solution.py:14
  33.3 1.4 copy-start.9
  34.6 3.6 %copy-start.3 = (f32[512,1024]{1,0:T(8,128)}, f32[512,1024]{1,0:T(8,128)S(1)}, u32[]{:S(2)}) copy-start(f32[512,1024]{1,0:T(8,128)S(1)} %get-tuple-element.22) | copy-start | bytes 6291460
  38.2 2.5 %copy-start.1 = (f32[768,1024]{1,0:T(8,128)}, f32[768,1024]{1,0:T(8,128)S(1)}, u32[]{:S(2)}) copy-start(f32[768,1024]{1,0:T(8,128)S(1)} %get-tuple-element.24) | copy-start | bytes 9437188
  41.4 7.4 %all-to-all-start.2 = ((f32[4,5,128]{2,1,0:T(8,128)}), f32[4,5,128]{2,1,0:T(8,128)S(1)}, u32[]{:S(2)}, u32[]{:S(2)}) async-start(f32[4,5,128]{2,1,0:T(8,128)} %pad_maximum_fusion.3), calls=%async_computation.2 | async-start | bytes 32768 | tf_op jit(solution)/shard_map/all_to_all | solution.py:14
  48.8 2.1 %copy-start.4 = (f32[512,1024]{1,0:T(8,128)S(1)}, f32[512,1024]{1,0:T(8,128)}, u32[]{:S(2)}) copy-start(f32[512,1024]{1,0:T(8,128)} %copy-done.3) | copy-start | bytes 6291460
  51.0 3.2 %copy-start.2 = (f32[768,1024]{1,0:T(8,128)S(1)}, f32[768,1024]{1,0:T(8,128)}, u32[]{:S(2)}) copy-start(f32[768,1024]{1,0:T(8,128)} %copy-done.1) | copy-start | bytes 9437188
  56.8 2.2 %copy-start.8 = (bf16[512,1024]{1,0:T(8,128)(2,1)}, bf16[512,1024]{1,0:T(8,128)(2,1)S(1)}, u32[]{:S(2)}) copy-start(bf16[512,1024]{1,0:T(8,128)(2,1)S(1)} %get-tuple-element.13) | copy-start | bytes 3145732
  56.8 2.2 %copy-start.10 = (bf16[384,1024]{1,0:T(8,128)(2,1)S(1)}, bf16[384,1024]{1,0:T(8,128)(2,1)}, u32[]{:S(2)}) copy-start(bf16[384,1024]{1,0:T(8,128)(2,1)} %param.6) | copy-start | bytes 2359300
  59.0 4.3 %copy-start.7 = (bf16[768,1024]{1,0:T(8,128)(2,1)}, bf16[768,1024]{1,0:T(8,128)(2,1)S(1)}, u32[]{:S(2)}) copy-start(bf16[768,1024]{1,0:T(8,128)(2,1)S(1)} %get-tuple-element.11) | copy-start | bytes 4718596
  63.3 9.2 %collective-permute-start.2 = (bf16[1024,512]{1,0:T(8,128)(2,1)}, bf16[1024,512]{1,0:T(8,128)(2,1)}, u32[]{:S(2)}, u32[]{:S(2)}) collective-permute-start(bf16[1024,512]{1,0:T(8,128)(2,1)} %convolution_convert_fusion), channel_id=1, source_target_pairs={{0,1},{1,0},{2,3},{3,2},{4,5},{5,4},{6,7},{7,6},{8,9},{9,8},{10,11... | collective-permute-start | bytes 3145736 | tf_op jit(solution)/shard_map/ppermute | solution.py:106
  77.3 18.3 %all-to-all-start.4 = ((bf16[4,16,16,512]{3,2,1,0:T(8,128)(2,1)}), bf16[4,16,16,512]{3,2,1,0:T(8,128)(2,1)S(1)}, u32[]{:S(2)}, u32[]{:S(2)}) async-start(bf16[4,16,16,512]{3,2,1,0:T(8,128)(2,1)} %bitcast.60), calls=%async_computation.4 | async-start | bytes 2097152 | tf_op jit(solution)/shard_map/all_to_all | solution.py:14
  83.2 17.5 %collective-permute-start.1 = (bf16[384,1024]{1,0:T(8,128)(2,1)}, bf16[384,1024]{1,0:T(8,128)(2,1)}, u32[]{:S(2)}, u32[]{:S(2)}) collective-permute-start(bf16[384,1024]{1,0:T(8,128)(2,1)} %slice.63), channel_id=1, source_target_pairs={{0,1},{1,0},{2,3},{3,2},{4,5},{5,4},{6,7},{7,6},{8,9},{9,8},{10,11... | collective-permute-start | bytes 2359304 | tf_op jit(solution)/shard_map/ppermute | solution.py:124
  95.6 1.1 copy-start.6
  96.7 17.4 %all-to-all-start.3 = ((bf16[4,128,1024]{2,1,0:T(8,128)(2,1)}), bf16[4,128,1024]{2,1,0:T(8,128)(2,1)S(1)}, u32[]{:S(2)}, u32[]{:S(2)}) async-start(bf16[4,128,1024]{2,1,0:T(8,128)(2,1)} %bitcast.61), calls=%async_computation.3 | async-start | bytes 2097152 | tf_op jit(solution)/shard_map/all_to_all | solution.py:14
  114.1 3.4 %copy-start.5 = (bf16[4,128,1024]{2,1,0:T(8,128)(2,1)}, bf16[4,128,1024]{2,1,0:T(8,128)(2,1)S(1)}, u32[]{:S(2)}) copy-start(bf16[4,128,1024]{2,1,0:T(8,128)(2,1)S(1)} %all-to-all-done.3) | copy-start | bytes 3145732
  114.1 8.9 %all-to-all-start.5 = ((bf16[4,16,16,128]{3,2,1,0:T(8,128)(2,1)}), bf16[4,16,16,128]{3,2,1,0:T(8,128)(2,1)S(1)}, u32[]{:S(2)}, u32[]{:S(2)}) async-start(bf16[4,16,16,128]{3,2,1,0:T(8,128)(2,1)} %copy.24), calls=%async_computation.5 | async-start | bytes 524288 | tf_op jit(solution)/shard_map/all_to_all | solution.py:14
  123.7 22.5 %all-to-all-start.6 = ((bf16[16,16,128]{2,1,0:T(8,128)(2,1)}), bf16[16,16,128]{2,1,0:T(8,128)(2,1)S(1)}, u32[]{:S(2)}, u32[]{:S(2)}) async-start(bf16[16,16,128]{2,1,0:T(8,128)(2,1)} %reduce_sum.154), calls=%async_computation.6 | async-start | bytes 131072 | tf_op jit(solution)/shard_map/all_to_all | solution.py:14
  146.9 13.5 %all-to-all-start.7 = ((f32[8,16,128]{2,1,0:T(8,128)}), f32[8,16,128]{2,1,0:T(8,128)S(1)}, u32[]{:S(2)}, u32[]{:S(2)}) async-start(f32[8,16,128]{2,1,0:T(8,128)} %broadcast_in_dim.112), calls=%async_computation.7 | async-start | bytes 131072 | tf_op jit(solution)/shard_map/all_to_all | solution.py:14

commit v2 on v1

v2 whole, which is shorter than its diff:
```python
import jax
import jax.numpy as jnp
from jax import lax
from jax.experimental import pallas as pl
from jax.experimental.pallas import tpu as pltpu
from jax.sharding import Mesh, PartitionSpec as P

score_scale = 50.0
epsilon = 1e-06

X, C, Y, Z = 4, 2, 4, 16
SWAP = ((0, 1), (1, 0))
ROWS = 128
WIDTH = 1024
OWN = 384
BLOCKS = OWN // ROWS
CHIP_BLOCKS = BLOCKS * C
NAMES = 8
EXTRA = 16
HALF = WIDTH // C
PART = 256
HBM = pl.BlockSpec(memory_space=pltpu.HBM)
VMEM = pl.BlockSpec(memory_space=pltpu.VMEM)
SMEM = pl.BlockSpec(memory_space=pltpu.SMEM)
F32, BF16 = jnp.float32, jnp.bfloat16


def shift(k):
    return tuple(((i + k) % X, i) for i in range(X))


def exchange(value, axis):
    return lax.all_to_all(value, axis, split_axis=0, concat_axis=0, tiled=True)


def matmul(a, b):
    return jnp.dot(a, b, preferred_element_type=F32)


def matmul_tn(a, b):
    return lax.dot_general(a, b, (((0,), (0,)), ((), ())), preferred_element_type=F32)


def matmul_nt(a, b):
    return lax.dot_general(a, b, (((1,), (1,)), ((), ())), preferred_element_type=F32)


def back_of(emb, r, grad):
    emb = emb.astype(F32)
    inner = jnp.sum(emb * grad, axis=-1, keepdims=True)
    return r * (grad - inner * emb)


def params(mib):
    return pltpu.CompilerParams(vmem_limit_bytes=mib << 20)


def shape(dims, dtype):
    return jax.ShapeDtypeStruct(dims, dtype)


def call(kernel, name, out_shape, in_specs, out_specs, scratch, mib, flops, moved, *args):
    return pl.pallas_call(
        kernel,
        name=name,
        out_shape=out_shape,
        in_specs=in_specs,
        out_specs=out_specs,
        scratch_shapes=scratch,
        compiler_params=params(mib),
        cost_estimate=pl.CostEstimate(flops=flops, bytes_accessed=moved, transcendentals=0),
    )(*args)


def pack_kernel(queries, positive, pairs, out, pos, names, wide, narrow, sems):
    copies = [pltpu.make_async_copy(positive, pos, sems.at[0]), pltpu.make_async_copy(pairs, names, sems.at[1])]
    for d in range(X):
        copies.append(pltpu.make_async_copy(queries, out.at[d, pl.ds(0, ROWS)], sems.at[2 + d]))
    for copy in copies:
        copy.start()
    wide[...] = jnp.full(wide.shape, 255.0, F32)
    copies[0].wait()
    copies[1].wait()
    index = pos[...]
    wide[0:1, 0:ROWS] = (index >> 7).astype(F32)
    wide[0:1, ROWS : 2 * ROWS] = (index & 127).astype(F32)
    wide[0:1, 2 * ROWS : 2 * ROWS + NAMES] = names[...].astype(F32)
    narrow[...] = wide[...].astype(BF16)
    for d in range(X):
        copies.append(pltpu.make_async_copy(narrow, out.at[d, pl.ds(ROWS, EXTRA)], sems.at[2 + X + d]))
        copies[-1].start()
    for copy in copies[2:]:
        copy.wait()


def pack(queries, positive, pairs):
    return call(
        pack_kernel, "pack",
        shape((X, ROWS + EXTRA, WIDTH), BF16),
        [HBM, HBM, HBM],
        HBM,
        [
            pltpu.VMEM((1, ROWS), jnp.int32),
            pltpu.VMEM((1, NAMES), jnp.int32),
            pltpu.VMEM((EXTRA, WIDTH), F32),
            pltpu.VMEM((EXTRA, WIDTH), BF16),
            pltpu.SemaphoreType.DMA((2 + 2 * X,)),
        ],
        4, 0, 1_400_000,
        queries, positive.reshape(1, ROWS), pairs,
    )


def project(source, weight, proj, r_out, emb, rows):
    for j in range(WIDTH // PART):
        cols = pl.ds(j * PART, PART)
        proj[:, cols] = matmul(source, weight[:, cols])
    for i in range(rows // ROWS):
        here = pl.ds(i * ROWS, ROWS)
        value = proj[here, :]
        r = lax.rsqrt(jnp.sum(value * value, axis=1, keepdims=True) + epsilon)
        r_out[here, :] = r
        emb[here, :] = (value * r).astype(BF16)


def passage_kernel(passages, weight, emb, r_out, proj):
    project(passages[...], weight, proj, r_out, emb, OWN)


def passage_side(passages, weight):
    return call(
        passage_kernel, "passage_side",
        (shape((OWN, WIDTH), BF16), shape((OWN, 1), F32)),
        [VMEM, VMEM],
        (VMEM, VMEM),
        [pltpu.VMEM((OWN, WIDTH), F32)],
        16, 2 * OWN * WIDTH * WIDTH, 4_000_000,
        passages, weight,
    )


def flat(value):
    return jnp.concatenate([value[k : k + 1] for k in range(X)], axis=1)


def rows_of(tiles, cols=slice(None)):
    return [tiles[k, 0:ROWS, cols] for k in range(X)]


def score_kernel(place, tiles, weight, emb_own, emb_sib, q_emb, q_r, exponent, send, pos_row, proj):
    x, c = place[0], place[1]
    lines = [tiles[k, ROWS : ROWS + EXTRA, 0 : 3 * ROWS].astype(F32)[0:1] for k in range(X)]
    lines = jnp.concatenate(lines, axis=0).astype(jnp.int32)
    pos_name, pos_rest = lines[:, :ROWS], lines[:, ROWS : 2 * ROWS]
    local = lines[:, 2 * ROWS : 3 * ROWS] - x * CHIP_BLOCKS
    turned = local + BLOCKS * c
    turned = jnp.where(turned >= CHIP_BLOCKS, turned - CHIP_BLOCKS, turned)
    slot = jnp.where((local >= 0) & (local < CHIP_BLOCKS), turned, -1)
    lane = lax.broadcasted_iota(jnp.int32, (X, ROWS), 1)
    pos_slot = jnp.full((X, ROWS), -1, jnp.int32)
    for n in range(NAMES):
        of_name = jnp.max(jnp.where(lane == n, slot, -1), axis=1, keepdims=True)
        pos_slot = jnp.where(pos_name == n, of_name, pos_slot)
    pos = flat(jnp.where(pos_slot >= 0, pos_slot * ROWS + pos_rest, -1))
    pos_row[...] = pos

    project(jnp.concatenate(rows_of(tiles), axis=0), weight, proj, q_r, q_emb, X * ROWS)
    line = lax.broadcasted_iota(jnp.int32, (ROWS, X * ROWS), 0)
    total = jnp.zeros((1, X * ROWS), F32)
    picked = jnp.zeros((1, X * ROWS), F32)
    for b in range(CHIP_BLOCKS):
        block = pl.ds(b * ROWS, ROWS)
        named = jnp.max(jnp.where(slot == b, 1, 0), axis=1, keepdims=True)
        named = flat(jnp.broadcast_to(named, (X, ROWS)))
        emb = (emb_own if b < BLOCKS else emb_sib)[pl.ds(b % BLOCKS * ROWS, ROWS), :]
        scores = matmul_nt(emb, q_emb[...]) * score_scale
        value = jnp.where(named > 0, jnp.exp(scores), 0.0)
        exponent[block, :] = value
        total = total + jnp.sum(value, axis=0, keepdims=True)
        picked = picked + jnp.sum(jnp.where(line == pos - b * ROWS, scores, 0.0), axis=0, keepdims=True)
    send[...] = jnp.zeros(send.shape, F32)
    for k in range(X):
        lanes = slice(k * ROWS, (k + 1) * ROWS)
        for d in range(X):
            send[d, k : k + 1, :] = total[:, lanes]
        send[k, X : X + 1, :] = picked[:, lanes]


def score_side(place, tiles, weight, emb_own, emb_sib):
    queries = X * ROWS
    passages = CHIP_BLOCKS * ROWS
    return call(
        score_kernel, "score_side",
        (
            shape((queries, WIDTH), BF16),
            shape((queries, 1), F32),
            shape((passages, queries), F32),
            shape((X, 8, ROWS), F32),
            shape((1, queries), jnp.int32),
        ),
        [SMEM] + [VMEM] * 4,
        (VMEM,) * 5,
        [pltpu.VMEM((queries, WIDTH), F32)],
        24, 2_000_000_000, 8_000_000,
        place, tiles, weight, emb_own, emb_sib,
    )


def grad_kernel(
    place, recv, pos_row, q_r, r_own, r_sib, exponent, q_emb, emb_own, emb_sib, tiles, own, sib,
    losses, g0, g1, g2, g3, emb_mine, r_mine, p_grad_own, p_grad_sib, backs_here, w_there,
    dscore, q_grad, backs,
):
    x, c = place[0], place[1]
    queries = X * ROWS
    total = recv[0] + recv[1] + recv[2] + recv[3]
    mine = jnp.zeros((1, ROWS), F32)
    for k in range(X):
        mine = mine + jnp.where(x == k, total[k : k + 1], 0.0)
    losses[...] = jnp.log(mine) - total[X : X + 1]
    inverse = 1.0 / flat(total)
    pos = pos_row[...]
    line = lax.broadcasted_iota(jnp.int32, (ROWS, queries), 0)
    for b in range(CHIP_BLOCKS):
        block = pl.ds(b * ROWS, ROWS)
        target = jnp.where(line == pos - b * ROWS, 1.0, 0.0)
        dscore[block, :] = (exponent[block, :] * inverse - target).astype(BF16)

    def keep(rows, emb, r, grad):
        value = back_of(emb, r, grad).astype(BF16)
        for h in range(C):
            backs[h, rows, :] = value[:, h * HALF : (h + 1) * HALF]

    for j in range(WIDTH // PART):
        cols = pl.ds(j * PART, PART)
        emb = jnp.concatenate([emb_own[:, cols], emb_sib[:, cols]], axis=0)
        q_grad[:, cols] = matmul_tn(dscore[...], emb) * score_scale
    for k in range(X):
        rows = pl.ds(k * ROWS, ROWS)
        keep(rows, q_emb[rows, :], q_r[rows, :], q_grad[rows, :])
    for k, out in enumerate((g0, g1, g2, g3)):
        rows = pl.ds(pl.multiple_of(lax.rem(x + k, X) * ROWS, ROWS), ROWS)
        out[...] = q_grad[rows, :].astype(out.dtype)
    rows = pl.ds(pl.multiple_of(x * ROWS, ROWS), ROWS)
    emb_mine[...] = q_emb[rows, :]
    r_mine[...] = q_r[rows, :]
    for b in range(CHIP_BLOCKS):
        rows = pl.ds(b * ROWS, ROWS)
        grad = matmul(dscore[rows, :], q_emb[...]) * score_scale
        first = b < BLOCKS
        near = pl.ds((b % BLOCKS) * ROWS, ROWS)
        (p_grad_own if first else p_grad_sib)[near, :] = grad.astype(F32 if first else BF16)
        emb = (emb_own if first else emb_sib)[near, :]
        r = (r_own if first else r_sib)[near, :]
        keep(pl.ds(queries + b * ROWS, ROWS), emb, r, grad)
    weight_terms(tiles, own, sib, backs.at[1 - c], w_there)
    backs_here[...] = backs[c]


def weight_terms(tiles, own, sib, backs, out):
    for j in range(WIDTH // PART):
        cols = pl.ds(j * PART, PART)
        hidden = jnp.concatenate(rows_of(tiles, cols) + [own[:, cols], sib[:, cols]], axis=0)
        out[cols, :] = matmul_tn(hidden, backs[...]).astype(out.dtype)


def grad_side(*args):
    queries = X * ROWS
    passages = CHIP_BLOCKS * ROWS
    tile = shape((ROWS, WIDTH), BF16)
    return call(
        grad_kernel, "grad_side",
        (
            shape((1, ROWS), F32),
            shape((ROWS, WIDTH), F32), tile, tile, tile,
            tile,
            shape((ROWS, 1), F32),
            shape((OWN, WIDTH), F32),
            shape((OWN, WIDTH), BF16),
            shape((queries + passages, HALF), BF16),
            shape((WIDTH, HALF), BF16),
        ),
        [SMEM] + [VMEM] * 12,
        (VMEM,) * 11,
        [
            pltpu.VMEM((passages, queries), BF16),
            pltpu.VMEM((queries, WIDTH), F32),
            pltpu.VMEM((C, queries + passages, HALF), BF16),
        ],
        32, 3_000_000_000, 14_000_000,
        *args,
    )


def weight_kernel(backs, tiles, own, sib, out):
    weight_terms(tiles, own, sib, backs, out)


def weight_here(backs, tiles, own, sib):
    return call(
        weight_kernel, "weight_here",
        shape((WIDTH, HALF), F32),
        [VMEM] * 4,
        VMEM,
        [],
        24, 1_350_000_000, 6_000_000,
        backs, tiles, own, sib,
    )


def spread_kernel(here, there, out):
    own_rows = WIDTH // (Z * Y)
    lanes = HALF // X
    for z in range(Z):
        rows = pl.ds(z * Y * own_rows, Y * own_rows)
        value = (here[rows, :] + there[rows, :].astype(F32)).astype(BF16)
        for y in range(Y):
            for x in range(X):
                out[y * X + x, z] = value[y * own_rows : (y + 1) * own_rows, x * lanes : (x + 1) * lanes]


def spread(here, there):
    return call(
        spread_kernel, "spread",
        shape((Y * X, Z, WIDTH // (Z * Y), HALF // X), BF16),
        [VMEM, VMEM],
        VMEM,
        [],
        16, 500_000, 4_000_000,
        here, there,
    )


def sum_kernel(pieces, out):
    total = pieces[0].astype(F32)
    for k in range(1, Y * X):
        total = total + pieces[k].astype(F32)
    out[...] = total.astype(BF16)


def sum_pieces(pieces):
    return call(
        sum_kernel, "sum_pieces", shape(pieces.shape[1:], BF16), [VMEM], VMEM, [], 8, 500_000, 1_000_000, pieces
    )


def last_sum_kernel(pieces, out):
    total = pieces[0].astype(F32)
    for k in range(1, Z):
        total = total + pieces[k].astype(F32)
    total = total * (1.0 / (Z * Y * X * C))
    for d in range(X * C):
        out[d] = total


def last_sum(pieces):
    dims = (X * C,) + pieces.shape[1:]
    return call(
        last_sum_kernel, "last_sum", shape(dims, F32), [VMEM], VMEM, [], 8, 50_000, 100_000, pieces
    )


def lay_kernel(pieces, out):
    lanes = HALF // X
    for x in range(X):
        for c in range(C):
            out[:, c * HALF + x * lanes : c * HALF + (x + 1) * lanes] = pieces[x * C + c]


def lay(pieces):
    dims = (WIDTH // (Z * Y), WIDTH)
    return call(lay_kernel, "lay", shape(dims, F32), [VMEM], VMEM, [], 8, 0, 200_000, pieces)


def hidden_kernel(*refs):
    *terms, emb, r, weight, out = refs
    grad = terms[0][...]
    for term in terms[1:]:
        grad = grad + term[...].astype(F32)
    back = back_of(emb[...], r[...], grad).astype(BF16)
    for j in range(WIDTH // PART):
        cols = pl.ds(j * PART, PART)
        out[:, cols] = matmul_nt(back, weight[cols, :]).astype(BF16)


def hidden_grad(terms, emb, r, weight):
    rows = emb.shape[0]
    return call(
        hidden_kernel, "hidden_grad",
        shape((rows, WIDTH), BF16),
        [VMEM] * (len(terms) + 3),
        VMEM,
        [],
        24, 2 * rows * WIDTH * WIDTH, 2_000_000 + rows * 10_000,
        *terms, emb, r, weight,
    )


def body(queries, passages, weight, pairs, positive):
    x = lax.axis_index("x")
    c = lax.axis_index("c")
    place = jnp.stack([x, c]).astype(jnp.int32)

    packed = pack(queries, positive, pairs)
    tiles = exchange(packed, "x")
    passages, weight, _ = lax.optimization_barrier((passages, weight, packed))
    emb_own, r_own = passage_side(passages, weight)
    outgoing, _ = lax.optimization_barrier((passages, emb_own))
    sibling = lax.ppermute(outgoing, "c", SWAP)
    emb_sib, r_sib = passage_side(sibling, weight)

    q_emb, q_r, exponent, send, pos_row = score_side(place, tiles, weight, emb_own, emb_sib)
    recv = exchange(send, "x")
    losses, g0, g1, g2, g3, emb_mine, r_mine, p_grad, p_grad_sib, backs, w_there = grad_side(
        place, recv, pos_row, q_r, r_own, r_sib, exponent, q_emb, emb_own, emb_sib, tiles, passages, sibling
    )

    w_there = lax.ppermute(w_there, "c", SWAP)
    w = spread(weight_here(backs, tiles, passages, sibling), w_there)
    p_grad_sib, _ = lax.optimization_barrier((p_grad_sib, w_there))
    p_grad_sib = lax.ppermute(p_grad_sib, "c", SWAP)
    passage_grad = hidden_grad((p_grad, p_grad_sib), emb_own, r_own, weight)

    w = sum_pieces(exchange(w, ("y", "x")))
    w, passage_grad = lax.optimization_barrier((w, passage_grad))
    (g1, g2, g3), w = lax.optimization_barrier(((g1, g2, g3), w))
    terms = [g0] + [lax.ppermute(term, "x", shift(X - k)) for k, term in enumerate((g1, g2, g3), 1)]
    query_grad = hidden_grad(terms, emb_mine, r_mine, weight)

    w = last_sum(exchange(w, "z"))
    weight_grad = lay(exchange(w, ("x", "c")))
    return losses.reshape(ROWS), query_grad, passage_grad, weight_grad


def solution(mesh):
    torus = Mesh(mesh.devices.reshape(Z, Y, X, C), ("z", "y", "x", "c"))
    every = ("z", "y", "x", "c")
    return jax.shard_map(
        body,
        mesh=torus,
        in_specs=(P(every, None), P(every, None), P(), P(every, None), P(every)),
        out_specs=(P(every), P(every, None), P(every, None), P(("z", "y"), None)),
        check_vma=False,
    )
```

time: 162 us -> 116 us (0.72)
  waiting for transfers between devices: 48.4 us -> 18.8 us
  matrix products: 26.4 us -> 0 us
  Pallas kernels: 0 us -> 25.3 us
  other arithmetic: 15.4 us -> 0.08 us
  starting transfers between devices: 58.6 us -> 48.6 us
  blocking collectives: 0 us -> 8.48 us
  local copies, waits for them, and re-layouts: 11.3 us -> 13.2 us
    all_to_all x8 -> x4, waiting for transfers between devices: 45.8 us -> 14.3 us  [exchange(): return lax.all_to_all(value, axis, split_axis=0, concat_axis=0, tiled=True)]
    dot_general x9 -> x0, matrix products: 26.4 us -> none  [the longest x3 9.13 us: matmul_nt(): lax.dot_general(a, b, (((1,), (1,)), ((), ())), preferred_element_type=jn...]
    pallas_call x0 -> x12, Pallas kernels: none -> 25.3 us  [call(): pl.pallas_call(kernel, name=name, out_shape=out_shape, in_specs=in_specs,...]
    all_to_all x8 -> x4, starting transfers between devices: 42.5 us -> 26.9 us  [exchange(): return lax.all_to_all(value, axis, split_axis=0, concat_axis=0, tiled=True)]
    unnamed x24 -> x54, local copies, waits for them, and re-layouts: 1.2 us -> 13.2 us
    all_to_all x0 -> x1, blocking collectives: none -> 8.48 us  [exchange(): return lax.all_to_all(value, axis, split_axis=0, concat_axis=0, tiled=True)]
    reduce_sum x8 -> x0, other arithmetic: 7.26 us -> none  [the longest x2 3.59 us: back_of(): inner = jnp.sum(proj * grad, axis=-1, keepdims=True)]
    ppermute x3 -> x6, starting transfers between devices: 16.1 us -> 21.8 us  [the longest x3 8.46 us: body(): lax.ppermute(term, 'x', shift(X - k))]
  transfers between devices with their start and end apart: 11 -> 10, of which waited for: 7 -> 5; matrix products, arithmetic and copies ran while one was open for 14% -> 0% of each run, Pallas kernels for 0% -> 10%
where the time goes in v2:
time: 116 us; the launch traced here: 115 us
  starting transfers between devices  48.6 us (42%)
  Pallas kernels  25.3 us (22%)
  waiting for transfers between devices  18.8 us (16%)
  local copies, waits for them, and re-layouts  13.2 us (11%)
  blocking collectives  8.48 us (7%)
    all_to_all x4, starting transfers between devices, exchange(): return lax.all_to_all(value, axis, split_axis=0, concat_axis=0, tiled=True)  26.9 us
    pallas_call x12, Pallas kernels, call(): pl.pallas_call(kernel, name=name, out_shape=out_shape, in_specs=in_specs,...  25.3 us
    all_to_all x4, waiting for transfers between devices, exchange(): return lax.all_to_all(value, axis, split_axis=0, concat_axis=0, tiled=True)  14.3 us
    unnamed x54, local copies, waits for them, and re-layouts  13.2 us
    all_to_all x1, blocking collectives, exchange(): return lax.all_to_all(value, axis, split_axis=0, concat_axis=0, tiled=True)  8.48 us
    ppermute x3, starting transfers between devices, body(): lax.ppermute(term, 'x', shift(X - k))  8.46 us
    ppermute x1, starting transfers between devices, body(): sibling = lax.ppermute(outgoing, 'c', SWAP)  7.48 us
    ppermute x1, starting transfers between devices, body(): w_there = lax.ppermute(w_there, 'c', SWAP)  3.71 us
  transfers between devices with their start and end apart: 10, of which 5 were waited for; matrix products, arithmetic and copies ran while one was open for 0% of the time, Pallas kernels for 10%

profile of v2, /device:TPU:1, one launch (start us, length us, event | category | flops | bytes accessed | tf_op | source)
XLA Modules:
  0.0 115.3 jit_solution(7659814242984620238)
XLA Ops:
  0.6 0.9 copy-done.10
  1.6 0.7 copy-done.16
  2.2 0.7 copy-done.17
  2.9 1.1 pack.1
  4.0 4.9 %all-to-all-start = ((bf16[4,144,1024]{2,1,0:T(8,128)(2,1)}), bf16[4,144,1024]{2,1,0:T(8,128)(2,1)S(1)}, u32[]{:S(2)}, u32[]{:S(2)}) async-start(bf16[4,144,1024]{2,1,0:T(8,128)(2,1)} %pack.1), calls=%async_computation | async-start | bytes 2359296 | tf_op jit(solution)/shard_map/all_to_all | solution.py:33
  8.9 2.2 %passage_side.2 = (bf16[384,1024]{1,0:T(8,128)(2,1)S(1)}, f32[384,1]{1,0:T(8,128)S(1)}) custom-call(bf16[384,1024]{1,0:T(8,128)(2,1)} %own.1, bf16[1024,1024]{1,0:T(8,128)(2,1)S(1)} %copy-done), custom_call_target="tpu_custom_call" | custom-call | flops 805306368 | bytes 4000000 | tf_op jit(solution)/shard_map/passage_side/pallas_call | solution.py:63
  11.1 0.0 copy-start.4
  11.1 0.9 copy-done.4
  12.0 0.7 copy-done.11
  12.7 7.5 %collective-permute-start = (bf16[384,1024]{1,0:T(8,128)(2,1)}, bf16[384,1024]{1,0:T(8,128)(2,1)}, u32[]{:S(2)}, u32[]{:S(2)}) collective-permute-start(bf16[384,1024]{1,0:T(8,128)(2,1)} %own.1), channel_id=1, source_target_pairs={{0,1},{1,0},{2,3},{3,2},{4,5},{5,4},{6,7},{7,6},{8,9},{9,8},{10,11... | collective-permute-start | bytes 2359304 | tf_op jit(solution)/shard_map/ppermute | solution.py:409
  20.2 0.1 pad_add_fusion.place
  20.2 2.2 %collective-permute-done.passages.sib = bf16[384,1024]{1,0:T(8,128)(2,1)} collective-permute-done((bf16[384,1024]{1,0:T(8,128)(2,1)}, bf16[384,1024]{1,0:T(8,128)(2,1)}, u32[]{:S(2)}, u32[]{:S(2)}) %collective-permute-start) | collective-permute-done | bytes 786464 | tf_op jit(solution)/shard_map/ppermute | solution.py:409
  22.4 2.2 %passage_side.3 = (bf16[384,1024]{1,0:T(8,128)(2,1)S(1)}, f32[384,1]{1,0:T(8,128)S(1)}) custom-call(bf16[384,1024]{1,0:T(8,128)(2,1)} %collective-permute-done.passages.sib, bf16[1024,1024]{1,0:T(8,128)(2,1)S(1)} %copy-done), custom_call_target="tpu_custom_call" | custom-call | flops 805306368 | bytes 4000000 | tf_op jit(solution)/shard_map/passage_side/pallas_call | solution.py:63
  24.6 0.9 copy-done.22
  25.5 0.7 copy-done.25
  26.2 0.0 all-to-all-done.tiles
  26.2 1.1 copy-done.5
  27.3 1.1 copy-done.23
  28.5 4.2 %score_side.1 = (bf16[512,1024]{1,0:T(8,128)(2,1)S(1)}, f32[512,1]{1,0:T(8,128)S(1)}, f32[768,512]{1,0:T(8,128)S(1)}, f32[4,8,128]{2,1,0:T(8,128)S(1)}, s32[1,512]{1,0:T(1,128)S(1)}) custom-call(s32[2]{0:T(128)S(1)} %pad_add_fusion.place, bf16[4,144,1024]{2,1,0:T(8,128)(2,1)S(1)} %all-to-all-done.tiles, bf16[1024,1024]{1,0:T(8,128)(2,1)S(1)} %copy-done, ...), custom_call_target="tpu_custom_call" | custom-call | flops 2000000000 | bytes 8000000 | tf_op jit(solution)/shard_map/score_side/pallas_call | solution.py:63
  32.7 8.5 %all_to_all.25.recv = f32[4,8,128]{2,1,0:T(8,128)S(1)} all-to-all(f32[4,8,128]{2,1,0:T(8,128)S(1)} %get-tuple-element.39), channel_id=1, replica_groups=mesh['z'=16,'y'=4,'x'=4,'c'=2] {'x'}, dimensions={0} | all-to-all | bytes 32768 | tf_op jit(solution)/shard_map/all_to_all | solution.py:33
  41.2 6.6 %grad_side.1 = (f32[1,128]{1,0:T(1,128)}, f32[128,1024]{1,0:T(8,128)S(1)}, bf16[128,1024]{1,0:T(8,128)(2,1)S(1)}, bf16[128,1024]{1,0:T(8,128)(2,1)S(1)}, bf16[12...) custom-call(s32[2]{0:T(128)S(1)} %pad_add_fusion.place, ...), custom_call_target="tpu_custom_call" | custom-call | flops 3000000000 | bytes 14000000 | tf_op jit(solution)/shard_map/grad_side/pallas_call | solution.py:63
  47.8 0.0 copy-start.21
  47.8 3.7 %collective-permute-start.1 = (bf16[1024,512]{1,0:T(8,128)(2,1)S(1)}, bf16[1024,512]{1,0:T(8,128)(2,1)S(1)}, u32[]{:S(2)}, u32[]{:S(2)}) collective-permute-start(bf16[1024,512]{1,0:T(8,128)(2,1)S(1)} %get-tuple-element.52), channel_id=1, source_target_pairs={{0,1},{1,0},{2,3},{3,2},{4,5},{5,4},{6,7},{7,6},{8,9},{9,8},{10,11... | collective-permute-start | bytes 3145736 | tf_op jit(solution)/shard_map/ppermute | solution.py:418
  51.5 2.9 %weight_here.1.here = f32[1024,512]{1,0:T(8,128)S(1)} custom-call(bf16[1280,512]{1,0:T(8,128)(2,1)S(1)} %get-tuple-element.51.backs, bf16[4,144,1024]{2,1,0:T(8,128)(2,1)S(1)} %all-to-all-done.tiles, bf16[384,1024]{1,0:T(8,128)(2,1)} %own.1, bf16[384,1024]{1,0:T(8,128)(2,1)} %collective-permute-done.passages.sib), custom_call_target="tpu_custom_call" | custom-call | flops 1350000000 | bytes 6000000 | tf_op jit(solution)/shard_map/weight_here/pallas_call | solution.py:63
  54.5 0.2 spread.1
  54.7 1.0 copy-done.1
  55.7 3.7 %all-to-all-start.2 = ((bf16[16,16,16,128]{3,2,1,0:T(8,128)(2,1)}), bf16[16,16,16,128]{3,2,1,0:T(8,128)(2,1)S(1)}, u32[]{:S(2)}, u32[]{:S(2)}) async-start(bf16[16,16,16,128]{3,2,1,0:T(8,128)(2,1)} %copy-done.1), calls=%async_computation.2 | async-start | bytes 2097152 | tf_op jit(solution)/shard_map/all_to_all | solution.py:33
  59.3 2.1 %collective-permute-start.2 = (bf16[384,1024]{1,0:T(8,128)(2,1)}, bf16[384,1024]{1,0:T(8,128)(2,1)S(1)}, u32[]{:S(2)}, u32[]{:S(2)}) collective-permute-start(bf16[384,1024]{1,0:T(8,128)(2,1)} %copy-done.18), channel_id=1, source_target_pairs={{0,1},{1,0},{2,3},{3,2},{4,5},{5,4},{6,7},{7,6},{8,9},{9,8},{10,11... | collective-permute-start | bytes 2359304 | tf_op jit(solution)/shard_map/ppermute | solution.py:421
  61.4 2.3 %collective-permute-done.2.refs_1_ = bf16[384,1024]{1,0:T(8,128)(2,1)S(1)} collective-permute-done((bf16[384,1024]{1,0:T(8,128)(2,1)}, bf16[384,1024]{1,0:T(8,128)(2,1)S(1)}, u32[]{:S(2)}, u32[]{:S(2)}) %collective-permute-start.2) | collective-permute-done | bytes 786464 | tf_op jit(solution)/shard_map/ppermute | solution.py:421
  63.7 1.4 %copy-done.3 = f32[384,1024]{1,0:T(8,128)S(1)} copy-done((f32[384,1024]{1,0:T(8,128)S(1)}, f32[384,1024]{1,0:T(8,128)}, u32[]{:S(2)}) %copy-start.3) | copy-done | bytes 1572888
  65.1 1.1 copy-done.7
  66.3 0.9 copy-done.13
  67.2 2.2 %hidden_grad.2 = bf16[384,1024]{1,0:T(8,128)(2,1)} custom-call(f32[384,1024]{1,0:T(8,128)S(1)} %copy-done.3, bf16[384,1024]{1,0:T(8,128)(2,1)S(1)} %collective-permute-done.2.refs_1_, bf16[384,1024]{1,0:T(8,128)(2,1)S(1)} %copy-done.7, f32[384,1]{1,0:T(8,128)S(1)} %copy-done.13, bf16[1024,1024]{1,0:T(8,128)(2,1)S(1)} %copy-done), custom_call_target="tpu_custom_call" | custom-call | flops 805306368 | bytes 5840000 | tf_op jit(solution)/shard_map/hidden_grad/pallas_call | solution.py:63
  69.3 9.1 %all-to-all-done.2.pieces = bf16[16,16,16,128]{3,2,1,0:T(8,128)(2,1)S(1)} async-done(((bf16[16,16,16,128]{3,2,1,0:T(8,128)(2,1)}), bf16[16,16,16,128]{3,2,1,0:T(8,128)(2,1)S(1)}, u32[]{:S(2)}, u32[]{:S(2)}) %all-to-all-start.2) | async-done | bytes 1048608 | tf_op jit(solution)/shard_map/all_to_all | solution.py:33
  78.5 0.8 sum_pieces.1
  79.2 12.1 %all-to-all-start.3 = ((bf16[16,16,128]{2,1,0:T(8,128)(2,1)}), bf16[16,16,128]{2,1,0:T(8,128)(2,1)S(1)}, u32[]{:S(2)}, u32[]{:S(2)}) async-start(bf16[16,16,128]{2,1,0:T(8,128)(2,1)} %sum_pieces.1), calls=%async_computation.3 | async-start | bytes 131072 | tf_op jit(solution)/shard_map/all_to_all | solution.py:33
  91.3 1.9 %collective-permute-start.3 = (bf16[128,1024]{1,0:T(8,128)(2,1)}, bf16[128,1024]{1,0:T(8,128)(2,1)S(1)}, u32[]{:S(2)}, u32[]{:S(2)}) collective-permute-start(bf16[128,1024]{1,0:T(8,128)(2,1)} %copy-done.21), channel_id=1, source_target_pairs={{6,0},{0,2},{2,4},{4,6},{7,1},{1,3},{3,5},{5,7},{14,8},{8,10},{10,... | collective-permute-start | bytes 786440 | tf_op jit(solution)/shard_map/ppermute | solution.py:427
  93.3 2.6 %collective-permute-start.4 = (bf16[128,1024]{1,0:T(8,128)(2,1)}, bf16[128,1024]{1,0:T(8,128)(2,1)S(1)}, u32[]{:S(2)}, u32[]{:S(2)}) collective-permute-start(bf16[128,1024]{1,0:T(8,128)(2,1)} %copy-done.20), channel_id=1, source_target_pairs={{4,0},{6,2},{0,4},{2,6},{5,1},{7,3},{1,5},{3,7},{12,8},{14,10},{8,... | collective-permute-start | bytes 786440 | tf_op jit(solution)/shard_map/ppermute | solution.py:427
  95.8 4.0 %collective-permute-start.5 = (bf16[128,1024]{1,0:T(8,128)(2,1)}, bf16[128,1024]{1,0:T(8,128)(2,1)S(1)}, u32[]{:S(2)}, u32[]{:S(2)}) collective-permute-start(bf16[128,1024]{1,0:T(8,128)(2,1)} %copy-done.19), channel_id=1, source_target_pairs={{2,0},{4,2},{6,4},{0,6},{3,1},{5,3},{7,5},{1,7},{10,8},{12,10},{14... | collective-permute-start | bytes 786440 | tf_op jit(solution)/shard_map/ppermute | solution.py:427
  99.8 3.1 %all-to-all-done.3.pieces = bf16[16,16,128]{2,1,0:T(8,128)(2,1)S(1)} async-done(((bf16[16,16,128]{2,1,0:T(8,128)(2,1)}), bf16[16,16,128]{2,1,0:T(8,128)(2,1)S(1)}, u32[]{:S(2)}, u32[]{:S(2)}) %all-to-all-start.3) | async-done | bytes 65568 | tf_op jit(solution)/shard_map/all_to_all | solution.py:33
  102.9 0.6 last_sum.1
  103.6 6.3 %all-to-all-start.4 = ((f32[8,16,128]{2,1,0:T(8,128)}), f32[8,16,128]{2,1,0:T(8,128)S(1)}, u32[]{:S(2)}, u32[]{:S(2)}) async-start(f32[8,16,128]{2,1,0:T(8,128)} %last_sum.1), calls=%async_computation.4 | async-start | bytes 131072 | tf_op jit(solution)/shard_map/all_to_all | solution.py:33
  109.8 0.0 collective-permute-done.4.refs_2_
  109.8 0.0 collective-permute-done.5.refs_3_
  109.9 1.0 copy-done.9
  110.9 1.7 %hidden_grad.3 = bf16[128,1024]{1,0:T(8,128)(2,1)} custom-call(f32[128,1024]{1,0:T(8,128)S(1)} %copy-done.9, bf16[128,1024]{1,0:T(8,128)(2,1)S(1)} %collective-permute-done.3.refs_1_, bf16[128,1024]{1,0:T(8,128)(2,1)S(1)} %collective-permute-done.4.refs_2_, bf16[128,1024]{1,0:T(8,128)(2,1)S(1)} %collective-permute-done.5.refs_3_, ...), custom_call_target="tpu_custom_call" | custom-call | flops 268435456 | bytes 3280000 | tf_op jit(solution)/shard_map/hidden_grad/pallas_call | solution.py:63
  112.6 2.1 %all-to-all-done.4.pieces = f32[8,16,128]{2,1,0:T(8,128)S(1)} async-done(((f32[8,16,128]{2,1,0:T(8,128)}), f32[8,16,128]{2,1,0:T(8,128)S(1)}, u32[]{:S(2)}, u32[]{:S(2)}) %all-to-all-start.4) | async-done | bytes 65568 | tf_op jit(solution)/shard_map/all_to_all | solution.py:33
  114.7 0.6 lay.1
  (40 shorter events, 0.1 us)
Async XLA Ops:
  0.6 1.0 copy-start.10
  1.6 0.7 copy-start.16
  2.2 0.7 copy-start.17
  2.9 6.0 %copy-start = (bf16[1024,1024]{1,0:T(8,128)(2,1)S(1)}, bf16[1024,1024]{1,0:T(8,128)(2,1)}, u32[]{:S(2)}) copy-start(bf16[1024,1024]{1,0:T(8,128)(2,1)} %refs_6_) | copy-start | bytes 6291460
  4.0 22.2 %all-to-all-start = ((bf16[4,144,1024]{2,1,0:T(8,128)(2,1)}), bf16[4,144,1024]{2,1,0:T(8,128)(2,1)S(1)}, u32[]{:S(2)}, u32[]{:S(2)}) async-start(bf16[4,144,1024]{2,1,0:T(8,128)(2,1)} %pack.1), calls=%async_computation | async-start | bytes 2359296 | tf_op jit(solution)/shard_map/all_to_all | solution.py:33
  11.1 0.9 copy-start.4
  12.0 0.7 copy-start.11
  12.7 9.7 %collective-permute-start = (bf16[384,1024]{1,0:T(8,128)(2,1)}, bf16[384,1024]{1,0:T(8,128)(2,1)}, u32[]{:S(2)}, u32[]{:S(2)}) collective-permute-start(bf16[384,1024]{1,0:T(8,128)(2,1)} %own.1), channel_id=1, source_target_pairs={{0,1},{1,0},{2,3},{3,2},{4,5},{5,4},{6,7},{7,6},{8,9},{9,8},{10,11... | collective-permute-start | bytes 2359304 | tf_op jit(solution)/shard_map/ppermute | solution.py:409
  24.6 0.9 copy-start.22
  25.5 0.7 copy-start.25
  26.2 1.1 copy-start.5
  27.3 1.1 copy-start.23
  28.5 12.7 %copy-start.6 = (bf16[384,1024]{1,0:T(8,128)(2,1)S(1)}, bf16[384,1024]{1,0:T(8,128)(2,1)}, u32[]{:S(2)}) copy-start(bf16[384,1024]{1,0:T(8,128)(2,1)} %copy-done.4) | copy-start | bytes 2359300
  28.5 12.7 %copy-start.12 = (f32[384,1]{1,0:T(8,128)S(1)}, f32[384,1]{1,0:T(8,128)}, u32[]{:S(2)}) copy-start(f32[384,1]{1,0:T(8,128)} %copy-done.11) | copy-start | bytes 4612
  28.5 12.7 %copy-start.24 = (bf16[384,1024]{1,0:T(8,128)(2,1)S(1)}, bf16[384,1024]{1,0:T(8,128)(2,1)}, u32[]{:S(2)}) copy-start(bf16[384,1024]{1,0:T(8,128)(2,1)} %copy-done.22) | copy-start | bytes 2359300
  28.5 12.7 %copy-start.26 = (f32[384,1]{1,0:T(8,128)S(1)}, f32[384,1]{1,0:T(8,128)}, u32[]{:S(2)}) copy-start(f32[384,1]{1,0:T(8,128)} %copy-done.25) | copy-start | bytes 4612
  47.7 6.7 %copy-start.2 = (f32[384,1024]{1,0:T(8,128)}, f32[384,1024]{1,0:T(8,128)S(1)}, u32[]{:S(2)}) copy-start(f32[384,1024]{1,0:T(8,128)S(1)} %get-tuple-element.53.refs_0_) | copy-start | bytes 4718596
  47.7 6.7 %copy-start.8 = (f32[128,1024]{1,0:T(8,128)}, f32[128,1024]{1,0:T(8,128)S(1)}, u32[]{:S(2)}) copy-start(f32[128,1024]{1,0:T(8,128)S(1)} %get-tuple-element.47.refs_0_) | copy-start | bytes 1572868
  47.7 6.7 %copy-start.14 = (f32[128,1]{1,0:T(8,128)}, f32[128,1]{1,0:T(8,128)S(1)}, u32[]{:S(2)}) copy-start(f32[128,1]{1,0:T(8,128)S(1)} %get-tuple-element.61.refs_5_) | copy-start | bytes 1540
  47.7 6.7 %copy-start.18 = (bf16[384,1024]{1,0:T(8,128)(2,1)}, bf16[384,1024]{1,0:T(8,128)(2,1)S(1)}, u32[]{:S(2)}) copy-start(bf16[384,1024]{1,0:T(8,128)(2,1)S(1)} %get-tuple-element.55) | copy-start | bytes 2359300
  47.7 6.7 %copy-start.19 = (bf16[128,1024]{1,0:T(8,128)(2,1)}, bf16[128,1024]{1,0:T(8,128)(2,1)S(1)}, u32[]{:S(2)}) copy-start(bf16[128,1024]{1,0:T(8,128)(2,1)S(1)} %get-tuple-element.59) | copy-start | bytes 786436
  47.8 6.7 %copy-start.20 = (bf16[128,1024]{1,0:T(8,128)(2,1)}, bf16[128,1024]{1,0:T(8,128)(2,1)S(1)}, u32[]{:S(2)}) copy-start(bf16[128,1024]{1,0:T(8,128)(2,1)S(1)} %get-tuple-element.58) | copy-start | bytes 786436
  47.8 6.7 %copy-start.21 = (bf16[128,1024]{1,0:T(8,128)(2,1)}, bf16[128,1024]{1,0:T(8,128)(2,1)S(1)}, u32[]{:S(2)}) copy-start(bf16[128,1024]{1,0:T(8,128)(2,1)S(1)} %get-tuple-element.57) | copy-start | bytes 786436
  47.8 6.7 %collective-permute-start.1 = (bf16[1024,512]{1,0:T(8,128)(2,1)S(1)}, bf16[1024,512]{1,0:T(8,128)(2,1)S(1)}, u32[]{:S(2)}, u32[]{:S(2)}) collective-permute-start(bf16[1024,512]{1,0:T(8,128)(2,1)S(1)} %get-tuple-element.52), channel_id=1, source_target_pairs={{0,1},{1,0},{2,3},{3,2},{4,5},{5,4},{6,7},{7,6},{8,9},{9,8},{10,11... | collective-permute-start | bytes 3145736 | tf_op jit(solution)/shard_map/ppermute | solution.py:418
  54.7 1.0 copy-start.1
  55.7 22.8 %all-to-all-start.2 = ((bf16[16,16,16,128]{3,2,1,0:T(8,128)(2,1)}), bf16[16,16,16,128]{3,2,1,0:T(8,128)(2,1)S(1)}, u32[]{:S(2)}, u32[]{:S(2)}) async-start(bf16[16,16,16,128]{3,2,1,0:T(8,128)(2,1)} %copy-done.1), calls=%async_computation.2 | async-start | bytes 2097152 | tf_op jit(solution)/shard_map/all_to_all | solution.py:33
  59.3 4.4 %collective-permute-start.2 = (bf16[384,1024]{1,0:T(8,128)(2,1)}, bf16[384,1024]{1,0:T(8,128)(2,1)S(1)}, u32[]{:S(2)}, u32[]{:S(2)}) collective-permute-start(bf16[384,1024]{1,0:T(8,128)(2,1)} %copy-done.18), channel_id=1, source_target_pairs={{0,1},{1,0},{2,3},{3,2},{4,5},{5,4},{6,7},{7,6},{8,9},{9,8},{10,11... | collective-permute-start | bytes 2359304 | tf_op jit(solution)/shard_map/ppermute | solution.py:421
  63.7 1.4 %copy-start.3 = (f32[384,1024]{1,0:T(8,128)S(1)}, f32[384,1024]{1,0:T(8,128)}, u32[]{:S(2)}) copy-start(f32[384,1024]{1,0:T(8,128)} %copy-done.2) | copy-start | bytes 4718596
  65.1 1.1 copy-start.7
  66.3 0.9 copy-start.13
  67.2 42.7 %copy-start.15 = (f32[128,1]{1,0:T(8,128)S(1)}, f32[128,1]{1,0:T(8,128)}, u32[]{:S(2)}) copy-start(f32[128,1]{1,0:T(8,128)} %copy-done.14) | copy-start | bytes 1540
  79.2 23.7 %all-to-all-start.3 = ((bf16[16,16,128]{2,1,0:T(8,128)(2,1)}), bf16[16,16,128]{2,1,0:T(8,128)(2,1)S(1)}, u32[]{:S(2)}, u32[]{:S(2)}) async-start(bf16[16,16,128]{2,1,0:T(8,128)(2,1)} %sum_pieces.1), calls=%async_computation.3 | async-start | bytes 131072 | tf_op jit(solution)/shard_map/all_to_all | solution.py:33
  91.3 18.5 %collective-permute-start.3 = (bf16[128,1024]{1,0:T(8,128)(2,1)}, bf16[128,1024]{1,0:T(8,128)(2,1)S(1)}, u32[]{:S(2)}, u32[]{:S(2)}) collective-permute-start(bf16[128,1024]{1,0:T(8,128)(2,1)} %copy-done.21), channel_id=1, source_target_pairs={{6,0},{0,2},{2,4},{4,6},{7,1},{1,3},{3,5},{5,7},{14,8},{8,10},{10,... | collective-permute-start | bytes 786440 | tf_op jit(solution)/shard_map/ppermute | solution.py:427
  93.3 16.6 %collective-permute-start.4 = (bf16[128,1024]{1,0:T(8,128)(2,1)}, bf16[128,1024]{1,0:T(8,128)(2,1)S(1)}, u32[]{:S(2)}, u32[]{:S(2)}) collective-permute-start(bf16[128,1024]{1,0:T(8,128)(2,1)} %copy-done.20), channel_id=1, source_target_pairs={{4,0},{6,2},{0,4},{2,6},{5,1},{7,3},{1,5},{3,7},{12,8},{14,10},{8,... | collective-permute-start | bytes 786440 | tf_op jit(solution)/shard_map/ppermute | solution.py:427
  95.8 14.0 %collective-permute-start.5 = (bf16[128,1024]{1,0:T(8,128)(2,1)}, bf16[128,1024]{1,0:T(8,128)(2,1)S(1)}, u32[]{:S(2)}, u32[]{:S(2)}) collective-permute-start(bf16[128,1024]{1,0:T(8,128)(2,1)} %copy-done.19), channel_id=1, source_target_pairs={{2,0},{4,2},{6,4},{0,6},{3,1},{5,3},{7,5},{1,7},{10,8},{12,10},{14... | collective-permute-start | bytes 786440 | tf_op jit(solution)/shard_map/ppermute | solution.py:427
  103.6 11.1 %all-to-all-start.4 = ((f32[8,16,128]{2,1,0:T(8,128)}), f32[8,16,128]{2,1,0:T(8,128)S(1)}, u32[]{:S(2)}, u32[]{:S(2)}) async-start(f32[8,16,128]{2,1,0:T(8,128)} %last_sum.1), calls=%async_computation.4 | async-start | bytes 131072 | tf_op jit(solution)/shard_map/all_to_all | solution.py:33
  109.9 1.0 copy-start.9

commit v3 on v2

v3 whole, which is shorter than its diff:
```python
import jax
import jax.numpy as jnp
from jax import lax
from jax.experimental import pallas as pl
from jax.experimental.pallas import tpu as pltpu
from jax.sharding import Mesh, PartitionSpec as P

score_scale = 50.0
epsilon = 1e-06

X, C, Y, Z = 4, 2, 4, 16
SWAP = ((0, 1), (1, 0))
ROWS = 128
WIDTH = 1024
OWN = 384
BLOCKS = OWN // ROWS
CHIP_BLOCKS = BLOCKS * C
NAMES = 8
LANES = 128
PIECES = WIDTH // LANES
EXTRA = 16
LINES = PIECES * ROWS + EXTRA
HALF = WIDTH // C
PART = 256
HBM = pl.BlockSpec(memory_space=pltpu.HBM)
VMEM = pl.BlockSpec(memory_space=pltpu.VMEM)
SMEM = pl.BlockSpec(memory_space=pltpu.SMEM)
F32, BF16 = jnp.float32, jnp.bfloat16
SCORE = 24
GRAD = 32


def shift(k):
    return tuple(((i + k) % X, i) for i in range(X))


def exchange(value, axis):
    return lax.all_to_all(value, axis, split_axis=0, concat_axis=0, tiled=True)


def matmul(a, b):
    return jnp.dot(a, b, preferred_element_type=F32)


def matmul_tn(a, b):
    return lax.dot_general(a, b, (((0,), (0,)), ((), ())), preferred_element_type=F32)


def matmul_nt(a, b):
    return lax.dot_general(a, b, (((1,), (1,)), ((), ())), preferred_element_type=F32)


def back_of(emb, r, grad):
    emb = emb.astype(F32)
    inner = jnp.sum(emb * grad, axis=-1, keepdims=True)
    return r * (grad - inner * emb)


def params(mib):
    return pltpu.CompilerParams(vmem_limit_bytes=mib << 20)


def in_hbm(*values):
    return [pltpu.with_memory_space_constraint(value, pltpu.HBM) for value in values]


def shape(dims, dtype):
    return jax.ShapeDtypeStruct(dims, dtype)


def call(kernel, name, out_shape, in_specs, out_specs, scratch, mib, flops, moved, *args):
    return pl.pallas_call(
        kernel,
        name=name,
        out_shape=out_shape,
        in_specs=in_specs,
        out_specs=out_specs,
        scratch_shapes=scratch,
        compiler_params=params(mib),
        cost_estimate=pl.CostEstimate(flops=flops, bytes_accessed=moved, transcendentals=0),
    )(*args)


def pack_kernel(queries, positive, pairs, out, pos, names, rows, wide, packed, sems):
    inner = [
        pltpu.make_async_copy(queries, rows, sems.at[X]),
        pltpu.make_async_copy(positive, pos, sems.at[X + 1]),
        pltpu.make_async_copy(pairs, names, sems.at[X + 2]),
    ]
    for copy in inner:
        copy.start()
    wide[...] = jnp.full(wide.shape, 255.0, F32)
    inner[1].wait()
    inner[2].wait()
    index = pos[...]
    wide[0:1, :] = (index >> 7).astype(F32)
    wide[1:2, :] = (index & 127).astype(F32)
    wide[2:3, 0:NAMES] = names[...].astype(F32)
    packed[pl.ds(PIECES * ROWS, EXTRA), :] = wide[...].astype(BF16)
    inner[0].wait()
    for j in range(PIECES):
        packed[pl.ds(j * ROWS, ROWS), :] = rows[:, j * LANES : (j + 1) * LANES]
    copies = [pltpu.make_async_copy(packed, out.at[d], sems.at[d]) for d in range(X)]
    for copy in copies:
        copy.start()
    for copy in copies:
        copy.wait()


def pack(queries, positive, pairs):
    return call(
        pack_kernel, "pack",
        pltpu.HBM((X, LINES, LANES), BF16),
        [HBM, HBM, HBM],
        HBM,
        [
            pltpu.VMEM((1, ROWS), jnp.int32),
            pltpu.VMEM((1, NAMES), jnp.int32),
            pltpu.VMEM((ROWS, WIDTH), BF16),
            pltpu.VMEM((EXTRA, LANES), F32),
            pltpu.VMEM((LINES, LANES), BF16),
            pltpu.SemaphoreType.DMA((X + 3,)),
        ],
        4, 0, 1_400_000,
        *in_hbm(queries, positive.reshape(1, ROWS), pairs),
    )


def project(source, weight, proj, r_out, emb, rows):
    for j in range(WIDTH // PART):
        cols = pl.ds(j * PART, PART)
        proj[:, cols] = matmul(source, weight[:, cols])
    for i in range(rows // ROWS):
        here = pl.ds(i * ROWS, ROWS)
        value = proj[here, :]
        r = lax.rsqrt(jnp.sum(value * value, axis=1, keepdims=True) + epsilon)
        r_out[here, :] = r
        emb[here, :] = (value * r).astype(BF16)


def passage_kernel(passages, weight, emb, r_out, proj):
    project(passages[...], weight, proj, r_out, emb, OWN)


def passage_side(passages, weight):
    return call(
        passage_kernel, "passage_side",
        (pltpu.HBM((OWN, WIDTH), BF16), pltpu.HBM((OWN, 1), F32)),
        [VMEM, VMEM],
        (VMEM, VMEM),
        [pltpu.VMEM((OWN, WIDTH), F32)],
        16, 1_000, 1_000,
        passages, weight,
    )


def flat(value):
    return jnp.concatenate([value[k : k + 1] for k in range(X)], axis=1)


def score_kernel(
    place, tiles, weight, emb_own, emb_sib, q_emb, q_r, exponent, send, pos_row, p_emb, rows, proj, sems
):
    x, c = place[0], place[1]
    copies = [
        pltpu.make_async_copy(emb_own, p_emb.at[pl.ds(0, OWN)], sems.at[0]),
        pltpu.make_async_copy(emb_sib, p_emb.at[pl.ds(OWN, OWN)], sems.at[1]),
    ]
    for copy in copies:
        copy.start()
    lines = [tiles[k, PIECES * ROWS : LINES, :].astype(F32) for k in range(X)]
    pos_name, pos_rest, names = [
        jnp.concatenate([line[i : i + 1] for line in lines], axis=0).astype(jnp.int32) for i in range(3)
    ]
    local = names - x * CHIP_BLOCKS
    turned = local + BLOCKS * c
    turned = jnp.where(turned >= CHIP_BLOCKS, turned - CHIP_BLOCKS, turned)
    slot = jnp.where((local >= 0) & (local < CHIP_BLOCKS), turned, -1)
    lane = lax.broadcasted_iota(jnp.int32, (X, ROWS), 1)
    pos_slot = jnp.full((X, ROWS), -1, jnp.int32)
    for n in range(NAMES):
        of_name = jnp.max(jnp.where(lane == n, slot, -1), axis=1, keepdims=True)
        pos_slot = jnp.where(pos_name == n, of_name, pos_slot)
    pos = flat(jnp.where(pos_slot >= 0, pos_slot * ROWS + pos_rest, -1))
    pos_row[...] = pos

    for k in range(X):
        for j in range(PIECES):
            rows[pl.ds(k * ROWS, ROWS), j * LANES : (j + 1) * LANES] = tiles[k, j * ROWS : (j + 1) * ROWS, :]
    project(rows[...], weight, proj, q_r, q_emb, X * ROWS)
    for copy in copies:
        copy.wait()
    line = lax.broadcasted_iota(jnp.int32, (ROWS, X * ROWS), 0)
    total = jnp.zeros((1, X * ROWS), F32)
    picked = jnp.zeros((1, X * ROWS), F32)
    for h in range(C):
        half = matmul_nt(p_emb[pl.ds(h * OWN, OWN), :], q_emb[...])
        for i in range(BLOCKS):
            b = h * BLOCKS + i
            named = jnp.max(jnp.where(slot == b, 1, 0), axis=1, keepdims=True)
            named = flat(jnp.broadcast_to(named, (X, ROWS)))
            scores = half[i * ROWS : (i + 1) * ROWS] * score_scale
            value = jnp.where(named > 0, jnp.exp(scores), 0.0)
            exponent[pl.ds(b * ROWS, ROWS), :] = value
            total = total + jnp.sum(value, axis=0, keepdims=True)
            picked = picked + jnp.sum(jnp.where(line == pos - b * ROWS, scores, 0.0), axis=0, keepdims=True)
    send[...] = jnp.zeros(send.shape, F32)
    for k in range(X):
        lanes = slice(k * ROWS, (k + 1) * ROWS)
        for d in range(X):
            send[d, k : k + 1, :] = total[:, lanes]
        send[k, X : X + 1, :] = picked[:, lanes]


def score_side(place, tiles, weight, emb_own, emb_sib):
    queries = X * ROWS
    passages = CHIP_BLOCKS * ROWS
    return call(
        score_kernel, "score_side",
        (
            shape((queries, WIDTH), BF16),
            shape((queries, 1), F32),
            shape((passages, queries), F32),
            shape((X, 8, ROWS), F32),
            shape((1, queries), jnp.int32),
            shape((passages, WIDTH), BF16),
            shape((queries, WIDTH), BF16),
        ),
        [SMEM] + [VMEM] * 2 + [HBM] * 2,
        (VMEM,) * 7,
        [
            pltpu.VMEM((queries, WIDTH), F32),
            pltpu.SemaphoreType.DMA((2,)),
        ],
        SCORE, 2_000_000_000, 8_000_000,
        place, tiles, weight, *in_hbm(emb_own, emb_sib),
    )


def grad_kernel(
    place, recv, pos_row, exponent, q_r, r_own, r_sib, q_emb, p_emb, q_rows, own, sib,
    losses, g0, g1, g2, g3, emb_mine, r_mine, p_grad_own, p_grad_sib, backs_here, passages, w_there,
    dscore, q_grad, p_grad, backs, sems,
):
    x, c = place[0], place[1]
    queries = X * ROWS
    copies = [
        pltpu.make_async_copy(own, passages.at[pl.ds(0, OWN)], sems.at[0]),
        pltpu.make_async_copy(sib, passages.at[pl.ds(OWN, OWN)], sems.at[1]),
    ]
    for copy in copies:
        copy.start()
    total = recv[0] + recv[1] + recv[2] + recv[3]
    mine = jnp.zeros((1, ROWS), F32)
    for k in range(X):
        mine = mine + jnp.where(x == k, total[k : k + 1], 0.0)
    losses[...] = jnp.log(mine) - total[X : X + 1]
    inverse = 1.0 / flat(total)
    pos = pos_row[...]
    line = lax.broadcasted_iota(jnp.int32, (ROWS, queries), 0)
    for b in range(CHIP_BLOCKS):
        block = pl.ds(b * ROWS, ROWS)
        target = jnp.where(line == pos - b * ROWS, 1.0, 0.0)
        dscore[block, :] = (exponent[block, :] * inverse - target).astype(BF16)

    def keep(rows, emb, r, grad):
        value = back_of(emb, r * score_scale, grad).astype(BF16)
        for h in range(C):
            backs[h, rows, :] = value[:, h * HALF : (h + 1) * HALF]

    for j in range(WIDTH // PART):
        cols = pl.ds(j * PART, PART)
        q_grad[:, cols] = matmul_tn(dscore[...], p_emb[:, cols])
    for j in range(WIDTH // PART):
        cols = pl.ds(j * PART, PART)
        p_grad[:, cols] = matmul(dscore[...], q_emb[:, cols])
    for k in range(X):
        rows = pl.ds(k * ROWS, ROWS)
        keep(rows, q_emb[rows, :], q_r[rows, :], q_grad[rows, :])
    for k, out in enumerate((g0, g1, g2, g3)):
        rows = pl.ds(pl.multiple_of(lax.rem(x + k, X) * ROWS, ROWS), ROWS)
        out[...] = q_grad[rows, :].astype(out.dtype)
    rows = pl.ds(pl.multiple_of(x * ROWS, ROWS), ROWS)
    emb_mine[...] = q_emb[rows, :]
    r_mine[...] = q_r[rows, :]
    for b in range(CHIP_BLOCKS):
        rows = pl.ds(b * ROWS, ROWS)
        first = b < BLOCKS
        near = pl.ds((b % BLOCKS) * ROWS, ROWS)
        grad = p_grad[rows, :]
        (p_grad_own if first else p_grad_sib)[near, :] = grad.astype(F32 if first else BF16)
        r = (r_own if first else r_sib)[near, :]
        keep(pl.ds(queries + b * ROWS, ROWS), p_emb[rows, :], r, grad)
    for copy in copies:
        copy.wait()
    weight_terms(q_rows, passages, backs.at[1 - c], w_there)
    backs_here[...] = backs[c]


def weight_terms(q_rows, passages, backs, out):
    for j in range(WIDTH // PART):
        cols = pl.ds(j * PART, PART)
        hidden = jnp.concatenate([q_rows[:, cols], passages[:, cols]], axis=0)
        out[cols, :] = matmul_tn(hidden, backs[...]).astype(out.dtype)


def grad_side(*args, own, sib):
    queries = X * ROWS
    passages = CHIP_BLOCKS * ROWS
    tile = shape((ROWS, WIDTH), BF16)
    return call(
        grad_kernel, "grad_side",
        (
            shape((1, ROWS), F32),
            pltpu.HBM((ROWS, WIDTH), F32), tile, tile, tile,
            pltpu.HBM((ROWS, WIDTH), BF16),
            pltpu.HBM((ROWS, 1), F32),
            shape((OWN, WIDTH), F32),
            shape((OWN, WIDTH), BF16),
            shape((queries + passages, HALF), BF16),
            shape((passages, WIDTH), BF16),
            shape((WIDTH, HALF), BF16),
        ),
        [SMEM] + [VMEM] * 9 + [HBM] * 2,
        (VMEM,) * 12,
        [
            pltpu.VMEM((passages, queries), BF16),
            pltpu.VMEM((queries, WIDTH), F32),
            pltpu.VMEM((passages, WIDTH), F32),
            pltpu.VMEM((C, queries + passages, HALF), BF16),
            pltpu.SemaphoreType.DMA((2,)),
        ],
        GRAD, 3_000_000_000, 14_000_000,
        *args, *in_hbm(own, sib),
    )


def weight_kernel(backs, q_rows, passages, out):
    weight_terms(q_rows, passages, backs, out)


def weight_here(backs, q_rows, passages):
    return call(
        weight_kernel, "weight_here",
        shape((WIDTH, HALF), F32),
        [VMEM] * 3,
        VMEM,
        [],
        24, 1_350_000_000, 6_000_000,
        backs, q_rows, passages,
    )


def spread_kernel(here, there, out, held, sems):
    own_rows = WIDTH // (Z * Y)
    lanes = HALF // X
    copies = []
    for y in range(Y):
        for z in range(Z):
            rows = pl.ds((z * Y + y) * own_rows, own_rows)
            value = (here[rows, :] + there[rows, :].astype(F32)).astype(BF16)
            for x in range(X):
                held[y * X + x, z] = value[:, x * lanes : (x + 1) * lanes]
        part = pl.ds(y * X, X)
        copies.append(pltpu.make_async_copy(held.at[part], out.at[part], sems.at[y]))
        copies[-1].start()
    for copy in copies:
        copy.wait()


def spread(here, there):
    dims = (Y * X, Z, WIDTH // (Z * Y), HALF // X)
    return call(
        spread_kernel, "spread",
        pltpu.HBM(dims, BF16),
        [VMEM, VMEM],
        HBM,
        [pltpu.VMEM(dims, BF16), pltpu.SemaphoreType.DMA((Y,))],
        16, 500_000, 4_000_000,
        here, there,
    )


def sum_kernel(pieces, out):
    total = pieces[0].astype(F32)
    for k in range(1, pieces.shape[0]):
        total = total + pieces[k].astype(F32)
    out[...] = total.astype(BF16)


def sum_pieces(pieces):
    return call(
        sum_kernel, "sum_pieces", shape(pieces.shape[1:], BF16), [VMEM], VMEM, [], 8, 500_000, 1_000_000, pieces
    )


def last_sum_kernel(pieces, out):
    total = pieces[0].astype(F32)
    for k in range(1, Z):
        total = total + pieces[k].astype(F32)
    total = total * (1.0 / (Z * Y * X * C))
    for d in range(X * C):
        out[d] = total


def last_sum(pieces):
    dims = (X * C,) + pieces.shape[1:]
    return call(
        last_sum_kernel, "last_sum", shape(dims, F32), [VMEM], VMEM, [], 8, 50_000, 100_000, pieces
    )


def lay_kernel(pieces, out):
    lanes = HALF // X
    for x in range(X):
        for c in range(C):
            out[:, c * HALF + x * lanes : c * HALF + (x + 1) * lanes] = pieces[x * C + c]


def lay(pieces):
    dims = (WIDTH // (Z * Y), WIDTH)
    return call(lay_kernel, "lay", shape(dims, F32), [VMEM], VMEM, [], 8, 0, 200_000, pieces)


def hidden_kernel(*refs):
    *terms, emb, r, weight, out = refs
    grad = terms[0][...]
    for term in terms[1:]:
        grad = grad + term[...].astype(F32)
    back = back_of(emb[...], r[...] * score_scale, grad).astype(BF16)
    for j in range(WIDTH // PART):
        cols = pl.ds(j * PART, PART)
        out[:, cols] = matmul_nt(back, weight[cols, :]).astype(BF16)


def hidden_grad(terms, emb, r, weight):
    rows = emb.shape[0]
    return call(
        hidden_kernel, "hidden_grad",
        shape((rows, WIDTH), BF16),
        [VMEM] * (len(terms) + 3),
        VMEM,
        [],
        24, 2 * rows * WIDTH * WIDTH, 2_000_000 + rows * 10_000,
        *in_hbm(terms[0]), *terms[1:], *in_hbm(emb, r), weight,
    )


def body(queries, passages, weight, pairs, positive):
    x = lax.axis_index("x")
    c = lax.axis_index("c")
    place = jnp.stack([x, c]).astype(jnp.int32)

    packed = pack(queries, positive, pairs)
    tiles = exchange(packed, "x")
    passages, weight, _ = lax.optimization_barrier((passages, weight, packed))
    emb_own, r_own = passage_side(passages, weight)
    outgoing, _ = lax.optimization_barrier((passages, emb_own))
    sibling = lax.ppermute(outgoing, "c", SWAP)
    emb_sib, r_sib = passage_side(sibling, weight)

    q_emb, q_r, exponent, send, pos_row, p_emb, q_rows = score_side(place, tiles, weight, emb_own, emb_sib)
    recv = exchange(send, "x")
    losses, g0, g1, g2, g3, emb_mine, r_mine, p_grad, p_grad_sib, backs, hidden, w_there = grad_side(
        place, recv, pos_row, exponent, q_r, r_own, r_sib, q_emb, p_emb, q_rows, own=passages, sib=sibling
    )

    w_there = lax.ppermute(w_there, "c", SWAP)
    w = spread(weight_here(backs, q_rows, hidden), w_there)
    (p_grad_sib, g1, g3), w = lax.optimization_barrier(((p_grad_sib, g1, g3), w))
    p_grad_sib = lax.ppermute(p_grad_sib, "c", SWAP)
    passage_grad = hidden_grad((p_grad, p_grad_sib), emb_own, r_own, weight)
    g1 = lax.ppermute(g1, "x", shift(X - 1))
    g3 = lax.ppermute(g3, "x", shift(X - 3))

    w = sum_pieces(exchange(w, ("y", "x")))
    w, g2, g1, g3, passage_grad = lax.optimization_barrier((w, g2, g1, g3, passage_grad))
    g2 = lax.ppermute(g2, "x", shift(X - 2))
    query_grad = hidden_grad((g0, g1, g2, g3), emb_mine, r_mine, weight)
    w = last_sum(exchange(w, "z"))
    weight_grad = lay(exchange(w, ("x", "c")))
    return losses.reshape(ROWS), query_grad, passage_grad, weight_grad


def solution(mesh):
    torus = Mesh(mesh.devices.reshape(Z, Y, X, C), ("z", "y", "x", "c"))
    every = ("z", "y", "x", "c")
    return jax.shard_map(
        body,
        mesh=torus,
        in_specs=(P(every, None), P(every, None), P(), P(every, None), P(every)),
        out_specs=(P(every), P(every, None), P(every, None), P(("z", "y"), None)),
        check_vma=False,
    )
```

time: 116 us -> 111 us (0.957)
  local copies, waits for them, and re-layouts: 13.2 us -> 0.04 us
  Pallas kernels: 25.3 us -> 29.7 us
  starting transfers between devices: 48.6 us -> 52 us
    unnamed x54 -> x16, local copies, waits for them, and re-layouts: 13.2 us -> 0.04 us
    pallas_call x12, Pallas kernels: 25.3 us -> 29.7 us  [call(): pl.pallas_call(kernel, name=name, out_shape=out_shape, in_specs=in_specs,...]
    ppermute x3, waiting for transfers between devices: 0.01 us -> 2.67 us  [the longest x1 2.66 us: body(): g1 = lax.ppermute(g1, 'x', shift(X - 1))]
    ppermute x1, waiting for transfers between devices: 2.28 us -> 0.01 us  [body(): p_grad_sib = lax.ppermute(p_grad_sib, 'c', SWAP)]
    ppermute x3, starting transfers between devices: 8.46 us -> 10.5 us  [the longest x1 3.9 us: body(): g2 = lax.ppermute(g2, 'x', shift(X - 2))]
    all_to_all x4, starting transfers between devices: 26.9 us -> 28.1 us  [exchange(): return lax.all_to_all(value, axis, split_axis=0, concat_axis=0, tiled=True)]
  transfers between devices with their start and end apart: 10 -> 10, of which waited for: 5 -> 6; matrix products, arithmetic and copies ran while one was open for 0% -> 0% of each run, Pallas kernels for 10% -> 14%
where the time goes in v3:
time: 111 us
  starting transfers between devices  52 us (47%)
  Pallas kernels  29.7 us (27%)
  waiting for transfers between devices  19.5 us (18%)
  blocking collectives  8.49 us (8%)
    pallas_call x12, Pallas kernels, call(): pl.pallas_call(kernel, name=name, out_shape=out_shape, in_specs=in_specs,...  29.7 us
    all_to_all x4, starting transfers between devices, exchange(): return lax.all_to_all(value, axis, split_axis=0, concat_axis=0, tiled=True)  28.1 us
    all_to_all x4, waiting for transfers between devices, exchange(): return lax.all_to_all(value, axis, split_axis=0, concat_axis=0, tiled=True)  14 us
    all_to_all x1, blocking collectives, exchange(): return lax.all_to_all(value, axis, split_axis=0, concat_axis=0, tiled=True)  8.49 us
    ppermute x1, starting transfers between devices, body(): sibling = lax.ppermute(outgoing, 'c', SWAP)  7.47 us
    ppermute x1, starting transfers between devices, body(): g2 = lax.ppermute(g2, 'x', shift(X - 2))  3.9 us
    ppermute x1, starting transfers between devices, body(): w_there = lax.ppermute(w_there, 'c', SWAP)  3.71 us
    ppermute x1, starting transfers between devices, body(): g1 = lax.ppermute(g1, 'x', shift(X - 1))  3.42 us
  transfers between devices with their start and end apart: 10, of which 6 were waited for; matrix products, arithmetic and copies ran while one was open for 0% of the time, Pallas kernels for 14%

profile of v3, /device:TPU:1, one launch (start us, length us, event | category | flops | bytes accessed | tf_op | source)
XLA Modules:
  0.0 110.6 jit_solution(11274260255595117204)
XLA Ops:
  0.6 0.0 copy-start
  0.6 2.2 %pack.1 = bf16[4,1040,128]{2,1,0:T(8,128)(2,1)} custom-call(bf16[128,1024]{1,0:T(8,128)(2,1)} %queries.1, s32[1,128]{1,0:T(1,128)} %bitcast.4, s32[1,8]{1,0:T(1,128)} %pairs.1), custom_call_target="tpu_custom_call" | custom-call | bytes 1400000 | tf_op jit(solution)/shard_map/pack/pallas_call | solution.py:72
  2.9 4.9 %all-to-all-start = ((bf16[4,1040,128]{2,1,0:T(8,128)(2,1)}), bf16[4,1040,128]{2,1,0:T(8,128)(2,1)S(1)}, u32[]{:S(2)}, u32[]{:S(2)}) async-start(bf16[4,1040,128]{2,1,0:T(8,128)(2,1)} %pack.1), calls=%async_computation | async-start | bytes 2129920 | tf_op jit(solution)/shard_map/all_to_all | solution.py:38
  7.7 0.0 copy-done
  7.7 3.2 %passage_side.2 = (bf16[384,1024]{1,0:T(8,128)(2,1)}, f32[384,1]{1,0:T(8,128)}) custom-call(bf16[384,1024]{1,0:T(8,128)(2,1)} %own, bf16[1024,1024]{1,0:T(8,128)(2,1)S(1)} %copy-done), custom_call_target="tpu_custom_call" | custom-call | flops 1000 | bytes 1000 | tf_op jit(solution)/shard_map/passage_side/pallas_call | solution.py:72
  10.9 7.5 %collective-permute-start = (bf16[384,1024]{1,0:T(8,128)(2,1)}, bf16[384,1024]{1,0:T(8,128)(2,1)}, u32[]{:S(2)}, u32[]{:S(2)}) collective-permute-start(bf16[384,1024]{1,0:T(8,128)(2,1)} %own), channel_id=1, source_target_pairs={{0,1},{1,0},{2,3},{3,2},{4,5},{5,4},{6,7},{7,6},{8,9},{9,8},{10,11... | collective-permute-start | bytes 2359304 | tf_op jit(solution)/shard_map/ppermute | solution.py:459
  18.4 0.1 pad_add_fusion.place
  18.5 2.2 %collective-permute-done.passages.sib = bf16[384,1024]{1,0:T(8,128)(2,1)} collective-permute-done((bf16[384,1024]{1,0:T(8,128)(2,1)}, bf16[384,1024]{1,0:T(8,128)(2,1)}, u32[]{:S(2)}, u32[]{:S(2)}) %collective-permute-start) | collective-permute-done | bytes 786464 | tf_op jit(solution)/shard_map/ppermute | solution.py:459
  20.6 3.2 %passage_side.3 = (bf16[384,1024]{1,0:T(8,128)(2,1)}, f32[384,1]{1,0:T(8,128)}) custom-call(bf16[384,1024]{1,0:T(8,128)(2,1)} %collective-permute-done.passages.sib, bf16[1024,1024]{1,0:T(8,128)(2,1)S(1)} %copy-done), custom_call_target="tpu_custom_call" | custom-call | flops 1000 | bytes 1000 | tf_op jit(solution)/shard_map/passage_side/pallas_call | solution.py:72
  23.8 0.0 all-to-all-done.tiles
  23.8 4.0 %score_side.1 = (bf16[512,1024]{1,0:T(8,128)(2,1)S(1)}, f32[512,1]{1,0:T(8,128)S(1)}, f32[768,512]{1,0:T(8,128)S(1)}, f32[4,8,128]{2,1,0:T(8,128)S(1)}, s32[1,51...) custom-call(s32[2]{0:T(128)S(1)} %pad_add_fusion.place, ...), custom_call_target="tpu_custom_call" | custom-call | flops 2000000000 | bytes 8000000 | tf_op jit(solution)/shard_map/score_side/pallas_call | solution.py:72
  27.8 8.5 %all_to_all.25.recv = f32[4,8,128]{2,1,0:T(8,128)S(1)} all-to-all(f32[4,8,128]{2,1,0:T(8,128)S(1)} %get-tuple-element.44), channel_id=1, replica_groups=mesh['z'=16,'y'=4,'x'=4,'c'=2] {'x'}, dimensions={0} | all-to-all | bytes 32768 | tf_op jit(solution)/shard_map/all_to_all | solution.py:38
  36.3 0.0 copy-done.2
  36.3 0.0 copy-done.7
  36.3 5.8 %grad_side.1 = (f32[1,128]{1,0:T(1,128)}, f32[128,1024]{1,0:T(8,128)}, bf16[128,1024]{1,0:T(8,128)(2,1)S(1)}, bf16[128,1024]{1,0:T(8,128)(2,1)S(1)}, bf16[128,10...) custom-call(s32[2]{0:T(128)S(1)} %pad_add_fusion.place, ...), custom_call_target="tpu_custom_call" | custom-call | flops 3000000000 | bytes 14000000 | tf_op jit(solution)/shard_map/grad_side/pallas_call | solution.py:72
  42.1 0.0 copy-start.1
  42.1 0.0 copy-start.3
  42.1 0.0 copy-start.4
  42.1 0.0 copy-start.5
  42.2 0.0 copy-start.6
  42.2 3.7 %collective-permute-start.1 = (bf16[1024,512]{1,0:T(8,128)(2,1)S(1)}, bf16[1024,512]{1,0:T(8,128)(2,1)S(1)}, u32[]{:S(2)}, u32[]{:S(2)}) collective-permute-start(bf16[1024,512]{1,0:T(8,128)(2,1)S(1)} %get-tuple-element.60), channel_id=1, source_target_pairs={{0,1},{1,0},{2,3},{3,2},{4,5},{5,4},{6,7},{7,6},{8,9},{9,8},{10,11... | collective-permute-start | bytes 3145736 | tf_op jit(solution)/shard_map/ppermute | solution.py:468
  45.9 1.6 %weight_here.1.here = f32[1024,512]{1,0:T(8,128)S(1)} custom-call(bf16[1280,512]{1,0:T(8,128)(2,1)S(1)} %get-tuple-element.58.backs, bf16[512,1024]{1,0:T(8,128)(2,1)S(1)} %get-tuple-element.52.q_rows, bf16[768,1024]{1,0:T(8,128)(2,1)S(1)} %get-tuple-element.59.passages), custom_call_target="tpu_custom_call" | custom-call | flops 1350000000 | bytes 6000000 | tf_op jit(solution)/shard_map/weight_here/pallas_call | solution.py:72
  47.4 0.0 copy-done.1
  47.5 0.0 copy-done.3
  47.5 0.0 copy-done.4
  47.5 0.0 copy-done.5
  47.5 0.0 copy-done.6
  47.5 0.7 collective-permute-done.1.there
  48.2 1.1 spread.1
  49.2 3.7 %all-to-all-start.2 = ((bf16[16,16,16,128]{3,2,1,0:T(8,128)(2,1)}), bf16[16,16,16,128]{3,2,1,0:T(8,128)(2,1)S(1)}, u32[]{:S(2)}, u32[]{:S(2)}) async-start(bf16[16,16,16,128]{3,2,1,0:T(8,128)(2,1)} %spread.1), calls=%async_computation.2 | async-start | bytes 2097152 | tf_op jit(solution)/shard_map/all_to_all | solution.py:38
  52.9 2.3 %collective-permute-start.4 = (bf16[384,1024]{1,0:T(8,128)(2,1)}, bf16[384,1024]{1,0:T(8,128)(2,1)S(1)}, u32[]{:S(2)}, u32[]{:S(2)}) collective-permute-start(bf16[384,1024]{1,0:T(8,128)(2,1)} %copy-done.3), channel_id=1, source_target_pairs={{0,1},{1,0},{2,3},{3,2},{4,5},{5,4},{6,7},{7,6},{8,9},{9,8},{10,11... | collective-permute-start | bytes 2359304 | tf_op jit(solution)/shard_map/ppermute | solution.py:471
  55.2 3.4 %collective-permute-start.2 = (bf16[128,1024]{1,0:T(8,128)(2,1)}, bf16[128,1024]{1,0:T(8,128)(2,1)S(1)}, u32[]{:S(2)}, u32[]{:S(2)}) collective-permute-start(bf16[128,1024]{1,0:T(8,128)(2,1)} %copy-done.6), channel_id=1, source_target_pairs={{6,0},{0,2},{2,4},{4,6},{7,1},{1,3},{3,5},{5,7},{14,8},{8,10},{10,... | collective-permute-start | bytes 786440 | tf_op jit(solution)/shard_map/ppermute | solution.py:473
  58.6 3.1 %collective-permute-start.3 = (bf16[128,1024]{1,0:T(8,128)(2,1)}, bf16[128,1024]{1,0:T(8,128)(2,1)}, u32[]{:S(2)}, u32[]{:S(2)}) collective-permute-start(bf16[128,1024]{1,0:T(8,128)(2,1)} %copy-done.5), channel_id=1, source_target_pairs={{2,0},{4,2},{6,4},{0,6},{3,1},{5,3},{7,5},{1,7},{10,8},{12,10},{14... | collective-permute-start | bytes 786440 | tf_op jit(solution)/shard_map/ppermute | solution.py:474
  61.8 0.0 collective-permute-done.4.refs_1_
  61.8 3.8 %hidden_grad.2 = bf16[384,1024]{1,0:T(8,128)(2,1)} custom-call(f32[384,1024]{1,0:T(8,128)} %copy-done.1, bf16[384,1024]{1,0:T(8,128)(2,1)S(1)} %collective-permute-done.4.refs_1_, bf16[384,1024]{1,0:T(8,128)(2,1)} %get-tuple-element.41.emb_own.refs_2_, f32[384,1]{1,0:T(8,128)} %get-tuple-element.48.r_own.refs_3_, bf16[1024,1024]{1,0:T(8,128)(2,1)S(1)} %copy-done), custom_call_target="tpu_custom_call" | custom-call | flops 805306368 | bytes 5840000 | tf_op jit(solution)/shard_map/hidden_grad/pallas_call | solution.py:72
  65.6 4.3 %all-to-all-done.2.pieces = bf16[16,16,16,128]{3,2,1,0:T(8,128)(2,1)S(1)} async-done(((bf16[16,16,16,128]{3,2,1,0:T(8,128)(2,1)}), bf16[16,16,16,128]{3,2,1,0:T(8,128)(2,1)S(1)}, u32[]{:S(2)}, u32[]{:S(2)}) %all-to-all-start.2) | async-done | bytes 1048608 | tf_op jit(solution)/shard_map/all_to_all | solution.py:38
  69.9 0.8 sum_pieces.1
  70.6 2.7 %collective-permute-done.2.refs_1_ = bf16[128,1024]{1,0:T(8,128)(2,1)S(1)} collective-permute-done((bf16[128,1024]{1,0:T(8,128)(2,1)}, bf16[128,1024]{1,0:T(8,128)(2,1)S(1)}, u32[]{:S(2)}, u32[]{:S(2)}) %collective-permute-start.2) | collective-permute-done | bytes 262176 | tf_op jit(solution)/shard_map/ppermute | solution.py:473
  73.3 0.0 collective-permute-done.3.refs_3_
  73.3 13.8 %all-to-all-start.3 = ((bf16[16,16,128]{2,1,0:T(8,128)(2,1)}), bf16[16,16,128]{2,1,0:T(8,128)(2,1)S(1)}, u32[]{:S(2)}, u32[]{:S(2)}) async-start(bf16[16,16,128]{2,1,0:T(8,128)(2,1)} %sum_pieces.1), calls=%async_computation.3 | async-start | bytes 131072 | tf_op jit(solution)/shard_map/all_to_all | solution.py:38
  87.1 3.9 %collective-permute-start.5 = (bf16[128,1024]{1,0:T(8,128)(2,1)}, bf16[128,1024]{1,0:T(8,128)(2,1)S(1)}, u32[]{:S(2)}, u32[]{:S(2)}) collective-permute-start(bf16[128,1024]{1,0:T(8,128)(2,1)} %copy-done.4), channel_id=1, source_target_pairs={{4,0},{6,2},{0,4},{2,6},{5,1},{7,3},{1,5},{3,7},{12,8},{14,10},{8,... | collective-permute-start | bytes 786440 | tf_op jit(solution)/shard_map/ppermute | solution.py:478
  91.0 7.7 %all-to-all-done.3.pieces = bf16[16,16,128]{2,1,0:T(8,128)(2,1)S(1)} async-done(((bf16[16,16,128]{2,1,0:T(8,128)(2,1)}), bf16[16,16,128]{2,1,0:T(8,128)(2,1)S(1)}, u32[]{:S(2)}, u32[]{:S(2)}) %all-to-all-start.3) | async-done | bytes 65568 | tf_op jit(solution)/shard_map/all_to_all | solution.py:38
  98.7 0.6 last_sum.1
  99.3 5.8 %all-to-all-start.4 = ((f32[8,16,128]{2,1,0:T(8,128)}), f32[8,16,128]{2,1,0:T(8,128)S(1)}, u32[]{:S(2)}, u32[]{:S(2)}) async-start(f32[8,16,128]{2,1,0:T(8,128)} %last_sum.1), calls=%async_computation.4 | async-start | bytes 131072 | tf_op jit(solution)/shard_map/all_to_all | solution.py:38
  105.1 0.0 collective-permute-done.5.refs_2_
  105.1 2.9 %hidden_grad.3 = bf16[128,1024]{1,0:T(8,128)(2,1)} custom-call(f32[128,1024]{1,0:T(8,128)} %get-tuple-element.54.refs_0_, bf16[128,1024]{1,0:T(8,128)(2,1)S(1)} %collective-permute-done.2.refs_1_, bf16[128,1024]{1,0:T(8,128)(2,1)S(1)} %collective-permute-done.5.refs_2_, bf16[128,1024]{1,0:T(8,128)(2,1)} %collective-permute-done.3.refs_3_, ...), custom_call_target="tpu_custom_call" | custom-call | flops 268435456 | bytes 3280000 | tf_op jit(solution)/shard_map/hidden_grad/pallas_call | solution.py:72
  108.0 2.0 %all-to-all-done.4.pieces = f32[8,16,128]{2,1,0:T(8,128)S(1)} async-done(((f32[8,16,128]{2,1,0:T(8,128)}), f32[8,16,128]{2,1,0:T(8,128)S(1)}, u32[]{:S(2)}, u32[]{:S(2)}) %all-to-all-start.4) | async-done | bytes 65568 | tf_op jit(solution)/shard_map/all_to_all | solution.py:38
  110.0 0.6 lay.1
  (2 shorter events, 0.0 us)
Async XLA Ops:
  0.6 7.1 %copy-start = (bf16[1024,1024]{1,0:T(8,128)(2,1)S(1)}, bf16[1024,1024]{1,0:T(8,128)(2,1)}, u32[]{:S(2)}) copy-start(bf16[1024,1024]{1,0:T(8,128)(2,1)} %refs_6_) | copy-start | bytes 6291460
  2.9 20.9 %all-to-all-start = ((bf16[4,1040,128]{2,1,0:T(8,128)(2,1)}), bf16[4,1040,128]{2,1,0:T(8,128)(2,1)S(1)}, u32[]{:S(2)}, u32[]{:S(2)}) async-start(bf16[4,1040,128]{2,1,0:T(8,128)(2,1)} %pack.1), calls=%async_computation | async-start | bytes 2129920 | tf_op jit(solution)/shard_map/all_to_all | solution.py:38
  10.9 9.7 %collective-permute-start = (bf16[384,1024]{1,0:T(8,128)(2,1)}, bf16[384,1024]{1,0:T(8,128)(2,1)}, u32[]{:S(2)}, u32[]{:S(2)}) collective-permute-start(bf16[384,1024]{1,0:T(8,128)(2,1)} %own), channel_id=1, source_target_pairs={{0,1},{1,0},{2,3},{3,2},{4,5},{5,4},{6,7},{7,6},{8,9},{9,8},{10,11... | collective-permute-start | bytes 2359304 | tf_op jit(solution)/shard_map/ppermute | solution.py:459
  23.8 12.5 %copy-start.2 = (f32[384,1]{1,0:T(8,128)S(1)}, f32[384,1]{1,0:T(8,128)}, u32[]{:S(2)}) copy-start(f32[384,1]{1,0:T(8,128)} %get-tuple-element.48.r_own.refs_3_) | copy-start | bytes 4612
  23.8 12.5 %copy-start.7 = (f32[384,1]{1,0:T(8,128)S(1)}, f32[384,1]{1,0:T(8,128)}, u32[]{:S(2)}) copy-start(f32[384,1]{1,0:T(8,128)} %get-tuple-element.49.r_sib) | copy-start | bytes 4612
  42.1 5.3 %copy-start.1 = (f32[384,1024]{1,0:T(8,128)}, f32[384,1024]{1,0:T(8,128)S(1)}, u32[]{:S(2)}) copy-start(f32[384,1024]{1,0:T(8,128)S(1)} %get-tuple-element.65.refs_0_) | copy-start | bytes 4718596
  42.1 5.3 %copy-start.3 = (bf16[384,1024]{1,0:T(8,128)(2,1)}, bf16[384,1024]{1,0:T(8,128)(2,1)S(1)}, u32[]{:S(2)}) copy-start(bf16[384,1024]{1,0:T(8,128)(2,1)S(1)} %get-tuple-element.66) | copy-start | bytes 2359300
  42.1 5.3 %copy-start.4 = (bf16[128,1024]{1,0:T(8,128)(2,1)}, bf16[128,1024]{1,0:T(8,128)(2,1)S(1)}, u32[]{:S(2)}) copy-start(bf16[128,1024]{1,0:T(8,128)(2,1)S(1)} %get-tuple-element.68) | copy-start | bytes 786436
  42.1 5.3 %copy-start.5 = (bf16[128,1024]{1,0:T(8,128)(2,1)}, bf16[128,1024]{1,0:T(8,128)(2,1)S(1)}, u32[]{:S(2)}) copy-start(bf16[128,1024]{1,0:T(8,128)(2,1)S(1)} %get-tuple-element.64) | copy-start | bytes 786436
  42.2 5.3 %copy-start.6 = (bf16[128,1024]{1,0:T(8,128)(2,1)}, bf16[128,1024]{1,0:T(8,128)(2,1)S(1)}, u32[]{:S(2)}) copy-start(bf16[128,1024]{1,0:T(8,128)(2,1)S(1)} %get-tuple-element.63) | copy-start | bytes 786436
  42.2 6.0 %collective-permute-start.1 = (bf16[1024,512]{1,0:T(8,128)(2,1)S(1)}, bf16[1024,512]{1,0:T(8,128)(2,1)S(1)}, u32[]{:S(2)}, u32[]{:S(2)}) collective-permute-start(bf16[1024,512]{1,0:T(8,128)(2,1)S(1)} %get-tuple-element.60), channel_id=1, source_target_pairs={{0,1},{1,0},{2,3},{3,2},{4,5},{5,4},{6,7},{7,6},{8,9},{9,8},{10,11... | collective-permute-start | bytes 3145736 | tf_op jit(solution)/shard_map/ppermute | solution.py:468
  49.2 20.7 %all-to-all-start.2 = ((bf16[16,16,16,128]{3,2,1,0:T(8,128)(2,1)}), bf16[16,16,16,128]{3,2,1,0:T(8,128)(2,1)S(1)}, u32[]{:S(2)}, u32[]{:S(2)}) async-start(bf16[16,16,16,128]{3,2,1,0:T(8,128)(2,1)} %spread.1), calls=%async_computation.2 | async-start | bytes 2097152 | tf_op jit(solution)/shard_map/all_to_all | solution.py:38
  52.9 8.9 %collective-permute-start.4 = (bf16[384,1024]{1,0:T(8,128)(2,1)}, bf16[384,1024]{1,0:T(8,128)(2,1)S(1)}, u32[]{:S(2)}, u32[]{:S(2)}) collective-permute-start(bf16[384,1024]{1,0:T(8,128)(2,1)} %copy-done.3), channel_id=1, source_target_pairs={{0,1},{1,0},{2,3},{3,2},{4,5},{5,4},{6,7},{7,6},{8,9},{9,8},{10,11... | collective-permute-start | bytes 2359304 | tf_op jit(solution)/shard_map/ppermute | solution.py:471
  55.2 18.1 %collective-permute-start.2 = (bf16[128,1024]{1,0:T(8,128)(2,1)}, bf16[128,1024]{1,0:T(8,128)(2,1)S(1)}, u32[]{:S(2)}, u32[]{:S(2)}) collective-permute-start(bf16[128,1024]{1,0:T(8,128)(2,1)} %copy-done.6), channel_id=1, source_target_pairs={{6,0},{0,2},{2,4},{4,6},{7,1},{1,3},{3,5},{5,7},{14,8},{8,10},{10,... | collective-permute-start | bytes 786440 | tf_op jit(solution)/shard_map/ppermute | solution.py:473
  58.6 14.7 %collective-permute-start.3 = (bf16[128,1024]{1,0:T(8,128)(2,1)}, bf16[128,1024]{1,0:T(8,128)(2,1)}, u32[]{:S(2)}, u32[]{:S(2)}) collective-permute-start(bf16[128,1024]{1,0:T(8,128)(2,1)} %copy-done.5), channel_id=1, source_target_pairs={{2,0},{4,2},{6,4},{0,6},{3,1},{5,3},{7,5},{1,7},{10,8},{12,10},{14... | collective-permute-start | bytes 786440 | tf_op jit(solution)/shard_map/ppermute | solution.py:474
  73.3 25.4 %all-to-all-start.3 = ((bf16[16,16,128]{2,1,0:T(8,128)(2,1)}), bf16[16,16,128]{2,1,0:T(8,128)(2,1)S(1)}, u32[]{:S(2)}, u32[]{:S(2)}) async-start(bf16[16,16,128]{2,1,0:T(8,128)(2,1)} %sum_pieces.1), calls=%async_computation.3 | async-start | bytes 131072 | tf_op jit(solution)/shard_map/all_to_all | solution.py:38
  87.1 18.0 %collective-permute-start.5 = (bf16[128,1024]{1,0:T(8,128)(2,1)}, bf16[128,1024]{1,0:T(8,128)(2,1)S(1)}, u32[]{:S(2)}, u32[]{:S(2)}) collective-permute-start(bf16[128,1024]{1,0:T(8,128)(2,1)} %copy-done.4), channel_id=1, source_target_pairs={{4,0},{6,2},{0,4},{2,6},{5,1},{7,3},{1,5},{3,7},{12,8},{14,10},{8,... | collective-permute-start | bytes 786440 | tf_op jit(solution)/shard_map/ppermute | solution.py:478
  99.3 10.6 %all-to-all-start.4 = ((f32[8,16,128]{2,1,0:T(8,128)}), f32[8,16,128]{2,1,0:T(8,128)S(1)}, u32[]{:S(2)}, u32[]{:S(2)}) async-start(f32[8,16,128]{2,1,0:T(8,128)} %last_sum.1), calls=%async_computation.4 | async-start | bytes 131072 | tf_op jit(solution)/shard_map/all_to_all | solution.py:38

commit v4 on v3

--- a/solution.py
+++ b/solution.py
@@ -21,7 +21,7 @@
 EXTRA = 16
 LINES = PIECES * ROWS + EXTRA
 HALF = WIDTH // C
-PART = 256
+PART = 512
 HBM = pl.BlockSpec(memory_space=pltpu.HBM)
 VMEM = pl.BlockSpec(memory_space=pltpu.VMEM)
 SMEM = pl.BlockSpec(memory_space=pltpu.SMEM)
@@ -159,14 +159,20 @@
 
 
 def score_kernel(
-    place, tiles, weight, emb_own, emb_sib, q_emb, q_r, exponent, send, pos_row, p_emb, rows, proj, sems
+    place, tiles, weight, emb_own, emb_sib, own, sib,
+    q_emb, q_r, exponent, send, pos_row, p_emb, rows, passages, emb_mine, r_mine,
+    proj, sems,
 ):
     x, c = place[0], place[1]
     copies = [
         pltpu.make_async_copy(emb_own, p_emb.at[pl.ds(0, OWN)], sems.at[0]),
         pltpu.make_async_copy(emb_sib, p_emb.at[pl.ds(OWN, OWN)], sems.at[1]),
     ]
-    for copy in copies:
+    late = [
+        pltpu.make_async_copy(own, passages.at[pl.ds(0, OWN)], sems.at[2]),
+        pltpu.make_async_copy(sib, passages.at[pl.ds(OWN, OWN)], sems.at[3]),
+    ]
+    for copy in copies + late:
         copy.start()
     lines = [tiles[k, PIECES * ROWS : LINES, :].astype(F32) for k in range(X)]
     pos_name, pos_rest, names = [
@@ -190,6 +196,13 @@
     project(rows[...], weight, proj, q_r, q_emb, X * ROWS)
     for copy in copies:
         copy.wait()
+    mine = pl.ds(pl.multiple_of(x * ROWS, ROWS), ROWS)
+    kept = [
+        pltpu.make_async_copy(q_emb.at[mine], emb_mine, sems.at[4]),
+        pltpu.make_async_copy(q_r.at[mine], r_mine, sems.at[5]),
+    ]
+    for copy in kept:
+        copy.start()
     line = lax.broadcasted_iota(jnp.int32, (ROWS, X * ROWS), 0)
     total = jnp.zeros((1, X * ROWS), F32)
     picked = jnp.zeros((1, X * ROWS), F32)
@@ -210,9 +223,11 @@
         for d in range(X):
             send[d, k : k + 1, :] = total[:, lanes]
         send[k, X : X + 1, :] = picked[:, lanes]
-
-
-def score_side(place, tiles, weight, emb_own, emb_sib):
+    for copy in late + kept:
+        copy.wait()
+
+
+def score_side(place, tiles, weight, emb_own, emb_sib, own, sib):
     queries = X * ROWS
     passages = CHIP_BLOCKS * ROWS
     return call(
@@ -225,31 +240,28 @@
             shape((1, queries), jnp.int32),
             shape((passages, WIDTH), BF16),
             shape((queries, WIDTH), BF16),
+            shape((passages, WIDTH), BF16),
+            pltpu.HBM((ROWS, WIDTH), BF16),
+            pltpu.HBM((ROWS, 1), F32),
         ),
-        [SMEM] + [VMEM] * 2 + [HBM] * 2,
-        (VMEM,) * 7,
+        [SMEM] + [VMEM] * 2 + [HBM] * 4,
+        (VMEM,) * 8 + (HBM,) * 2,
         [
             pltpu.VMEM((queries, WIDTH), F32),
-            pltpu.SemaphoreType.DMA((2,)),
+            pltpu.SemaphoreType.DMA((6,)),
         ],
         SCORE, 2_000_000_000, 8_000_000,
-        place, tiles, weight, *in_hbm(emb_own, emb_sib),
+        place, tiles, weight, *in_hbm(emb_own, emb_sib, own, sib),
     )
 
 
 def grad_kernel(
-    place, recv, pos_row, exponent, q_r, r_own, r_sib, q_emb, p_emb, q_rows, own, sib,
-    losses, g0, g1, g2, g3, emb_mine, r_mine, p_grad_own, p_grad_sib, backs_here, passages, w_there,
-    dscore, q_grad, p_grad, backs, sems,
+    place, recv, pos_row, exponent, q_r, r_own, r_sib, q_emb, p_emb, q_rows, passages,
+    losses, g0, g1, g2, g3, p_grad_own, p_grad_sib, backs_here, w_there,
+    dscore, q_grad, p_grad, backs,
 ):
     x, c = place[0], place[1]
     queries = X * ROWS
-    copies = [
-        pltpu.make_async_copy(own, passages.at[pl.ds(0, OWN)], sems.at[0]),
-        pltpu.make_async_copy(sib, passages.at[pl.ds(OWN, OWN)], sems.at[1]),
-    ]
-    for copy in copies:
-        copy.start()
     total = recv[0] + recv[1] + recv[2] + recv[3]
     mine = jnp.zeros((1, ROWS), F32)
     for k in range(X):
@@ -265,14 +277,15 @@
 
     def keep(rows, emb, r, grad):
         value = back_of(emb, r * score_scale, grad).astype(BF16)
-        for h in range(C):
-            backs[h, rows, :] = value[:, h * HALF : (h + 1) * HALF]
-
-    for j in range(WIDTH // PART):
-        cols = pl.ds(j * PART, PART)
+        low, high = value[:, :HALF], value[:, HALF:]
+        backs[0, rows, :] = jnp.where(c == 0, low, high)
+        backs[1, rows, :] = jnp.where(c == 0, high, low)
+
+    for j in range(WIDTH // HALF):
+        cols = pl.ds(j * HALF, HALF)
         q_grad[:, cols] = matmul_tn(dscore[...], p_emb[:, cols])
-    for j in range(WIDTH // PART):
-        cols = pl.ds(j * PART, PART)
+    for j in range(WIDTH // HALF):
+        cols = pl.ds(j * HALF, HALF)
         p_grad[:, cols] = matmul(dscore[...], q_emb[:, cols])
     for k in range(X):
         rows = pl.ds(k * ROWS, ROWS)
@@ -280,9 +293,6 @@
     for k, out in enumerate((g0, g1, g2, g3)):
         rows = pl.ds(pl.multiple_of(lax.rem(x + k, X) * ROWS, ROWS), ROWS)
         out[...] = q_grad[rows, :].astype(out.dtype)
-    rows = pl.ds(pl.multiple_of(x * ROWS, ROWS), ROWS)
-    emb_mine[...] = q_emb[rows, :]
-    r_mine[...] = q_r[rows, :]
     for b in range(CHIP_BLOCKS):
         rows = pl.ds(b * ROWS, ROWS)
         first = b < BLOCKS
@@ -291,20 +301,18 @@
         (p_grad_own if first else p_grad_sib)[near, :] = grad.astype(F32 if first else BF16)
         r = (r_own if first else r_sib)[near, :]
         keep(pl.ds(queries + b * ROWS, ROWS), p_emb[rows, :], r, grad)
-    for copy in copies:
-        copy.wait()
-    weight_terms(q_rows, passages, backs.at[1 - c], w_there)
-    backs_here[...] = backs[c]
+    weight_terms(q_rows, passages, backs.at[1], w_there)
+    backs_here[...] = backs[0]
 
 
 def weight_terms(q_rows, passages, backs, out):
-    for j in range(WIDTH // PART):
-        cols = pl.ds(j * PART, PART)
+    for j in range(WIDTH // HALF):
+        cols = pl.ds(j * HALF, HALF)
         hidden = jnp.concatenate([q_rows[:, cols], passages[:, cols]], axis=0)
         out[cols, :] = matmul_tn(hidden, backs[...]).astype(out.dtype)
 
 
-def grad_side(*args, own, sib):
+def grad_side(*args):
     queries = X * ROWS
     passages = CHIP_BLOCKS * ROWS
     tile = shape((ROWS, WIDTH), BF16)
@@ -312,26 +320,22 @@
         grad_kernel, "grad_side",
         (
             shape((1, ROWS), F32),
-            pltpu.HBM((ROWS, WIDTH), F32), tile, tile, tile,
-            pltpu.HBM((ROWS, WIDTH), BF16),
-            pltpu.HBM((ROWS, 1), F32),
+            tile, tile, tile, tile,
             shape((OWN, WIDTH), F32),
             shape((OWN, WIDTH), BF16),
             shape((queries + passages, HALF), BF16),
-            shape((passages, WIDTH), BF16),
             shape((WIDTH, HALF), BF16),
         ),
-        [SMEM] + [VMEM] * 9 + [HBM] * 2,
-        (VMEM,) * 12,
+        [SMEM] + [VMEM] * 10,
+        (VMEM,) * 9,
         [
             pltpu.VMEM((passages, queries), BF16),
             pltpu.VMEM((queries, WIDTH), F32),
             pltpu.VMEM((passages, WIDTH), F32),
             pltpu.VMEM((C, queries + passages, HALF), BF16),
-            pltpu.SemaphoreType.DMA((2,)),
         ],
         GRAD, 3_000_000_000, 14_000_000,
-        *args, *in_hbm(own, sib),
+        *args,
     )
 
 
@@ -424,7 +428,7 @@
 
 def hidden_kernel(*refs):
     *terms, emb, r, weight, out = refs
-    grad = terms[0][...]
+    grad = terms[0][...].astype(F32)
     for term in terms[1:]:
         grad = grad + term[...].astype(F32)
     back = back_of(emb[...], r[...] * score_scale, grad).astype(BF16)
@@ -442,7 +446,7 @@
         VMEM,
         [],
         24, 2 * rows * WIDTH * WIDTH, 2_000_000 + rows * 10_000,
-        *in_hbm(terms[0]), *terms[1:], *in_hbm(emb, r), weight,
+        *terms, *in_hbm(emb, r), weight,
     )
 
 
@@ -459,10 +463,12 @@
     sibling = lax.ppermute(outgoing, "c", SWAP)
     emb_sib, r_sib = passage_side(sibling, weight)
 
-    q_emb, q_r, exponent, send, pos_row, p_emb, q_rows = score_side(place, tiles, weight, emb_own, emb_sib)
+    q_emb, q_r, exponent, send, pos_row, p_emb, q_rows, hidden, emb_mine, r_mine = score_side(
+        place, tiles, weight, emb_own, emb_sib, passages, sibling
+    )
     recv = exchange(send, "x")
-    losses, g0, g1, g2, g3, emb_mine, r_mine, p_grad, p_grad_sib, backs, hidden, w_there = grad_side(
-        place, recv, pos_row, exponent, q_r, r_own, r_sib, q_emb, p_emb, q_rows, own=passages, sib=sibling
+    losses, g0, g1, g2, g3, p_grad, p_grad_sib, backs, w_there = grad_side(
+        place, recv, pos_row, exponent, q_r, r_own, r_sib, q_emb, p_emb, q_rows, hidden
     )
 
     w_there = lax.ppermute(w_there, "c", SWAP)

time: 111 us -> 111 us (level)
  local copies, waits for them, and re-layouts: 0.04 us -> 1.43 us
  Pallas kernels: 29.7 us -> 28.4 us
    unnamed x16 -> x18, local copies, waits for them, and re-layouts: 0.04 us -> 1.43 us
    pallas_call x12, Pallas kernels: 29.7 us -> 28.4 us  [call(): pl.pallas_call(kernel, name=name, out_shape=out_shape, in_specs=in_specs,...]
where the time goes in v4:
time: 111 us; the launch traced here: 110 us
  starting transfers between devices  52 us (47%)
  Pallas kernels  28.4 us (26%)
  waiting for transfers between devices  18.7 us (17%)
  blocking collectives  8.49 us (8%)
  local copies, waits for them, and re-layouts  1.43 us (1%)
    pallas_call x12, Pallas kernels, call(): pl.pallas_call(kernel, name=name, out_shape=out_shape, in_specs=in_specs,...  28.4 us
    all_to_all x4, starting transfers between devices, exchange(): return lax.all_to_all(value, axis, split_axis=0, concat_axis=0, tiled=True)  28.1 us
    all_to_all x4, waiting for transfers between devices, exchange(): return lax.all_to_all(value, axis, split_axis=0, concat_axis=0, tiled=True)  13.1 us
    all_to_all x1, blocking collectives, exchange(): return lax.all_to_all(value, axis, split_axis=0, concat_axis=0, tiled=True)  8.49 us
    ppermute x1, starting transfers between devices, body(): sibling = lax.ppermute(outgoing, 'c', SWAP)  7.47 us
    ppermute x1, starting transfers between devices, body(): g2 = lax.ppermute(g2, 'x', shift(X - 2))  3.9 us
    ppermute x1, starting transfers between devices, body(): w_there = lax.ppermute(w_there, 'c', SWAP)  3.71 us
    ppermute x1, starting transfers between devices, body(): g1 = lax.ppermute(g1, 'x', shift(X - 1))  3.42 us
  transfers between devices with their start and end apart: 10, of which 6 were waited for; matrix products, arithmetic and copies ran while one was open for 0% of the time, Pallas kernels for 14%

profile of v4, /device:TPU:1, one launch (start us, length us, event | category | flops | bytes accessed | tf_op | source)
XLA Modules:
  0.0 110.0 jit_solution(15883690429609083858)
XLA Ops:
  0.6 0.0 copy-start
  0.6 2.2 %pack.1 = bf16[4,1040,128]{2,1,0:T(8,128)(2,1)} custom-call(bf16[128,1024]{1,0:T(8,128)(2,1)} %queries.1, s32[1,128]{1,0:T(1,128)} %bitcast.4, s32[1,8]{1,0:T(1,128)} %pairs.1), custom_call_target="tpu_custom_call" | custom-call | bytes 1400000 | tf_op jit(solution)/shard_map/pack/pallas_call | solution.py:72
  2.9 4.9 %all-to-all-start = ((bf16[4,1040,128]{2,1,0:T(8,128)(2,1)}), bf16[4,1040,128]{2,1,0:T(8,128)(2,1)S(1)}, u32[]{:S(2)}, u32[]{:S(2)}) async-start(bf16[4,1040,128]{2,1,0:T(8,128)(2,1)} %pack.1), calls=%async_computation | async-start | bytes 2129920 | tf_op jit(solution)/shard_map/all_to_all | solution.py:38
  7.7 0.0 copy-done
  7.7 3.2 %passage_side.2 = (bf16[384,1024]{1,0:T(8,128)(2,1)}, f32[384,1]{1,0:T(8,128)}) custom-call(bf16[384,1024]{1,0:T(8,128)(2,1)} %own, bf16[1024,1024]{1,0:T(8,128)(2,1)S(1)} %copy-done), custom_call_target="tpu_custom_call" | custom-call | flops 1000 | bytes 1000 | tf_op jit(solution)/shard_map/passage_side/pallas_call | solution.py:72
  10.9 7.5 %collective-permute-start = (bf16[384,1024]{1,0:T(8,128)(2,1)}, bf16[384,1024]{1,0:T(8,128)(2,1)}, u32[]{:S(2)}, u32[]{:S(2)}) collective-permute-start(bf16[384,1024]{1,0:T(8,128)(2,1)} %own), channel_id=1, source_target_pairs={{0,1},{1,0},{2,3},{3,2},{4,5},{5,4},{6,7},{7,6},{8,9},{9,8},{10,11... | collective-permute-start | bytes 2359304 | tf_op jit(solution)/shard_map/ppermute | solution.py:463
  18.4 0.1 pad_add_fusion.place
  18.5 2.2 %collective-permute-done.passages.sib = bf16[384,1024]{1,0:T(8,128)(2,1)} collective-permute-done((bf16[384,1024]{1,0:T(8,128)(2,1)}, bf16[384,1024]{1,0:T(8,128)(2,1)}, u32[]{:S(2)}, u32[]{:S(2)}) %collective-permute-start) | collective-permute-done | bytes 786464 | tf_op jit(solution)/shard_map/ppermute | solution.py:463
  20.6 3.2 %passage_side.3 = (bf16[384,1024]{1,0:T(8,128)(2,1)}, f32[384,1]{1,0:T(8,128)}) custom-call(bf16[384,1024]{1,0:T(8,128)(2,1)} %collective-permute-done.passages.sib, bf16[1024,1024]{1,0:T(8,128)(2,1)S(1)} %copy-done), custom_call_target="tpu_custom_call" | custom-call | flops 1000 | bytes 1000 | tf_op jit(solution)/shard_map/passage_side/pallas_call | solution.py:72
  23.8 0.0 all-to-all-done.tiles
  23.8 0.0 copy-start.3
  23.8 0.0 copy-start.8
  23.8 4.3 %score_side.1 = (bf16[512,1024]{1,0:T(8,128)(2,1)S(1)}, f32[512,1]{1,0:T(8,128)S(1)}, f32[768,512]{1,0:T(8,128)S(1)}, f32[4,8,128]{2,1,0:T(8,128)S(1)}, s32[1,51...) custom-call(s32[2]{0:T(128)S(1)} %pad_add_fusion.place, ...), custom_call_target="tpu_custom_call" | custom-call | flops 2000000000 | bytes 8000000 | tf_op jit(solution)/shard_map/score_side/pallas_call | solution.py:72
  28.0 8.5 %all_to_all.25.recv = f32[4,8,128]{2,1,0:T(8,128)S(1)} all-to-all(f32[4,8,128]{2,1,0:T(8,128)S(1)} %get-tuple-element.44), channel_id=1, replica_groups=mesh['z'=16,'y'=4,'x'=4,'c'=2] {'x'}, dimensions={0} | all-to-all | bytes 32768 | tf_op jit(solution)/shard_map/all_to_all | solution.py:38
  36.5 0.0 copy-done.3
  36.5 0.0 copy-done.8
  36.5 4.9 %grad_side.1 = (f32[1,128]{1,0:T(1,128)}, bf16[128,1024]{1,0:T(8,128)(2,1)S(1)}, bf16[128,1024]{1,0:T(8,128)(2,1)S(1)}, bf16[128,1024]{1,0:T(8,128)(2,1)S(1)}, b...) custom-call(s32[2]{0:T(128)S(1)} %pad_add_fusion.place, ...), custom_call_target="tpu_custom_call" | custom-call | flops 3000000000 | bytes 14000000 | tf_op jit(solution)/shard_map/grad_side/pallas_call | solution.py:72
  41.4 0.0 copy-start.7
  41.4 3.7 %collective-permute-start.1 = (bf16[1024,512]{1,0:T(8,128)(2,1)S(1)}, bf16[1024,512]{1,0:T(8,128)(2,1)S(1)}, u32[]{:S(2)}, u32[]{:S(2)}) collective-permute-start(bf16[1024,512]{1,0:T(8,128)(2,1)S(1)} %get-tuple-element.60), channel_id=1, source_target_pairs={{0,1},{1,0},{2,3},{3,2},{4,5},{5,4},{6,7},{7,6},{8,9},{9,8},{10,11... | collective-permute-start | bytes 3145736 | tf_op jit(solution)/shard_map/ppermute | solution.py:474
  45.2 1.6 %weight_here.1.here = f32[1024,512]{1,0:T(8,128)S(1)} custom-call(bf16[1280,512]{1,0:T(8,128)(2,1)S(1)} %get-tuple-element.59.backs, bf16[512,1024]{1,0:T(8,128)(2,1)S(1)} %get-tuple-element.52.q_rows, bf16[768,1024]{1,0:T(8,128)(2,1)S(1)} %get-tuple-element.53.passages), custom_call_target="tpu_custom_call" | custom-call | flops 1350000000 | bytes 6000000 | tf_op jit(solution)/shard_map/weight_here/pallas_call | solution.py:72
  46.7 0.0 copy-done.1
  46.7 0.0 copy-done.4
  46.7 0.0 copy-done.5
  46.7 0.0 copy-done.6
  46.8 0.0 copy-done.7
  46.8 0.7 collective-permute-done.1.there
  47.4 1.1 spread.1
  48.5 3.7 %all-to-all-start.2 = ((bf16[16,16,16,128]{3,2,1,0:T(8,128)(2,1)}), bf16[16,16,16,128]{3,2,1,0:T(8,128)(2,1)S(1)}, u32[]{:S(2)}, u32[]{:S(2)}) async-start(bf16[16,16,16,128]{3,2,1,0:T(8,128)(2,1)} %spread.1), calls=%async_computation.2 | async-start | bytes 2097152 | tf_op jit(solution)/shard_map/all_to_all | solution.py:38
  52.1 2.3 %collective-permute-start.4 = (bf16[384,1024]{1,0:T(8,128)(2,1)}, bf16[384,1024]{1,0:T(8,128)(2,1)S(1)}, u32[]{:S(2)}, u32[]{:S(2)}) collective-permute-start(bf16[384,1024]{1,0:T(8,128)(2,1)} %copy-done.4), channel_id=1, source_target_pairs={{0,1},{1,0},{2,3},{3,2},{4,5},{5,4},{6,7},{7,6},{8,9},{9,8},{10,11... | collective-permute-start | bytes 2359304 | tf_op jit(solution)/shard_map/ppermute | solution.py:477
  54.4 3.4 %collective-permute-start.2 = (bf16[128,1024]{1,0:T(8,128)(2,1)}, bf16[128,1024]{1,0:T(8,128)(2,1)}, u32[]{:S(2)}, u32[]{:S(2)}) collective-permute-start(bf16[128,1024]{1,0:T(8,128)(2,1)} %copy-done.7), channel_id=1, source_target_pairs={{6,0},{0,2},{2,4},{4,6},{7,1},{1,3},{3,5},{5,7},{14,8},{8,10},{10,... | collective-permute-start | bytes 786440 | tf_op jit(solution)/shard_map/ppermute | solution.py:479
  57.9 3.1 %collective-permute-start.3 = (bf16[128,1024]{1,0:T(8,128)(2,1)}, bf16[128,1024]{1,0:T(8,128)(2,1)}, u32[]{:S(2)}, u32[]{:S(2)}) collective-permute-start(bf16[128,1024]{1,0:T(8,128)(2,1)} %copy-done.6), channel_id=1, source_target_pairs={{2,0},{4,2},{6,4},{0,6},{3,1},{5,3},{7,5},{1,7},{10,8},{12,10},{14... | collective-permute-start | bytes 786440 | tf_op jit(solution)/shard_map/ppermute | solution.py:480
  61.0 0.0 collective-permute-done.4.refs_1_
  61.0 0.0 copy-start.2
  61.0 1.4 %copy-done.2 = f32[384,1024]{1,0:T(8,128)S(1)} copy-done((f32[384,1024]{1,0:T(8,128)S(1)}, f32[384,1024]{1,0:T(8,128)}, u32[]{:S(2)}) %copy-start.2) | copy-done | bytes 1572888
  62.4 3.3 %hidden_grad.2 = bf16[384,1024]{1,0:T(8,128)(2,1)} custom-call(f32[384,1024]{1,0:T(8,128)S(1)} %copy-done.2, bf16[384,1024]{1,0:T(8,128)(2,1)S(1)} %collective-permute-done.4.refs_1_, bf16[384,1024]{1,0:T(8,128)(2,1)} %get-tuple-element.41.emb_own.refs_2_, f32[384,1]{1,0:T(8,128)} %get-tuple-element.48.r_own.refs_3_, bf16[1024,1024]{1,0:T(8,128)(2,1)S(1)} %copy-done), custom_call_target="tpu_custom_call" | custom-call | flops 805306368 | bytes 5840000 | tf_op jit(solution)/shard_map/hidden_grad/pallas_call | solution.py:72
  65.8 3.4 %all-to-all-done.2.pieces = bf16[16,16,16,128]{3,2,1,0:T(8,128)(2,1)S(1)} async-done(((bf16[16,16,16,128]{3,2,1,0:T(8,128)(2,1)}), bf16[16,16,16,128]{3,2,1,0:T(8,128)(2,1)S(1)}, u32[]{:S(2)}, u32[]{:S(2)}) %all-to-all-start.2) | async-done | bytes 1048608 | tf_op jit(solution)/shard_map/all_to_all | solution.py:38
  69.1 0.8 sum_pieces.1
  69.9 2.8 %collective-permute-done.2.refs_1_ = bf16[128,1024]{1,0:T(8,128)(2,1)} collective-permute-done((bf16[128,1024]{1,0:T(8,128)(2,1)}, bf16[128,1024]{1,0:T(8,128)(2,1)}, u32[]{:S(2)}, u32[]{:S(2)}) %collective-permute-start.2) | collective-permute-done | bytes 262176 | tf_op jit(solution)/shard_map/ppermute | solution.py:479
  72.7 0.0 collective-permute-done.3.refs_3_
  72.7 13.8 %all-to-all-start.3 = ((bf16[16,16,128]{2,1,0:T(8,128)(2,1)}), bf16[16,16,128]{2,1,0:T(8,128)(2,1)S(1)}, u32[]{:S(2)}, u32[]{:S(2)}) async-start(bf16[16,16,128]{2,1,0:T(8,128)(2,1)} %sum_pieces.1), calls=%async_computation.3 | async-start | bytes 131072 | tf_op jit(solution)/shard_map/all_to_all | solution.py:38
  86.5 3.9 %collective-permute-start.5 = (bf16[128,1024]{1,0:T(8,128)(2,1)}, bf16[128,1024]{1,0:T(8,128)(2,1)S(1)}, u32[]{:S(2)}, u32[]{:S(2)}) collective-permute-start(bf16[128,1024]{1,0:T(8,128)(2,1)} %copy-done.5), channel_id=1, source_target_pairs={{4,0},{6,2},{0,4},{2,6},{5,1},{7,3},{1,5},{3,7},{12,8},{14,10},{8,... | collective-permute-start | bytes 786440 | tf_op jit(solution)/shard_map/ppermute | solution.py:484
  90.4 7.7 %all-to-all-done.3.pieces = bf16[16,16,128]{2,1,0:T(8,128)(2,1)S(1)} async-done(((bf16[16,16,128]{2,1,0:T(8,128)(2,1)}), bf16[16,16,128]{2,1,0:T(8,128)(2,1)S(1)}, u32[]{:S(2)}, u32[]{:S(2)}) %all-to-all-start.3) | async-done | bytes 65568 | tf_op jit(solution)/shard_map/all_to_all | solution.py:38
  98.1 0.7 last_sum.1
  98.7 5.8 %all-to-all-start.4 = ((f32[8,16,128]{2,1,0:T(8,128)}), f32[8,16,128]{2,1,0:T(8,128)S(1)}, u32[]{:S(2)}, u32[]{:S(2)}) async-start(f32[8,16,128]{2,1,0:T(8,128)} %last_sum.1), calls=%async_computation.4 | async-start | bytes 131072 | tf_op jit(solution)/shard_map/all_to_all | solution.py:38
  104.5 0.0 collective-permute-done.5.refs_2_
  104.5 2.8 %hidden_grad.3 = bf16[128,1024]{1,0:T(8,128)(2,1)} custom-call(bf16[128,1024]{1,0:T(8,128)(2,1)S(1)} %get-tuple-element.55.refs_0_, bf16[128,1024]{1,0:T(8,128)(2,1)} %collective-permute-done.2.refs_1_, bf16[128,1024]{1,0:T(8,128)(2,1)S(1)} %collective-permute-done.5.refs_2_, bf16[128,1024]{1,0:T(8,128)(2,1)} %collective-permute-done.3.refs_3_, ...), custom_call_target="tpu_custom_call" | custom-call | flops 268435456 | bytes 3280000 | tf_op jit(solution)/shard_map/hidden_grad/pallas_call | solution.py:72
  107.3 2.1 %all-to-all-done.4.pieces = f32[8,16,128]{2,1,0:T(8,128)S(1)} async-done(((f32[8,16,128]{2,1,0:T(8,128)}), f32[8,16,128]{2,1,0:T(8,128)S(1)}, u32[]{:S(2)}, u32[]{:S(2)}) %all-to-all-start.4) | async-done | bytes 65568 | tf_op jit(solution)/shard_map/all_to_all | solution.py:38
  109.3 0.6 lay.1
  (4 shorter events, 0.0 us)
Async XLA Ops:
  0.6 7.1 %copy-start = (bf16[1024,1024]{1,0:T(8,128)(2,1)S(1)}, bf16[1024,1024]{1,0:T(8,128)(2,1)}, u32[]{:S(2)}) copy-start(bf16[1024,1024]{1,0:T(8,128)(2,1)} %refs_6_) | copy-start | bytes 6291460
  2.9 20.9 %all-to-all-start = ((bf16[4,1040,128]{2,1,0:T(8,128)(2,1)}), bf16[4,1040,128]{2,1,0:T(8,128)(2,1)S(1)}, u32[]{:S(2)}, u32[]{:S(2)}) async-start(bf16[4,1040,128]{2,1,0:T(8,128)(2,1)} %pack.1), calls=%async_computation | async-start | bytes 2129920 | tf_op jit(solution)/shard_map/all_to_all | solution.py:38
  10.9 9.7 %collective-permute-start = (bf16[384,1024]{1,0:T(8,128)(2,1)}, bf16[384,1024]{1,0:T(8,128)(2,1)}, u32[]{:S(2)}, u32[]{:S(2)}) collective-permute-start(bf16[384,1024]{1,0:T(8,128)(2,1)} %own), channel_id=1, source_target_pairs={{0,1},{1,0},{2,3},{3,2},{4,5},{5,4},{6,7},{7,6},{8,9},{9,8},{10,11... | collective-permute-start | bytes 2359304 | tf_op jit(solution)/shard_map/ppermute | solution.py:463
  23.8 12.8 %copy-start.3 = (f32[384,1]{1,0:T(8,128)S(1)}, f32[384,1]{1,0:T(8,128)}, u32[]{:S(2)}) copy-start(f32[384,1]{1,0:T(8,128)} %get-tuple-element.48.r_own.refs_3_) | copy-start | bytes 4612
  23.8 12.8 %copy-start.8 = (f32[384,1]{1,0:T(8,128)S(1)}, f32[384,1]{1,0:T(8,128)}, u32[]{:S(2)}) copy-start(f32[384,1]{1,0:T(8,128)} %get-tuple-element.49.r_sib) | copy-start | bytes 4612
  41.4 5.3 %copy-start.1 = (f32[384,1024]{1,0:T(8,128)}, f32[384,1024]{1,0:T(8,128)S(1)}, u32[]{:S(2)}) copy-start(f32[384,1024]{1,0:T(8,128)S(1)} %get-tuple-element.65.refs_0_) | copy-start | bytes 4718596
  41.4 5.3 %copy-start.4 = (bf16[384,1024]{1,0:T(8,128)(2,1)}, bf16[384,1024]{1,0:T(8,128)(2,1)S(1)}, u32[]{:S(2)}) copy-start(bf16[384,1024]{1,0:T(8,128)(2,1)S(1)} %get-tuple-element.66) | copy-start | bytes 2359300
  41.4 5.3 %copy-start.5 = (bf16[128,1024]{1,0:T(8,128)(2,1)}, bf16[128,1024]{1,0:T(8,128)(2,1)S(1)}, u32[]{:S(2)}) copy-start(bf16[128,1024]{1,0:T(8,128)(2,1)S(1)} %get-tuple-element.68) | copy-start | bytes 786436
  41.4 5.3 %copy-start.6 = (bf16[128,1024]{1,0:T(8,128)(2,1)}, bf16[128,1024]{1,0:T(8,128)(2,1)S(1)}, u32[]{:S(2)}) copy-start(bf16[128,1024]{1,0:T(8,128)(2,1)S(1)} %get-tuple-element.64) | copy-start | bytes 786436
  41.4 5.3 %copy-start.7 = (bf16[128,1024]{1,0:T(8,128)(2,1)}, bf16[128,1024]{1,0:T(8,128)(2,1)S(1)}, u32[]{:S(2)}) copy-start(bf16[128,1024]{1,0:T(8,128)(2,1)S(1)} %get-tuple-element.63) | copy-start | bytes 786436
  41.4 6.0 %collective-permute-start.1 = (bf16[1024,512]{1,0:T(8,128)(2,1)S(1)}, bf16[1024,512]{1,0:T(8,128)(2,1)S(1)}, u32[]{:S(2)}, u32[]{:S(2)}) collective-permute-start(bf16[1024,512]{1,0:T(8,128)(2,1)S(1)} %get-tuple-element.60), channel_id=1, source_target_pairs={{0,1},{1,0},{2,3},{3,2},{4,5},{5,4},{6,7},{7,6},{8,9},{9,8},{10,11... | collective-permute-start | bytes 3145736 | tf_op jit(solution)/shard_map/ppermute | solution.py:474
  48.5 20.7 %all-to-all-start.2 = ((bf16[16,16,16,128]{3,2,1,0:T(8,128)(2,1)}), bf16[16,16,16,128]{3,2,1,0:T(8,128)(2,1)S(1)}, u32[]{:S(2)}, u32[]{:S(2)}) async-start(bf16[16,16,16,128]{3,2,1,0:T(8,128)(2,1)} %spread.1), calls=%async_computation.2 | async-start | bytes 2097152 | tf_op jit(solution)/shard_map/all_to_all | solution.py:38
  52.1 8.9 %collective-permute-start.4 = (bf16[384,1024]{1,0:T(8,128)(2,1)}, bf16[384,1024]{1,0:T(8,128)(2,1)S(1)}, u32[]{:S(2)}, u32[]{:S(2)}) collective-permute-start(bf16[384,1024]{1,0:T(8,128)(2,1)} %copy-done.4), channel_id=1, source_target_pairs={{0,1},{1,0},{2,3},{3,2},{4,5},{5,4},{6,7},{7,6},{8,9},{9,8},{10,11... | collective-permute-start | bytes 2359304 | tf_op jit(solution)/shard_map/ppermute | solution.py:477
  54.4 18.2 %collective-permute-start.2 = (bf16[128,1024]{1,0:T(8,128)(2,1)}, bf16[128,1024]{1,0:T(8,128)(2,1)}, u32[]{:S(2)}, u32[]{:S(2)}) collective-permute-start(bf16[128,1024]{1,0:T(8,128)(2,1)} %copy-done.7), channel_id=1, source_target_pairs={{6,0},{0,2},{2,4},{4,6},{7,1},{1,3},{3,5},{5,7},{14,8},{8,10},{10,... | collective-permute-start | bytes 786440 | tf_op jit(solution)/shard_map/ppermute | solution.py:479
  57.9 14.8 %collective-permute-start.3 = (bf16[128,1024]{1,0:T(8,128)(2,1)}, bf16[128,1024]{1,0:T(8,128)(2,1)}, u32[]{:S(2)}, u32[]{:S(2)}) collective-permute-start(bf16[128,1024]{1,0:T(8,128)(2,1)} %copy-done.6), channel_id=1, source_target_pairs={{2,0},{4,2},{6,4},{0,6},{3,1},{5,3},{7,5},{1,7},{10,8},{12,10},{14... | collective-permute-start | bytes 786440 | tf_op jit(solution)/shard_map/ppermute | solution.py:480
  61.0 1.4 %copy-start.2 = (f32[384,1024]{1,0:T(8,128)S(1)}, f32[384,1024]{1,0:T(8,128)}, u32[]{:S(2)}) copy-start(f32[384,1024]{1,0:T(8,128)} %copy-done.1) | copy-start | bytes 4718596
  72.7 25.4 %all-to-all-start.3 = ((bf16[16,16,128]{2,1,0:T(8,128)(2,1)}), bf16[16,16,128]{2,1,0:T(8,128)(2,1)S(1)}, u32[]{:S(2)}, u32[]{:S(2)}) async-start(bf16[16,16,128]{2,1,0:T(8,128)(2,1)} %sum_pieces.1), calls=%async_computation.3 | async-start | bytes 131072 | tf_op jit(solution)/shard_map/all_to_all | solution.py:38
  86.5 18.0 %collective-permute-start.5 = (bf16[128,1024]{1,0:T(8,128)(2,1)}, bf16[128,1024]{1,0:T(8,128)(2,1)S(1)}, u32[]{:S(2)}, u32[]{:S(2)}) collective-permute-start(bf16[128,1024]{1,0:T(8,128)(2,1)} %copy-done.5), channel_id=1, source_target_pairs={{4,0},{6,2},{0,4},{2,6},{5,1},{7,3},{1,5},{3,7},{12,8},{14,10},{8,... | collective-permute-start | bytes 786440 | tf_op jit(solution)/shard_map/ppermute | solution.py:484
  98.7 10.6 %all-to-all-start.4 = ((f32[8,16,128]{2,1,0:T(8,128)}), f32[8,16,128]{2,1,0:T(8,128)S(1)}, u32[]{:S(2)}, u32[]{:S(2)}) async-start(f32[8,16,128]{2,1,0:T(8,128)} %last_sum.1), calls=%async_computation.4 | async-start | bytes 131072 | tf_op jit(solution)/shard_map/all_to_all | solution.py:38

commit v5 on v4

--- a/solution.py
+++ b/solution.py
@@ -437,7 +437,7 @@
         out[:, cols] = matmul_nt(back, weight[cols, :]).astype(BF16)
 
 
-def hidden_grad(terms, emb, r, weight):
+def hidden_grad(terms, emb, r, weight, far=False):
     rows = emb.shape[0]
     return call(
         hidden_kernel, "hidden_grad",
@@ -446,7 +446,7 @@
         VMEM,
         [],
         24, 2 * rows * WIDTH * WIDTH, 2_000_000 + rows * 10_000,
-        *terms, *in_hbm(emb, r), weight,
+        *(in_hbm(terms[0]) if far else terms[:1]), *terms[1:], *in_hbm(emb, r), weight,
     )
 
 
@@ -473,17 +473,19 @@
 
     w_there = lax.ppermute(w_there, "c", SWAP)
     w = spread(weight_here(backs, q_rows, hidden), w_there)
-    (p_grad_sib, g1, g3), w = lax.optimization_barrier(((p_grad_sib, g1, g3), w))
-    p_grad_sib = lax.ppermute(p_grad_sib, "c", SWAP)
-    passage_grad = hidden_grad((p_grad, p_grad_sib), emb_own, r_own, weight)
+    (p_grad_sib, g1, g2, g3), w = lax.optimization_barrier(((p_grad_sib, g1, g2, g3), w))
+    g2 = lax.ppermute(g2, "x", shift(X - 2))
     g1 = lax.ppermute(g1, "x", shift(X - 1))
     g3 = lax.ppermute(g3, "x", shift(X - 3))
+    query_grad = hidden_grad((g0, g1, g2, g3), emb_mine, r_mine, weight)
+    p_grad_sib = lax.ppermute(p_grad_sib, "c", SWAP)
+    passage_grad = hidden_grad((p_grad, p_grad_sib), emb_own, r_own, weight, far=True)
 
     w = sum_pieces(exchange(w, ("y", "x")))
-    w, g2, g1, g3, passage_grad = lax.optimization_barrier((w, g2, g1, g3, passage_grad))
-    g2 = lax.ppermute(g2, "x", shift(X - 2))
-    query_grad = hidden_grad((g0, g1, g2, g3), emb_mine, r_mine, weight)
-    w = last_sum(exchange(w, "z"))
+    w, passage_grad = lax.optimization_barrier((w, passage_grad))
+    w = exchange(w, "z")
+    w, query_grad = lax.optimization_barrier((w, query_grad))
+    w = last_sum(w)
     weight_grad = lay(exchange(w, ("x", "c")))
     return losses.reshape(ROWS), query_grad, passage_grad, weight_grad
 

time: 111 us -> 108 us (0.973)
  blocking collectives: 8.49 us -> 19 us
  waiting for transfers between devices: 18.7 us -> 11.6 us
  starting transfers between devices: 52 us -> 46.8 us
  local copies, waits for them, and re-layouts: 1.43 us -> 0.03 us
    all_to_all x1 -> x2, blocking collectives: 8.49 us -> 19 us  [exchange(): return lax.all_to_all(value, axis, split_axis=0, concat_axis=0, tiled=True)]
    all_to_all x4 -> x3, starting transfers between devices: 28.1 us -> 22.6 us  [exchange(): return lax.all_to_all(value, axis, split_axis=0, concat_axis=0, tiled=True)]
    all_to_all x4 -> x3, waiting for transfers between devices: 13.1 us -> 8.78 us  [exchange(): return lax.all_to_all(value, axis, split_axis=0, concat_axis=0, tiled=True)]
    ppermute x1, waiting for transfers between devices: 2.76 us -> 0.01 us  [body(): g1 = lax.ppermute(g1, 'x', shift(X - 1))]
    unnamed x18 -> x16, local copies, waits for them, and re-layouts: 1.43 us -> 0.03 us
  transfers between devices with their start and end apart: 10 -> 9, of which waited for: 6 -> 4; matrix products, arithmetic and copies ran while one was open for 0% -> 0% of each run, Pallas kernels for 14% -> 14%
where the time goes in v5:
time: 108 us; the launch traced here: 107 us
  starting transfers between devices  46.8 us (43%)
  Pallas kernels  28.4 us (26%)
  blocking collectives  19 us (18%)
  waiting for transfers between devices  11.6 us (11%)
    pallas_call x12, Pallas kernels, call(): pl.pallas_call(kernel, name=name, out_shape=out_shape, in_specs=in_specs,...  28.4 us
    all_to_all x3, starting transfers between devices, exchange(): return lax.all_to_all(value, axis, split_axis=0, concat_axis=0, tiled=True)  22.6 us
    all_to_all x2, blocking collectives, exchange(): return lax.all_to_all(value, axis, split_axis=0, concat_axis=0, tiled=True)  19 us
    all_to_all x3, waiting for transfers between devices, exchange(): return lax.all_to_all(value, axis, split_axis=0, concat_axis=0, tiled=True)  8.78 us
    ppermute x1, starting transfers between devices, body(): sibling = lax.ppermute(outgoing, 'c', SWAP)  7.47 us
    ppermute x1, starting transfers between devices, body(): g2 = lax.ppermute(g2, 'x', shift(X - 2))  4.32 us
    ppermute x1, starting transfers between devices, body(): w_there = lax.ppermute(w_there, 'c', SWAP)  3.7 us
    ppermute x1, starting transfers between devices, body(): g1 = lax.ppermute(g1, 'x', shift(X - 1))  3.42 us
  transfers between devices with their start and end apart: 9, of which 4 were waited for; matrix products, arithmetic and copies ran while one was open for 0% of the time, Pallas kernels for 14%

profile of v5, /device:TPU:1, one launch (start us, length us, event | category | flops | bytes accessed | tf_op | source)
XLA Modules:
  0.0 106.8 jit_solution(3465892617897255168)
XLA Ops:
  0.6 0.0 copy-start
  0.6 2.2 %pack.1 = bf16[4,1040,128]{2,1,0:T(8,128)(2,1)} custom-call(bf16[128,1024]{1,0:T(8,128)(2,1)} %queries.1, s32[1,128]{1,0:T(1,128)} %bitcast.4, s32[1,8]{1,0:T(1,128)} %pairs.1), custom_call_target="tpu_custom_call" | custom-call | bytes 1400000 | tf_op jit(solution)/shard_map/pack/pallas_call | solution.py:72
  2.9 4.9 %all-to-all-start = ((bf16[4,1040,128]{2,1,0:T(8,128)(2,1)}), bf16[4,1040,128]{2,1,0:T(8,128)(2,1)S(1)}, u32[]{:S(2)}, u32[]{:S(2)}) async-start(bf16[4,1040,128]{2,1,0:T(8,128)(2,1)} %pack.1), calls=%async_computation | async-start | bytes 2129920 | tf_op jit(solution)/shard_map/all_to_all | solution.py:38
  7.7 0.0 copy-done
  7.7 3.2 %passage_side.2 = (bf16[384,1024]{1,0:T(8,128)(2,1)}, f32[384,1]{1,0:T(8,128)}) custom-call(bf16[384,1024]{1,0:T(8,128)(2,1)} %own, bf16[1024,1024]{1,0:T(8,128)(2,1)S(1)} %copy-done), custom_call_target="tpu_custom_call" | custom-call | flops 1000 | bytes 1000 | tf_op jit(solution)/shard_map/passage_side/pallas_call | solution.py:72
  10.9 7.5 %collective-permute-start = (bf16[384,1024]{1,0:T(8,128)(2,1)}, bf16[384,1024]{1,0:T(8,128)(2,1)}, u32[]{:S(2)}, u32[]{:S(2)}) collective-permute-start(bf16[384,1024]{1,0:T(8,128)(2,1)} %own), channel_id=1, source_target_pairs={{0,1},{1,0},{2,3},{3,2},{4,5},{5,4},{6,7},{7,6},{8,9},{9,8},{10,11... | collective-permute-start | bytes 2359304 | tf_op jit(solution)/shard_map/ppermute | solution.py:463
  18.4 0.1 pad_add_fusion.place
  18.4 2.2 %collective-permute-done.passages.sib = bf16[384,1024]{1,0:T(8,128)(2,1)} collective-permute-done((bf16[384,1024]{1,0:T(8,128)(2,1)}, bf16[384,1024]{1,0:T(8,128)(2,1)}, u32[]{:S(2)}, u32[]{:S(2)}) %collective-permute-start) | collective-permute-done | bytes 786464 | tf_op jit(solution)/shard_map/ppermute | solution.py:463
  20.6 3.2 %passage_side.3 = (bf16[384,1024]{1,0:T(8,128)(2,1)}, f32[384,1]{1,0:T(8,128)}) custom-call(bf16[384,1024]{1,0:T(8,128)(2,1)} %collective-permute-done.passages.sib, bf16[1024,1024]{1,0:T(8,128)(2,1)S(1)} %copy-done), custom_call_target="tpu_custom_call" | custom-call | flops 1000 | bytes 1000 | tf_op jit(solution)/shard_map/passage_side/pallas_call | solution.py:72
  23.8 0.0 all-to-all-done.tiles
  23.8 0.0 copy-start.2
  23.8 0.0 copy-start.7
  23.8 4.3 %score_side.1 = (bf16[512,1024]{1,0:T(8,128)(2,1)S(1)}, f32[512,1]{1,0:T(8,128)S(1)}, f32[768,512]{1,0:T(8,128)S(1)}, f32[4,8,128]{2,1,0:T(8,128)S(1)}, s32[1,51...) custom-call(s32[2]{0:T(128)S(1)} %pad_add_fusion.place, ...), custom_call_target="tpu_custom_call" | custom-call | flops 2000000000 | bytes 8000000 | tf_op jit(solution)/shard_map/score_side/pallas_call | solution.py:72
  28.0 8.5 %all_to_all.25.recv = f32[4,8,128]{2,1,0:T(8,128)S(1)} all-to-all(f32[4,8,128]{2,1,0:T(8,128)S(1)} %get-tuple-element.44), channel_id=1, replica_groups=mesh['z'=16,'y'=4,'x'=4,'c'=2] {'x'}, dimensions={0} | all-to-all | bytes 32768 | tf_op jit(solution)/shard_map/all_to_all | solution.py:38
  36.5 0.0 copy-done.2
  36.5 0.0 copy-done.7
  36.5 4.9 %grad_side.1 = (f32[1,128]{1,0:T(1,128)}, bf16[128,1024]{1,0:T(8,128)(2,1)S(1)}, bf16[128,1024]{1,0:T(8,128)(2,1)S(1)}, bf16[128,1024]{1,0:T(8,128)(2,1)S(1)}, b...) custom-call(s32[2]{0:T(128)S(1)} %pad_add_fusion.place, ...), custom_call_target="tpu_custom_call" | custom-call | flops 3000000000 | bytes 14000000 | tf_op jit(solution)/shard_map/grad_side/pallas_call | solution.py:72
  41.4 0.0 copy-start.1
  41.4 0.0 copy-start.3
  41.4 0.0 copy-start.4
  41.4 0.0 copy-start.5
  41.4 0.0 copy-start.6
  41.4 3.7 %collective-permute-start.1 = (bf16[1024,512]{1,0:T(8,128)(2,1)S(1)}, bf16[1024,512]{1,0:T(8,128)(2,1)S(1)}, u32[]{:S(2)}, u32[]{:S(2)}) collective-permute-start(bf16[1024,512]{1,0:T(8,128)(2,1)S(1)} %get-tuple-element.60), channel_id=1, source_target_pairs={{0,1},{1,0},{2,3},{3,2},{4,5},{5,4},{6,7},{7,6},{8,9},{9,8},{10,11... | collective-permute-start | bytes 3145736 | tf_op jit(solution)/shard_map/ppermute | solution.py:474
  45.1 1.6 %weight_here.1.here = f32[1024,512]{1,0:T(8,128)S(1)} custom-call(bf16[1280,512]{1,0:T(8,128)(2,1)S(1)} %get-tuple-element.59.backs, bf16[512,1024]{1,0:T(8,128)(2,1)S(1)} %get-tuple-element.52.q_rows, bf16[768,1024]{1,0:T(8,128)(2,1)S(1)} %get-tuple-element.53.passages), custom_call_target="tpu_custom_call" | custom-call | flops 1350000000 | bytes 6000000 | tf_op jit(solution)/shard_map/weight_here/pallas_call | solution.py:72
  46.7 0.0 copy-done.1
  46.7 0.0 copy-done.3
  46.7 0.0 copy-done.4
  46.7 0.0 copy-done.5
  46.7 0.0 copy-done.6
  46.7 0.7 collective-permute-done.1.there
  47.4 1.0 spread.1
  48.4 3.7 %all-to-all-start.2 = ((bf16[16,16,16,128]{3,2,1,0:T(8,128)(2,1)}), bf16[16,16,16,128]{3,2,1,0:T(8,128)(2,1)S(1)}, u32[]{:S(2)}, u32[]{:S(2)}) async-start(bf16[16,16,16,128]{3,2,1,0:T(8,128)(2,1)} %spread.1), calls=%async_computation.2 | async-start | bytes 2097152 | tf_op jit(solution)/shard_map/all_to_all | solution.py:38
  52.1 2.3 %collective-permute-start.2 = (bf16[384,1024]{1,0:T(8,128)(2,1)}, bf16[384,1024]{1,0:T(8,128)(2,1)S(1)}, u32[]{:S(2)}, u32[]{:S(2)}) collective-permute-start(bf16[384,1024]{1,0:T(8,128)(2,1)} %copy-done.3), channel_id=1, source_target_pairs={{0,1},{1,0},{2,3},{3,2},{4,5},{5,4},{6,7},{7,6},{8,9},{9,8},{10,11... | collective-permute-start | bytes 2359304 | tf_op jit(solution)/shard_map/ppermute | solution.py:481
  54.4 3.4 %collective-permute-start.3 = (bf16[128,1024]{1,0:T(8,128)(2,1)}, bf16[128,1024]{1,0:T(8,128)(2,1)}, u32[]{:S(2)}, u32[]{:S(2)}) collective-permute-start(bf16[128,1024]{1,0:T(8,128)(2,1)} %copy-done.6), channel_id=1, source_target_pairs={{6,0},{0,2},{2,4},{4,6},{7,1},{1,3},{3,5},{5,7},{14,8},{8,10},{10,... | collective-permute-start | bytes 786440 | tf_op jit(solution)/shard_map/ppermute | solution.py:478
  57.8 4.3 %collective-permute-start.4 = (bf16[128,1024]{1,0:T(8,128)(2,1)}, bf16[128,1024]{1,0:T(8,128)(2,1)}, u32[]{:S(2)}, u32[]{:S(2)}) collective-permute-start(bf16[128,1024]{1,0:T(8,128)(2,1)} %copy-done.5), channel_id=1, source_target_pairs={{4,0},{6,2},{0,4},{2,6},{5,1},{7,3},{1,5},{3,7},{12,8},{14,10},{8,... | collective-permute-start | bytes 786440 | tf_op jit(solution)/shard_map/ppermute | solution.py:477
  62.2 3.1 %collective-permute-start.5 = (bf16[128,1024]{1,0:T(8,128)(2,1)}, bf16[128,1024]{1,0:T(8,128)(2,1)}, u32[]{:S(2)}, u32[]{:S(2)}) collective-permute-start(bf16[128,1024]{1,0:T(8,128)(2,1)} %copy-done.4), channel_id=1, source_target_pairs={{2,0},{4,2},{6,4},{0,6},{3,1},{5,3},{7,5},{1,7},{10,8},{12,10},{14... | collective-permute-start | bytes 786440 | tf_op jit(solution)/shard_map/ppermute | solution.py:479
  65.3 0.0 collective-permute-done.2.refs_1_
  65.3 3.8 %hidden_grad.2 = bf16[384,1024]{1,0:T(8,128)(2,1)} custom-call(f32[384,1024]{1,0:T(8,128)} %copy-done.1, bf16[384,1024]{1,0:T(8,128)(2,1)S(1)} %collective-permute-done.2.refs_1_, bf16[384,1024]{1,0:T(8,128)(2,1)} %get-tuple-element.41.emb_own.refs_2_, f32[384,1]{1,0:T(8,128)} %get-tuple-element.48.r_own.refs_3_, bf16[1024,1024]{1,0:T(8,128)(2,1)S(1)} %copy-done), custom_call_target="tpu_custom_call" | custom-call | flops 805306368 | bytes 5840000 | tf_op jit(solution)/shard_map/hidden_grad/pallas_call | solution.py:72
  69.1 0.1 all-to-all-done.2.pieces
  69.2 0.8 sum_pieces.1
  69.9 14.0 %all-to-all-start.3 = ((bf16[16,16,128]{2,1,0:T(8,128)(2,1)}), bf16[16,16,128]{2,1,0:T(8,128)(2,1)S(1)}, u32[]{:S(2)}, u32[]{:S(2)}) async-start(bf16[16,16,128]{2,1,0:T(8,128)(2,1)} %sum_pieces.1), calls=%async_computation.3 | async-start | bytes 131072 | tf_op jit(solution)/shard_map/all_to_all | solution.py:38
  84.0 0.0 collective-permute-done.3.refs_1_
  84.0 0.0 collective-permute-done.4.refs_2_
  84.0 0.0 collective-permute-done.5.refs_3_
  84.0 2.9 %hidden_grad.3 = bf16[128,1024]{1,0:T(8,128)(2,1)} custom-call(bf16[128,1024]{1,0:T(8,128)(2,1)S(1)} %get-tuple-element.65.refs_0_, bf16[128,1024]{1,0:T(8,128)(2,1)} %collective-permute-done.3.refs_1_, bf16[128,1024]{1,0:T(8,128)(2,1)} %collective-permute-done.4.refs_2_, bf16[128,1024]{1,0:T(8,128)(2,1)} %collective-permute-done.5.refs_3_, ...), custom_call_target="tpu_custom_call" | custom-call | flops 268435456 | bytes 3280000 | tf_op jit(solution)/shard_map/hidden_grad/pallas_call | solution.py:72
  86.9 8.7 %all-to-all-done.3.pieces = bf16[16,16,128]{2,1,0:T(8,128)(2,1)S(1)} async-done(((bf16[16,16,128]{2,1,0:T(8,128)(2,1)}), bf16[16,16,128]{2,1,0:T(8,128)(2,1)S(1)}, u32[]{:S(2)}, u32[]{:S(2)}) %all-to-all-start.3) | async-done | bytes 65568 | tf_op jit(solution)/shard_map/all_to_all | solution.py:38
  95.6 10.6 %all_to_all.26.pieces = f32[8,16,128]{2,1,0:T(8,128)S(1)} all-to-all(f32[8,16,128]{2,1,0:T(8,128)S(1)} %last_sum.1), channel_id=1, replica_groups=mesh['z'=16,'y'=4,'x'=4,'c'=2] {'x','c'}, dimensions={0} | all-to-all | bytes 131072 | tf_op jit(solution)/shard_map/all_to_all | solution.py:38
  106.1 0.6 lay.1
  (1 shorter events, 0.0 us)
Async XLA Ops:
  0.6 7.1 %copy-start = (bf16[1024,1024]{1,0:T(8,128)(2,1)S(1)}, bf16[1024,1024]{1,0:T(8,128)(2,1)}, u32[]{:S(2)}) copy-start(bf16[1024,1024]{1,0:T(8,128)(2,1)} %refs_6_) | copy-start | bytes 6291460
  2.9 20.9 %all-to-all-start = ((bf16[4,1040,128]{2,1,0:T(8,128)(2,1)}), bf16[4,1040,128]{2,1,0:T(8,128)(2,1)S(1)}, u32[]{:S(2)}, u32[]{:S(2)}) async-start(bf16[4,1040,128]{2,1,0:T(8,128)(2,1)} %pack.1), calls=%async_computation | async-start | bytes 2129920 | tf_op jit(solution)/shard_map/all_to_all | solution.py:38
  10.9 9.7 %collective-permute-start = (bf16[384,1024]{1,0:T(8,128)(2,1)}, bf16[384,1024]{1,0:T(8,128)(2,1)}, u32[]{:S(2)}, u32[]{:S(2)}) collective-permute-start(bf16[384,1024]{1,0:T(8,128)(2,1)} %own), channel_id=1, source_target_pairs={{0,1},{1,0},{2,3},{3,2},{4,5},{5,4},{6,7},{7,6},{8,9},{9,8},{10,11... | collective-permute-start | bytes 2359304 | tf_op jit(solution)/shard_map/ppermute | solution.py:463
  23.8 12.8 %copy-start.2 = (f32[384,1]{1,0:T(8,128)S(1)}, f32[384,1]{1,0:T(8,128)}, u32[]{:S(2)}) copy-start(f32[384,1]{1,0:T(8,128)} %get-tuple-element.48.r_own.refs_3_) | copy-start | bytes 4612
  23.8 12.8 %copy-start.7 = (f32[384,1]{1,0:T(8,128)S(1)}, f32[384,1]{1,0:T(8,128)}, u32[]{:S(2)}) copy-start(f32[384,1]{1,0:T(8,128)} %get-tuple-element.49.r_sib) | copy-start | bytes 4612
  41.4 5.3 %copy-start.1 = (f32[384,1024]{1,0:T(8,128)}, f32[384,1024]{1,0:T(8,128)S(1)}, u32[]{:S(2)}) copy-start(f32[384,1024]{1,0:T(8,128)S(1)} %get-tuple-element.62.refs_0_) | copy-start | bytes 4718596
  41.4 5.3 %copy-start.3 = (bf16[384,1024]{1,0:T(8,128)(2,1)}, bf16[384,1024]{1,0:T(8,128)(2,1)S(1)}, u32[]{:S(2)}) copy-start(bf16[384,1024]{1,0:T(8,128)(2,1)S(1)} %get-tuple-element.63) | copy-start | bytes 2359300
  41.4 5.3 %copy-start.4 = (bf16[128,1024]{1,0:T(8,128)(2,1)}, bf16[128,1024]{1,0:T(8,128)(2,1)S(1)}, u32[]{:S(2)}) copy-start(bf16[128,1024]{1,0:T(8,128)(2,1)S(1)} %get-tuple-element.68) | copy-start | bytes 786436
  41.4 5.3 %copy-start.5 = (bf16[128,1024]{1,0:T(8,128)(2,1)}, bf16[128,1024]{1,0:T(8,128)(2,1)S(1)}, u32[]{:S(2)}) copy-start(bf16[128,1024]{1,0:T(8,128)(2,1)S(1)} %get-tuple-element.67) | copy-start | bytes 786436
  41.4 5.3 %copy-start.6 = (bf16[128,1024]{1,0:T(8,128)(2,1)}, bf16[128,1024]{1,0:T(8,128)(2,1)S(1)}, u32[]{:S(2)}) copy-start(bf16[128,1024]{1,0:T(8,128)(2,1)S(1)} %get-tuple-element.66) | copy-start | bytes 786436
  41.4 6.0 %collective-permute-start.1 = (bf16[1024,512]{1,0:T(8,128)(2,1)S(1)}, bf16[1024,512]{1,0:T(8,128)(2,1)S(1)}, u32[]{:S(2)}, u32[]{:S(2)}) collective-permute-start(bf16[1024,512]{1,0:T(8,128)(2,1)S(1)} %get-tuple-element.60), channel_id=1, source_target_pairs={{0,1},{1,0},{2,3},{3,2},{4,5},{5,4},{6,7},{7,6},{8,9},{9,8},{10,11... | collective-permute-start | bytes 3145736 | tf_op jit(solution)/shard_map/ppermute | solution.py:474
  48.4 20.7 %all-to-all-start.2 = ((bf16[16,16,16,128]{3,2,1,0:T(8,128)(2,1)}), bf16[16,16,16,128]{3,2,1,0:T(8,128)(2,1)S(1)}, u32[]{:S(2)}, u32[]{:S(2)}) async-start(bf16[16,16,16,128]{3,2,1,0:T(8,128)(2,1)} %spread.1), calls=%async_computation.2 | async-start | bytes 2097152 | tf_op jit(solution)/shard_map/all_to_all | solution.py:38
  52.1 13.1 %collective-permute-start.2 = (bf16[384,1024]{1,0:T(8,128)(2,1)}, bf16[384,1024]{1,0:T(8,128)(2,1)S(1)}, u32[]{:S(2)}, u32[]{:S(2)}) collective-permute-start(bf16[384,1024]{1,0:T(8,128)(2,1)} %copy-done.3), channel_id=1, source_target_pairs={{0,1},{1,0},{2,3},{3,2},{4,5},{5,4},{6,7},{7,6},{8,9},{9,8},{10,11... | collective-permute-start | bytes 2359304 | tf_op jit(solution)/shard_map/ppermute | solution.py:481
  54.4 29.6 %collective-permute-start.3 = (bf16[128,1024]{1,0:T(8,128)(2,1)}, bf16[128,1024]{1,0:T(8,128)(2,1)}, u32[]{:S(2)}, u32[]{:S(2)}) collective-permute-start(bf16[128,1024]{1,0:T(8,128)(2,1)} %copy-done.6), channel_id=1, source_target_pairs={{6,0},{0,2},{2,4},{4,6},{7,1},{1,3},{3,5},{5,7},{14,8},{8,10},{10,... | collective-permute-start | bytes 786440 | tf_op jit(solution)/shard_map/ppermute | solution.py:478
  57.8 26.1 %collective-permute-start.4 = (bf16[128,1024]{1,0:T(8,128)(2,1)}, bf16[128,1024]{1,0:T(8,128)(2,1)}, u32[]{:S(2)}, u32[]{:S(2)}) collective-permute-start(bf16[128,1024]{1,0:T(8,128)(2,1)} %copy-done.5), channel_id=1, source_target_pairs={{4,0},{6,2},{0,4},{2,6},{5,1},{7,3},{1,5},{3,7},{12,8},{14,10},{8,... | collective-permute-start | bytes 786440 | tf_op jit(solution)/shard_map/ppermute | solution.py:477
  62.2 21.8 %collective-permute-start.5 = (bf16[128,1024]{1,0:T(8,128)(2,1)}, bf16[128,1024]{1,0:T(8,128)(2,1)}, u32[]{:S(2)}, u32[]{:S(2)}) collective-permute-start(bf16[128,1024]{1,0:T(8,128)(2,1)} %copy-done.4), channel_id=1, source_target_pairs={{2,0},{4,2},{6,4},{0,6},{3,1},{5,3},{7,5},{1,7},{10,8},{12,10},{14... | collective-permute-start | bytes 786440 | tf_op jit(solution)/shard_map/ppermute | solution.py:479
  69.9 25.6 %all-to-all-start.3 = ((bf16[16,16,128]{2,1,0:T(8,128)(2,1)}), bf16[16,16,128]{2,1,0:T(8,128)(2,1)S(1)}, u32[]{:S(2)}, u32[]{:S(2)}) async-start(bf16[16,16,128]{2,1,0:T(8,128)(2,1)} %sum_pieces.1), calls=%async_computation.3 | async-start | bytes 131072 | tf_op jit(solution)/shard_map/all_to_all | solution.py:38

commit v6 on v5

--- a/solution.py
+++ b/solution.py
@@ -172,7 +172,7 @@
         pltpu.make_async_copy(own, passages.at[pl.ds(0, OWN)], sems.at[2]),
         pltpu.make_async_copy(sib, passages.at[pl.ds(OWN, OWN)], sems.at[3]),
     ]
-    for copy in copies + late:
+    for copy in copies:
         copy.start()
     lines = [tiles[k, PIECES * ROWS : LINES, :].astype(F32) for k in range(X)]
     pos_name, pos_rest, names = [
@@ -201,7 +201,7 @@
         pltpu.make_async_copy(q_emb.at[mine], emb_mine, sems.at[4]),
         pltpu.make_async_copy(q_r.at[mine], r_mine, sems.at[5]),
     ]
-    for copy in kept:
+    for copy in late + kept:
         copy.start()
     line = lax.broadcasted_iota(jnp.int32, (ROWS, X * ROWS), 0)
     total = jnp.zeros((1, X * ROWS), F32)
@@ -298,7 +298,7 @@
         first = b < BLOCKS
         near = pl.ds((b % BLOCKS) * ROWS, ROWS)
         grad = p_grad[rows, :]
-        (p_grad_own if first else p_grad_sib)[near, :] = grad.astype(F32 if first else BF16)
+        (p_grad_own if first else p_grad_sib)[near, :] = grad.astype(BF16)
         r = (r_own if first else r_sib)[near, :]
         keep(pl.ds(queries + b * ROWS, ROWS), p_emb[rows, :], r, grad)
     weight_terms(q_rows, passages, backs.at[1], w_there)
@@ -321,7 +321,7 @@
         (
             shape((1, ROWS), F32),
             tile, tile, tile, tile,
-            shape((OWN, WIDTH), F32),
+            shape((OWN, WIDTH), BF16),
             shape((OWN, WIDTH), BF16),
             shape((queries + passages, HALF), BF16),
             shape((WIDTH, HALF), BF16),
@@ -360,14 +360,15 @@
     lanes = HALF // X
     copies = []
     for y in range(Y):
-        for z in range(Z):
-            rows = pl.ds((z * Y + y) * own_rows, own_rows)
-            value = (here[rows, :] + there[rows, :].astype(F32)).astype(BF16)
-            for x in range(X):
-                held[y * X + x, z] = value[:, x * lanes : (x + 1) * lanes]
-        part = pl.ds(y * X, X)
-        copies.append(pltpu.make_async_copy(held.at[part], out.at[part], sems.at[y]))
-        copies[-1].start()
+        for h in range(2):
+            for z in range(h * Z // 2, (h + 1) * Z // 2):
+                rows = pl.ds((z * Y + y) * own_rows, own_rows)
+                value = (here[rows, :] + there[rows, :].astype(F32)).astype(BF16)
+                for x in range(X):
+                    held[y * X + x, z] = value[:, x * lanes : (x + 1) * lanes]
+            part = (pl.ds(y * X, X), pl.ds(h * Z // 2, Z // 2))
+            copies.append(pltpu.make_async_copy(held.at[part], out.at[part], sems.at[2 * y + h]))
+            copies[-1].start()
     for copy in copies:
         copy.wait()
 
@@ -379,7 +380,7 @@
         pltpu.HBM(dims, BF16),
         [VMEM, VMEM],
         HBM,
-        [pltpu.VMEM(dims, BF16), pltpu.SemaphoreType.DMA((Y,))],
+        [pltpu.VMEM(dims, BF16), pltpu.SemaphoreType.DMA((2 * Y,))],
         16, 500_000, 4_000_000,
         here, there,
     )

time: 108 us -> 108 us (level)
  no operation moved by 1% of the time
where the time goes in v6:
time: 108 us
  starting transfers between devices  46.6 us (43%)
  Pallas kernels  28.9 us (27%)
  blocking collectives  19.3 us (18%)
  waiting for transfers between devices  11.8 us (11%)
    pallas_call x12, Pallas kernels, call(): pl.pallas_call(kernel, name=name, out_shape=out_shape, in_specs=in_specs,...  28.9 us
    all_to_all x3, starting transfers between devices, exchange(): return lax.all_to_all(value, axis, split_axis=0, concat_axis=0, tiled=True)  22.3 us
    all_to_all x2, blocking collectives, exchange(): return lax.all_to_all(value, axis, split_axis=0, concat_axis=0, tiled=True)  19.3 us
    all_to_all x3, waiting for transfers between devices, exchange(): return lax.all_to_all(value, axis, split_axis=0, concat_axis=0, tiled=True)  8.99 us
    ppermute x1, starting transfers between devices, body(): sibling = lax.ppermute(outgoing, 'c', SWAP)  7.47 us
    ppermute x1, starting transfers between devices, body(): g2 = lax.ppermute(g2, 'x', shift(X - 2))  4.32 us
    ppermute x1, starting transfers between devices, body(): w_there = lax.ppermute(w_there, 'c', SWAP)  3.71 us
    ppermute x1, starting transfers between devices, body(): g1 = lax.ppermute(g1, 'x', shift(X - 1))  3.42 us
  transfers between devices with their start and end apart: 9, of which 4 were waited for; matrix products, arithmetic and copies ran while one was open for 0% of the time, Pallas kernels for 14%

profile of v6, /device:TPU:1, one launch (start us, length us, event | category | flops | bytes accessed | tf_op | source)
XLA Modules:
  0.0 107.6 jit_solution(4346285981042061369)
XLA Ops:
  0.6 0.0 copy-start
  0.6 2.2 %pack.1 = bf16[4,1040,128]{2,1,0:T(8,128)(2,1)} custom-call(bf16[128,1024]{1,0:T(8,128)(2,1)} %queries.1, s32[1,128]{1,0:T(1,128)} %bitcast.4, s32[1,8]{1,0:T(1,128)} %pairs.1), custom_call_target="tpu_custom_call" | custom-call | bytes 1400000 | tf_op jit(solution)/shard_map/pack/pallas_call | solution.py:72
  2.8 4.9 %all-to-all-start = ((bf16[4,1040,128]{2,1,0:T(8,128)(2,1)}), bf16[4,1040,128]{2,1,0:T(8,128)(2,1)S(1)}, u32[]{:S(2)}, u32[]{:S(2)}) async-start(bf16[4,1040,128]{2,1,0:T(8,128)(2,1)} %pack.1), calls=%async_computation | async-start | bytes 2129920 | tf_op jit(solution)/shard_map/all_to_all | solution.py:38
  7.7 0.0 copy-done
  7.7 3.2 %passage_side.2 = (bf16[384,1024]{1,0:T(8,128)(2,1)}, f32[384,1]{1,0:T(8,128)}) custom-call(bf16[384,1024]{1,0:T(8,128)(2,1)} %own, bf16[1024,1024]{1,0:T(8,128)(2,1)S(1)} %copy-done), custom_call_target="tpu_custom_call" | custom-call | flops 1000 | bytes 1000 | tf_op jit(solution)/shard_map/passage_side/pallas_call | solution.py:72
  10.8 7.5 %collective-permute-start = (bf16[384,1024]{1,0:T(8,128)(2,1)}, bf16[384,1024]{1,0:T(8,128)(2,1)}, u32[]{:S(2)}, u32[]{:S(2)}) collective-permute-start(bf16[384,1024]{1,0:T(8,128)(2,1)} %own), channel_id=1, source_target_pairs={{0,1},{1,0},{2,3},{3,2},{4,5},{5,4},{6,7},{7,6},{8,9},{9,8},{10,11... | collective-permute-start | bytes 2359304 | tf_op jit(solution)/shard_map/ppermute | solution.py:464
  18.3 0.1 pad_add_fusion.place
  18.4 2.2 %collective-permute-done.passages.sib = bf16[384,1024]{1,0:T(8,128)(2,1)} collective-permute-done((bf16[384,1024]{1,0:T(8,128)(2,1)}, bf16[384,1024]{1,0:T(8,128)(2,1)}, u32[]{:S(2)}, u32[]{:S(2)}) %collective-permute-start) | collective-permute-done | bytes 786464 | tf_op jit(solution)/shard_map/ppermute | solution.py:464
  20.6 3.2 %passage_side.3 = (bf16[384,1024]{1,0:T(8,128)(2,1)}, f32[384,1]{1,0:T(8,128)}) custom-call(bf16[384,1024]{1,0:T(8,128)(2,1)} %collective-permute-done.passages.sib, bf16[1024,1024]{1,0:T(8,128)(2,1)S(1)} %copy-done), custom_call_target="tpu_custom_call" | custom-call | flops 1000 | bytes 1000 | tf_op jit(solution)/shard_map/passage_side/pallas_call | solution.py:72
  23.7 0.0 all-to-all-done.tiles
  23.7 0.0 copy-start.2
  23.7 0.0 copy-start.7
  23.7 5.0 %score_side.1 = (bf16[512,1024]{1,0:T(8,128)(2,1)S(1)}, f32[512,1]{1,0:T(8,128)S(1)}, f32[768,512]{1,0:T(8,128)S(1)}, f32[4,8,128]{2,1,0:T(8,128)S(1)}, s32[1,51...) custom-call(s32[2]{0:T(128)S(1)} %pad_add_fusion.place, ...), custom_call_target="tpu_custom_call" | custom-call | flops 2000000000 | bytes 8000000 | tf_op jit(solution)/shard_map/score_side/pallas_call | solution.py:72
  28.7 8.5 %all_to_all.25.recv = f32[4,8,128]{2,1,0:T(8,128)S(1)} all-to-all(f32[4,8,128]{2,1,0:T(8,128)S(1)} %get-tuple-element.44), channel_id=1, replica_groups=mesh['z'=16,'y'=4,'x'=4,'c'=2] {'x'}, dimensions={0} | all-to-all | bytes 32768 | tf_op jit(solution)/shard_map/all_to_all | solution.py:38
  37.2 0.0 copy-done.2
  37.2 0.0 copy-done.7
  37.2 4.9 %grad_side.1 = (f32[1,128]{1,0:T(1,128)}, bf16[128,1024]{1,0:T(8,128)(2,1)S(1)}, bf16[128,1024]{1,0:T(8,128)(2,1)S(1)}, bf16[128,1024]{1,0:T(8,128)(2,1)S(1)}, b...) custom-call(s32[2]{0:T(128)S(1)} %pad_add_fusion.place, ...), custom_call_target="tpu_custom_call" | custom-call | flops 3000000000 | bytes 14000000 | tf_op jit(solution)/shard_map/grad_side/pallas_call | solution.py:72
  42.1 0.0 copy-start.1
  42.1 0.0 copy-start.3
  42.1 0.0 copy-start.4
  42.1 0.0 copy-start.5
  42.1 0.0 copy-start.6
  42.2 3.7 %collective-permute-start.1 = (bf16[1024,512]{1,0:T(8,128)(2,1)S(1)}, bf16[1024,512]{1,0:T(8,128)(2,1)S(1)}, u32[]{:S(2)}, u32[]{:S(2)}) collective-permute-start(bf16[1024,512]{1,0:T(8,128)(2,1)S(1)} %get-tuple-element.60), channel_id=1, source_target_pairs={{0,1},{1,0},{2,3},{3,2},{4,5},{5,4},{6,7},{7,6},{8,9},{9,8},{10,11... | collective-permute-start | bytes 3145736 | tf_op jit(solution)/shard_map/ppermute | solution.py:475
  45.9 1.6 %weight_here.1.here = f32[1024,512]{1,0:T(8,128)S(1)} custom-call(bf16[1280,512]{1,0:T(8,128)(2,1)S(1)} %get-tuple-element.59.backs, bf16[512,1024]{1,0:T(8,128)(2,1)S(1)} %get-tuple-element.52.q_rows, bf16[768,1024]{1,0:T(8,128)(2,1)S(1)} %get-tuple-element.53.passages), custom_call_target="tpu_custom_call" | custom-call | flops 1350000000 | bytes 6000000 | tf_op jit(solution)/shard_map/weight_here/pallas_call | solution.py:72
  47.4 0.0 copy-done.1
  47.4 0.0 copy-done.3
  47.4 0.0 copy-done.4
  47.5 0.0 copy-done.5
  47.5 0.0 copy-done.6
  47.5 0.7 collective-permute-done.1.there
  48.1 1.1 spread.1
  49.2 3.7 %all-to-all-start.2 = ((bf16[16,16,16,128]{3,2,1,0:T(8,128)(2,1)}), bf16[16,16,16,128]{3,2,1,0:T(8,128)(2,1)S(1)}, u32[]{:S(2)}, u32[]{:S(2)}) async-start(bf16[16,16,16,128]{3,2,1,0:T(8,128)(2,1)} %spread.1), calls=%async_computation.2 | async-start | bytes 2097152 | tf_op jit(solution)/shard_map/all_to_all | solution.py:38
  52.9 2.3 %collective-permute-start.2 = (bf16[384,1024]{1,0:T(8,128)(2,1)}, bf16[384,1024]{1,0:T(8,128)(2,1)S(1)}, u32[]{:S(2)}, u32[]{:S(2)}) collective-permute-start(bf16[384,1024]{1,0:T(8,128)(2,1)} %copy-done.3), channel_id=1, source_target_pairs={{0,1},{1,0},{2,3},{3,2},{4,5},{5,4},{6,7},{7,6},{8,9},{9,8},{10,11... | collective-permute-start | bytes 2359304 | tf_op jit(solution)/shard_map/ppermute | solution.py:482
  55.2 3.4 %collective-permute-start.3 = (bf16[128,1024]{1,0:T(8,128)(2,1)}, bf16[128,1024]{1,0:T(8,128)(2,1)}, u32[]{:S(2)}, u32[]{:S(2)}) collective-permute-start(bf16[128,1024]{1,0:T(8,128)(2,1)} %copy-done.6), channel_id=1, source_target_pairs={{6,0},{0,2},{2,4},{4,6},{7,1},{1,3},{3,5},{5,7},{14,8},{8,10},{10,... | collective-permute-start | bytes 786440 | tf_op jit(solution)/shard_map/ppermute | solution.py:479
  58.6 4.3 %collective-permute-start.4 = (bf16[128,1024]{1,0:T(8,128)(2,1)}, bf16[128,1024]{1,0:T(8,128)(2,1)}, u32[]{:S(2)}, u32[]{:S(2)}) collective-permute-start(bf16[128,1024]{1,0:T(8,128)(2,1)} %copy-done.5), channel_id=1, source_target_pairs={{4,0},{6,2},{0,4},{2,6},{5,1},{7,3},{1,5},{3,7},{12,8},{14,10},{8,... | collective-permute-start | bytes 786440 | tf_op jit(solution)/shard_map/ppermute | solution.py:478
  62.9 3.1 %collective-permute-start.5 = (bf16[128,1024]{1,0:T(8,128)(2,1)}, bf16[128,1024]{1,0:T(8,128)(2,1)}, u32[]{:S(2)}, u32[]{:S(2)}) collective-permute-start(bf16[128,1024]{1,0:T(8,128)(2,1)} %copy-done.4), channel_id=1, source_target_pairs={{2,0},{4,2},{6,4},{0,6},{3,1},{5,3},{7,5},{1,7},{10,8},{12,10},{14... | collective-permute-start | bytes 786440 | tf_op jit(solution)/shard_map/ppermute | solution.py:480
  66.0 0.0 collective-permute-done.2.refs_1_
  66.0 3.6 %hidden_grad.2 = bf16[384,1024]{1,0:T(8,128)(2,1)} custom-call(bf16[384,1024]{1,0:T(8,128)(2,1)} %copy-done.1, bf16[384,1024]{1,0:T(8,128)(2,1)S(1)} %collective-permute-done.2.refs_1_, bf16[384,1024]{1,0:T(8,128)(2,1)} %get-tuple-element.41.emb_own.refs_2_, f32[384,1]{1,0:T(8,128)} %get-tuple-element.48.r_own.refs_3_, bf16[1024,1024]{1,0:T(8,128)(2,1)S(1)} %copy-done), custom_call_target="tpu_custom_call" | custom-call | flops 805306368 | bytes 5840000 | tf_op jit(solution)/shard_map/hidden_grad/pallas_call | solution.py:72
  69.6 0.3 all-to-all-done.2.pieces
  69.9 0.8 sum_pieces.1
  70.7 13.8 %all-to-all-start.3 = ((bf16[16,16,128]{2,1,0:T(8,128)(2,1)}), bf16[16,16,128]{2,1,0:T(8,128)(2,1)S(1)}, u32[]{:S(2)}, u32[]{:S(2)}) async-start(bf16[16,16,128]{2,1,0:T(8,128)(2,1)} %sum_pieces.1), calls=%async_computation.3 | async-start | bytes 131072 | tf_op jit(solution)/shard_map/all_to_all | solution.py:38
  84.5 0.0 collective-permute-done.3.refs_1_
  84.5 0.0 collective-permute-done.4.refs_2_
  84.5 0.0 collective-permute-done.5.refs_3_
  84.5 2.9 %hidden_grad.3 = bf16[128,1024]{1,0:T(8,128)(2,1)} custom-call(bf16[128,1024]{1,0:T(8,128)(2,1)S(1)} %get-tuple-element.65.refs_0_, bf16[128,1024]{1,0:T(8,128)(2,1)} %collective-permute-done.3.refs_1_, bf16[128,1024]{1,0:T(8,128)(2,1)} %collective-permute-done.4.refs_2_, bf16[128,1024]{1,0:T(8,128)(2,1)} %collective-permute-done.5.refs_3_, ...), custom_call_target="tpu_custom_call" | custom-call | flops 268435456 | bytes 3280000 | tf_op jit(solution)/shard_map/hidden_grad/pallas_call | solution.py:72
  87.4 8.7 %all-to-all-done.3.pieces = bf16[16,16,128]{2,1,0:T(8,128)(2,1)S(1)} async-done(((bf16[16,16,128]{2,1,0:T(8,128)(2,1)}), bf16[16,16,128]{2,1,0:T(8,128)(2,1)S(1)}, u32[]{:S(2)}, u32[]{:S(2)}) %all-to-all-start.3) | async-done | bytes 65568 | tf_op jit(solution)/shard_map/all_to_all | solution.py:38
  96.1 10.8 %all_to_all.26.pieces = f32[8,16,128]{2,1,0:T(8,128)S(1)} all-to-all(f32[8,16,128]{2,1,0:T(8,128)S(1)} %last_sum.1), channel_id=1, replica_groups=mesh['z'=16,'y'=4,'x'=4,'c'=2] {'x','c'}, dimensions={0} | all-to-all | bytes 131072 | tf_op jit(solution)/shard_map/all_to_all | solution.py:38
  106.9 0.6 lay.1
  (1 shorter events, 0.0 us)
Async XLA Ops:
  0.6 7.0 %copy-start = (bf16[1024,1024]{1,0:T(8,128)(2,1)S(1)}, bf16[1024,1024]{1,0:T(8,128)(2,1)}, u32[]{:S(2)}) copy-start(bf16[1024,1024]{1,0:T(8,128)(2,1)} %refs_6_) | copy-start | bytes 6291460
  2.8 20.9 %all-to-all-start = ((bf16[4,1040,128]{2,1,0:T(8,128)(2,1)}), bf16[4,1040,128]{2,1,0:T(8,128)(2,1)S(1)}, u32[]{:S(2)}, u32[]{:S(2)}) async-start(bf16[4,1040,128]{2,1,0:T(8,128)(2,1)} %pack.1), calls=%async_computation | async-start | bytes 2129920 | tf_op jit(solution)/shard_map/all_to_all | solution.py:38
  10.8 9.7 %collective-permute-start = (bf16[384,1024]{1,0:T(8,128)(2,1)}, bf16[384,1024]{1,0:T(8,128)(2,1)}, u32[]{:S(2)}, u32[]{:S(2)}) collective-permute-start(bf16[384,1024]{1,0:T(8,128)(2,1)} %own), channel_id=1, source_target_pairs={{0,1},{1,0},{2,3},{3,2},{4,5},{5,4},{6,7},{7,6},{8,9},{9,8},{10,11... | collective-permute-start | bytes 2359304 | tf_op jit(solution)/shard_map/ppermute | solution.py:464
  23.7 13.5 %copy-start.2 = (f32[384,1]{1,0:T(8,128)S(1)}, f32[384,1]{1,0:T(8,128)}, u32[]{:S(2)}) copy-start(f32[384,1]{1,0:T(8,128)} %get-tuple-element.48.r_own.refs_3_) | copy-start | bytes 4612
  23.7 13.5 %copy-start.7 = (f32[384,1]{1,0:T(8,128)S(1)}, f32[384,1]{1,0:T(8,128)}, u32[]{:S(2)}) copy-start(f32[384,1]{1,0:T(8,128)} %get-tuple-element.49.r_sib) | copy-start | bytes 4612
  42.1 5.3 %copy-start.1 = (bf16[384,1024]{1,0:T(8,128)(2,1)}, bf16[384,1024]{1,0:T(8,128)(2,1)S(1)}, u32[]{:S(2)}) copy-start(bf16[384,1024]{1,0:T(8,128)(2,1)S(1)} %get-tuple-element.62.refs_0_) | copy-start | bytes 2359300
  42.1 5.3 %copy-start.3 = (bf16[384,1024]{1,0:T(8,128)(2,1)}, bf16[384,1024]{1,0:T(8,128)(2,1)S(1)}, u32[]{:S(2)}) copy-start(bf16[384,1024]{1,0:T(8,128)(2,1)S(1)} %get-tuple-element.63) | copy-start | bytes 2359300
  42.1 5.3 %copy-start.4 = (bf16[128,1024]{1,0:T(8,128)(2,1)}, bf16[128,1024]{1,0:T(8,128)(2,1)S(1)}, u32[]{:S(2)}) copy-start(bf16[128,1024]{1,0:T(8,128)(2,1)S(1)} %get-tuple-element.68) | copy-start | bytes 786436
  42.1 5.3 %copy-start.5 = (bf16[128,1024]{1,0:T(8,128)(2,1)}, bf16[128,1024]{1,0:T(8,128)(2,1)S(1)}, u32[]{:S(2)}) copy-start(bf16[128,1024]{1,0:T(8,128)(2,1)S(1)} %get-tuple-element.67) | copy-start | bytes 786436
  42.1 5.3 %copy-start.6 = (bf16[128,1024]{1,0:T(8,128)(2,1)}, bf16[128,1024]{1,0:T(8,128)(2,1)S(1)}, u32[]{:S(2)}) copy-start(bf16[128,1024]{1,0:T(8,128)(2,1)S(1)} %get-tuple-element.66) | copy-start | bytes 786436
  42.2 6.0 %collective-permute-start.1 = (bf16[1024,512]{1,0:T(8,128)(2,1)S(1)}, bf16[1024,512]{1,0:T(8,128)(2,1)S(1)}, u32[]{:S(2)}, u32[]{:S(2)}) collective-permute-start(bf16[1024,512]{1,0:T(8,128)(2,1)S(1)} %get-tuple-element.60), channel_id=1, source_target_pairs={{0,1},{1,0},{2,3},{3,2},{4,5},{5,4},{6,7},{7,6},{8,9},{9,8},{10,11... | collective-permute-start | bytes 3145736 | tf_op jit(solution)/shard_map/ppermute | solution.py:475
  49.2 20.7 %all-to-all-start.2 = ((bf16[16,16,16,128]{3,2,1,0:T(8,128)(2,1)}), bf16[16,16,16,128]{3,2,1,0:T(8,128)(2,1)S(1)}, u32[]{:S(2)}, u32[]{:S(2)}) async-start(bf16[16,16,16,128]{3,2,1,0:T(8,128)(2,1)} %spread.1), calls=%async_computation.2 | async-start | bytes 2097152 | tf_op jit(solution)/shard_map/all_to_all | solution.py:38
  52.9 13.1 %collective-permute-start.2 = (bf16[384,1024]{1,0:T(8,128)(2,1)}, bf16[384,1024]{1,0:T(8,128)(2,1)S(1)}, u32[]{:S(2)}, u32[]{:S(2)}) collective-permute-start(bf16[384,1024]{1,0:T(8,128)(2,1)} %copy-done.3), channel_id=1, source_target_pairs={{0,1},{1,0},{2,3},{3,2},{4,5},{5,4},{6,7},{7,6},{8,9},{9,8},{10,11... | collective-permute-start | bytes 2359304 | tf_op jit(solution)/shard_map/ppermute | solution.py:482
  55.2 29.3 %collective-permute-start.3 = (bf16[128,1024]{1,0:T(8,128)(2,1)}, bf16[128,1024]{1,0:T(8,128)(2,1)}, u32[]{:S(2)}, u32[]{:S(2)}) collective-permute-start(bf16[128,1024]{1,0:T(8,128)(2,1)} %copy-done.6), channel_id=1, source_target_pairs={{6,0},{0,2},{2,4},{4,6},{7,1},{1,3},{3,5},{5,7},{14,8},{8,10},{10,... | collective-permute-start | bytes 786440 | tf_op jit(solution)/shard_map/ppermute | solution.py:479
  58.6 25.9 %collective-permute-start.4 = (bf16[128,1024]{1,0:T(8,128)(2,1)}, bf16[128,1024]{1,0:T(8,128)(2,1)}, u32[]{:S(2)}, u32[]{:S(2)}) collective-permute-start(bf16[128,1024]{1,0:T(8,128)(2,1)} %copy-done.5), channel_id=1, source_target_pairs={{4,0},{6,2},{0,4},{2,6},{5,1},{7,3},{1,5},{3,7},{12,8},{14,10},{8,... | collective-permute-start | bytes 786440 | tf_op jit(solution)/shard_map/ppermute | solution.py:478
  62.9 21.6 %collective-permute-start.5 = (bf16[128,1024]{1,0:T(8,128)(2,1)}, bf16[128,1024]{1,0:T(8,128)(2,1)}, u32[]{:S(2)}, u32[]{:S(2)}) collective-permute-start(bf16[128,1024]{1,0:T(8,128)(2,1)} %copy-done.4), channel_id=1, source_target_pairs={{2,0},{4,2},{6,4},{0,6},{3,1},{5,3},{7,5},{1,7},{10,8},{12,10},{14... | collective-permute-start | bytes 786440 | tf_op jit(solution)/shard_map/ppermute | solution.py:480
  70.7 25.4 %all-to-all-start.3 = ((bf16[16,16,128]{2,1,0:T(8,128)(2,1)}), bf16[16,16,128]{2,1,0:T(8,128)(2,1)S(1)}, u32[]{:S(2)}, u32[]{:S(2)}) async-start(bf16[16,16,128]{2,1,0:T(8,128)(2,1)} %sum_pieces.1), calls=%async_computation.3 | async-start | bytes 131072 | tf_op jit(solution)/shard_map/all_to_all | solution.py:38

commit v7 on v6

--- a/solution.py
+++ b/solution.py
@@ -172,7 +172,7 @@
         pltpu.make_async_copy(own, passages.at[pl.ds(0, OWN)], sems.at[2]),
         pltpu.make_async_copy(sib, passages.at[pl.ds(OWN, OWN)], sems.at[3]),
     ]
-    for copy in copies:
+    for copy in copies + late:
         copy.start()
     lines = [tiles[k, PIECES * ROWS : LINES, :].astype(F32) for k in range(X)]
     pos_name, pos_rest, names = [
@@ -201,7 +201,7 @@
         pltpu.make_async_copy(q_emb.at[mine], emb_mine, sems.at[4]),
         pltpu.make_async_copy(q_r.at[mine], r_mine, sems.at[5]),
     ]
-    for copy in late + kept:
+    for copy in kept:
         copy.start()
     line = lax.broadcasted_iota(jnp.int32, (ROWS, X * ROWS), 0)
     total = jnp.zeros((1, X * ROWS), F32)
@@ -440,15 +440,19 @@
 
 def hidden_grad(terms, emb, r, weight, far=False):
     rows = emb.shape[0]
-    return call(
-        hidden_kernel, "hidden_grad",
-        shape((rows, WIDTH), BF16),
-        [VMEM] * (len(terms) + 3),
-        VMEM,
-        [],
-        24, 2 * rows * WIDTH * WIDTH, 2_000_000 + rows * 10_000,
-        *(in_hbm(terms[0]) if far else terms[:1]), *terms[1:], *in_hbm(emb, r), weight,
-    )
+    block = pl.BlockSpec((ROWS, WIDTH), lambda i: (i, 0))
+    return pl.pallas_call(
+        hidden_kernel,
+        name="hidden_grad",
+        grid=(rows // ROWS,),
+        out_shape=shape((rows, WIDTH), BF16),
+        in_specs=[block] * (len(terms) + 1) + [pl.BlockSpec((ROWS, 1), lambda i: (i, 0)), VMEM],
+        out_specs=block,
+        compiler_params=params(24),
+        cost_estimate=pl.CostEstimate(
+            flops=2 * rows * WIDTH * WIDTH, bytes_accessed=2_000_000 + rows * 10_000, transcendentals=0
+        ),
+    )(*(in_hbm(terms[0]) if far else terms[:1]), *terms[1:], *in_hbm(emb, r), weight)
 
 
 def body(queries, passages, weight, pairs, positive):

time: 108 us -> 107 us (level)
  blocking collectives: 19.3 us -> 18 us
    pallas_call x0 -> x2, Pallas kernels: none -> 7.6 us  [hidden_grad(): pl.pallas_call(hidden_kernel, name='hidden_grad', grid=(rows // ROWS,), o...]
    pallas_call x12 -> x10, Pallas kernels: 28.9 us -> 21.7 us  [call(): pl.pallas_call(kernel, name=name, out_shape=out_shape, in_specs=in_specs,...]
    all_to_all x2, blocking collectives: 19.3 us -> 18 us  [exchange(): return lax.all_to_all(value, axis, split_axis=0, concat_axis=0, tiled=True)]
  transfers between devices with their start and end apart: 9 -> 9, of which waited for: 4 -> 3; matrix products, arithmetic and copies ran while one was open for 0% -> 0% of each run, Pallas kernels for 14% -> 15%
where the time goes in v7:
time: 107 us
  starting transfers between devices  46.9 us (44%)
  Pallas kernels  29.3 us (27%)
  blocking collectives  18 us (17%)
  waiting for transfers between devices  11.5 us (11%)
    all_to_all x3, starting transfers between devices, exchange(): return lax.all_to_all(value, axis, split_axis=0, concat_axis=0, tiled=True)  22.7 us
    pallas_call x10, Pallas kernels, call(): pl.pallas_call(kernel, name=name, out_shape=out_shape, in_specs=in_specs,...  21.7 us
    all_to_all x2, blocking collectives, exchange(): return lax.all_to_all(value, axis, split_axis=0, concat_axis=0, tiled=True)  18 us
    all_to_all x3, waiting for transfers between devices, exchange(): return lax.all_to_all(value, axis, split_axis=0, concat_axis=0, tiled=True)  8.69 us
    pallas_call x2, Pallas kernels, hidden_grad(): pl.pallas_call(hidden_kernel, name='hidden_grad', grid=(rows // ROWS,), o...  7.6 us
    ppermute x1, starting transfers between devices, body(): sibling = lax.ppermute(outgoing, 'c', SWAP)  7.47 us
    ppermute x1, starting transfers between devices, body(): g2 = lax.ppermute(g2, 'x', shift(X - 2))  4.32 us
    ppermute x1, starting transfers between devices, body(): w_there = lax.ppermute(w_there, 'c', SWAP)  3.71 us
  transfers between devices with their start and end apart: 9, of which 3 were waited for; matrix products, arithmetic and copies ran while one was open for 0% of the time, Pallas kernels for 15%

profile of v7, /device:TPU:1, one launch (start us, length us, event | category | flops | bytes accessed | tf_op | source)
XLA Modules:
  0.0 106.7 jit_solution(15793161307609250011)
XLA Ops:
  0.6 0.0 copy-start
  0.6 2.2 %pack.1 = bf16[4,1040,128]{2,1,0:T(8,128)(2,1)} custom-call(bf16[128,1024]{1,0:T(8,128)(2,1)} %queries.1, s32[1,128]{1,0:T(1,128)} %bitcast.4, s32[1,8]{1,0:T(1,128)} %pairs.1), custom_call_target="tpu_custom_call" | custom-call | bytes 1400000 | tf_op jit(solution)/shard_map/pack/pallas_call | solution.py:72
  2.8 4.9 %all-to-all-start = ((bf16[4,1040,128]{2,1,0:T(8,128)(2,1)}), bf16[4,1040,128]{2,1,0:T(8,128)(2,1)S(1)}, u32[]{:S(2)}, u32[]{:S(2)}) async-start(bf16[4,1040,128]{2,1,0:T(8,128)(2,1)} %pack.1), calls=%async_computation | async-start | bytes 2129920 | tf_op jit(solution)/shard_map/all_to_all | solution.py:38
  7.7 0.0 copy-done
  7.7 3.2 %passage_side.2 = (bf16[384,1024]{1,0:T(8,128)(2,1)}, f32[384,1]{1,0:T(8,128)}) custom-call(bf16[384,1024]{1,0:T(8,128)(2,1)} %own, bf16[1024,1024]{1,0:T(8,128)(2,1)S(1)} %copy-done), custom_call_target="tpu_custom_call" | custom-call | flops 1000 | bytes 1000 | tf_op jit(solution)/shard_map/passage_side/pallas_call | solution.py:72
  10.8 7.5 %collective-permute-start = (bf16[384,1024]{1,0:T(8,128)(2,1)}, bf16[384,1024]{1,0:T(8,128)(2,1)}, u32[]{:S(2)}, u32[]{:S(2)}) collective-permute-start(bf16[384,1024]{1,0:T(8,128)(2,1)} %own), channel_id=1, source_target_pairs={{0,1},{1,0},{2,3},{3,2},{4,5},{5,4},{6,7},{7,6},{8,9},{9,8},{10,11... | collective-permute-start | bytes 2359304 | tf_op jit(solution)/shard_map/ppermute | solution.py:468
  18.3 0.1 pad_add_fusion.place
  18.4 2.2 %collective-permute-done.passages.sib = bf16[384,1024]{1,0:T(8,128)(2,1)} collective-permute-done((bf16[384,1024]{1,0:T(8,128)(2,1)}, bf16[384,1024]{1,0:T(8,128)(2,1)}, u32[]{:S(2)}, u32[]{:S(2)}) %collective-permute-start) | collective-permute-done | bytes 786464 | tf_op jit(solution)/shard_map/ppermute | solution.py:468
  20.6 3.2 %passage_side.3 = (bf16[384,1024]{1,0:T(8,128)(2,1)}, f32[384,1]{1,0:T(8,128)}) custom-call(bf16[384,1024]{1,0:T(8,128)(2,1)} %collective-permute-done.passages.sib, bf16[1024,1024]{1,0:T(8,128)(2,1)S(1)} %copy-done), custom_call_target="tpu_custom_call" | custom-call | flops 1000 | bytes 1000 | tf_op jit(solution)/shard_map/passage_side/pallas_call | solution.py:72
  23.7 0.0 all-to-all-done.tiles
  23.7 0.0 copy-start.2
  23.7 0.0 copy-start.7
  23.7 4.3 %score_side.1 = (bf16[512,1024]{1,0:T(8,128)(2,1)S(1)}, f32[512,1]{1,0:T(8,128)S(1)}, f32[768,512]{1,0:T(8,128)S(1)}, f32[4,8,128]{2,1,0:T(8,128)S(1)}, s32[1,51...) custom-call(s32[2]{0:T(128)S(1)} %pad_add_fusion.place, ...), custom_call_target="tpu_custom_call" | custom-call | flops 2000000000 | bytes 8000000 | tf_op jit(solution)/shard_map/score_side/pallas_call | solution.py:72
  28.0 8.5 %all_to_all.25.recv = f32[4,8,128]{2,1,0:T(8,128)S(1)} all-to-all(f32[4,8,128]{2,1,0:T(8,128)S(1)} %get-tuple-element.44), channel_id=1, replica_groups=mesh['z'=16,'y'=4,'x'=4,'c'=2] {'x'}, dimensions={0} | all-to-all | bytes 32768 | tf_op jit(solution)/shard_map/all_to_all | solution.py:38
  36.5 0.0 copy-done.2
  36.5 0.0 copy-done.7
  36.5 4.9 %grad_side.1 = (f32[1,128]{1,0:T(1,128)}, bf16[128,1024]{1,0:T(8,128)(2,1)S(1)}, bf16[128,1024]{1,0:T(8,128)(2,1)S(1)}, bf16[128,1024]{1,0:T(8,128)(2,1)S(1)}, b...) custom-call(s32[2]{0:T(128)S(1)} %pad_add_fusion.place, ...), custom_call_target="tpu_custom_call" | custom-call | flops 3000000000 | bytes 14000000 | tf_op jit(solution)/shard_map/grad_side/pallas_call | solution.py:72
  41.4 0.0 copy-start.1
  41.4 0.0 copy-start.3
  41.4 0.0 copy-start.4
  41.4 0.0 copy-start.5
  41.4 0.0 copy-start.6
  41.4 3.7 %collective-permute-start.1 = (bf16[1024,512]{1,0:T(8,128)(2,1)S(1)}, bf16[1024,512]{1,0:T(8,128)(2,1)S(1)}, u32[]{:S(2)}, u32[]{:S(2)}) collective-permute-start(bf16[1024,512]{1,0:T(8,128)(2,1)S(1)} %get-tuple-element.60), channel_id=1, source_target_pairs={{0,1},{1,0},{2,3},{3,2},{4,5},{5,4},{6,7},{7,6},{8,9},{9,8},{10,11... | collective-permute-start | bytes 3145736 | tf_op jit(solution)/shard_map/ppermute | solution.py:479
  45.1 1.6 %weight_here.1.here = f32[1024,512]{1,0:T(8,128)S(1)} custom-call(bf16[1280,512]{1,0:T(8,128)(2,1)S(1)} %get-tuple-element.59.backs, bf16[512,1024]{1,0:T(8,128)(2,1)S(1)} %get-tuple-element.52.q_rows, bf16[768,1024]{1,0:T(8,128)(2,1)S(1)} %get-tuple-element.53.passages), custom_call_target="tpu_custom_call" | custom-call | flops 1350000000 | bytes 6000000 | tf_op jit(solution)/shard_map/weight_here/pallas_call | solution.py:72
  46.7 0.0 copy-done.1
  46.7 0.0 copy-done.3
  46.7 0.0 copy-done.4
  46.7 0.0 copy-done.5
  46.7 0.0 copy-done.6
  46.7 0.7 collective-permute-done.1.there
  47.4 1.1 spread.1
  48.5 3.7 %all-to-all-start.2 = ((bf16[16,16,16,128]{3,2,1,0:T(8,128)(2,1)}), bf16[16,16,16,128]{3,2,1,0:T(8,128)(2,1)S(1)}, u32[]{:S(2)}, u32[]{:S(2)}) async-start(bf16[16,16,16,128]{3,2,1,0:T(8,128)(2,1)} %spread.1), calls=%async_computation.2 | async-start | bytes 2097152 | tf_op jit(solution)/shard_map/all_to_all | solution.py:38
  52.1 2.3 %collective-permute-start.2 = (bf16[384,1024]{1,0:T(8,128)(2,1)}, bf16[384,1024]{1,0:T(8,128)(2,1)S(1)}, u32[]{:S(2)}, u32[]{:S(2)}) collective-permute-start(bf16[384,1024]{1,0:T(8,128)(2,1)} %copy-done.3), channel_id=1, source_target_pairs={{0,1},{1,0},{2,3},{3,2},{4,5},{5,4},{6,7},{7,6},{8,9},{9,8},{10,11... | collective-permute-start | bytes 2359304 | tf_op jit(solution)/shard_map/ppermute | solution.py:486
  54.4 3.4 %collective-permute-start.3 = (bf16[128,1024]{1,0:T(8,128)(2,1)}, bf16[128,1024]{1,0:T(8,128)(2,1)}, u32[]{:S(2)}, u32[]{:S(2)}) collective-permute-start(bf16[128,1024]{1,0:T(8,128)(2,1)} %copy-done.6), channel_id=1, source_target_pairs={{6,0},{0,2},{2,4},{4,6},{7,1},{1,3},{3,5},{5,7},{14,8},{8,10},{10,... | collective-permute-start | bytes 786440 | tf_op jit(solution)/shard_map/ppermute | solution.py:483
  57.9 4.3 %collective-permute-start.4 = (bf16[128,1024]{1,0:T(8,128)(2,1)}, bf16[128,1024]{1,0:T(8,128)(2,1)}, u32[]{:S(2)}, u32[]{:S(2)}) collective-permute-start(bf16[128,1024]{1,0:T(8,128)(2,1)} %copy-done.5), channel_id=1, source_target_pairs={{4,0},{6,2},{0,4},{2,6},{5,1},{7,3},{1,5},{3,7},{12,8},{14,10},{8,... | collective-permute-start | bytes 786440 | tf_op jit(solution)/shard_map/ppermute | solution.py:482
  62.2 3.1 %collective-permute-start.5 = (bf16[128,1024]{1,0:T(8,128)(2,1)}, bf16[128,1024]{1,0:T(8,128)(2,1)}, u32[]{:S(2)}, u32[]{:S(2)}) collective-permute-start(bf16[128,1024]{1,0:T(8,128)(2,1)} %copy-done.4), channel_id=1, source_target_pairs={{2,0},{4,2},{6,4},{0,6},{3,1},{5,3},{7,5},{1,7},{10,8},{12,10},{14... | collective-permute-start | bytes 786440 | tf_op jit(solution)/shard_map/ppermute | solution.py:484
  65.3 0.0 collective-permute-done.2.refs_1_
  65.3 4.7 %hidden_grad.2 = bf16[384,1024]{1,0:T(8,128)(2,1)} custom-call(bf16[384,1024]{1,0:T(8,128)(2,1)} %copy-done.1, bf16[384,1024]{1,0:T(8,128)(2,1)S(1)} %collective-permute-done.2.refs_1_, bf16[384,1024]{1,0:T(8,128)(2,1)} %get-tuple-element.41.emb_own.refs_2_, f32[384,1]{1,0:T(8,128)} %get-tuple-element.48.r_own.refs_3_, bf16[1024,1024]{1,0:T(8,128)(2,1)S(1)} %copy-done), custom_call_target="tpu_custom_call" | custom-call | flops 805306368 | bytes 5840000 | tf_op jit(solution)/shard_map/hidden_grad/pallas_call | solution.py:444
  70.0 0.0 all-to-all-done.2.pieces
  70.0 0.8 sum_pieces.1
  70.8 14.1 %all-to-all-start.3 = ((bf16[16,16,128]{2,1,0:T(8,128)(2,1)}), bf16[16,16,128]{2,1,0:T(8,128)(2,1)S(1)}, u32[]{:S(2)}, u32[]{:S(2)}) async-start(bf16[16,16,128]{2,1,0:T(8,128)(2,1)} %sum_pieces.1), calls=%async_computation.3 | async-start | bytes 131072 | tf_op jit(solution)/shard_map/all_to_all | solution.py:38
  84.9 0.0 collective-permute-done.3.refs_1_
  84.9 0.0 collective-permute-done.4.refs_2_
  84.9 0.0 collective-permute-done.5.refs_3_
  85.0 2.9 %hidden_grad.3 = bf16[128,1024]{1,0:T(8,128)(2,1)} custom-call(bf16[128,1024]{1,0:T(8,128)(2,1)S(1)} %get-tuple-element.65.refs_0_, bf16[128,1024]{1,0:T(8,128)(2,1)} %collective-permute-done.3.refs_1_, bf16[128,1024]{1,0:T(8,128)(2,1)} %collective-permute-done.4.refs_2_, bf16[128,1024]{1,0:T(8,128)(2,1)} %collective-permute-done.5.refs_3_, ...), custom_call_target="tpu_custom_call" | custom-call | flops 268435456 | bytes 3280000 | tf_op jit(solution)/shard_map/hidden_grad/pallas_call | solution.py:444
  87.8 8.7 %all-to-all-done.3.pieces = bf16[16,16,128]{2,1,0:T(8,128)(2,1)S(1)} async-done(((bf16[16,16,128]{2,1,0:T(8,128)(2,1)}), bf16[16,16,128]{2,1,0:T(8,128)(2,1)S(1)}, u32[]{:S(2)}, u32[]{:S(2)}) %all-to-all-start.3) | async-done | bytes 65568 | tf_op jit(solution)/shard_map/all_to_all | solution.py:38
  96.5 9.6 %all_to_all.26.pieces = f32[8,16,128]{2,1,0:T(8,128)S(1)} all-to-all(f32[8,16,128]{2,1,0:T(8,128)S(1)} %last_sum.1), channel_id=1, replica_groups=mesh['z'=16,'y'=4,'x'=4,'c'=2] {'x','c'}, dimensions={0} | all-to-all | bytes 131072 | tf_op jit(solution)/shard_map/all_to_all | solution.py:38
  106.1 0.6 lay.1
  (1 shorter events, 0.0 us)
Async XLA Ops:
  0.6 7.0 %copy-start = (bf16[1024,1024]{1,0:T(8,128)(2,1)S(1)}, bf16[1024,1024]{1,0:T(8,128)(2,1)}, u32[]{:S(2)}) copy-start(bf16[1024,1024]{1,0:T(8,128)(2,1)} %refs_6_) | copy-start | bytes 6291460
  2.8 20.9 %all-to-all-start = ((bf16[4,1040,128]{2,1,0:T(8,128)(2,1)}), bf16[4,1040,128]{2,1,0:T(8,128)(2,1)S(1)}, u32[]{:S(2)}, u32[]{:S(2)}) async-start(bf16[4,1040,128]{2,1,0:T(8,128)(2,1)} %pack.1), calls=%async_computation | async-start | bytes 2129920 | tf_op jit(solution)/shard_map/all_to_all | solution.py:38
  10.8 9.7 %collective-permute-start = (bf16[384,1024]{1,0:T(8,128)(2,1)}, bf16[384,1024]{1,0:T(8,128)(2,1)}, u32[]{:S(2)}, u32[]{:S(2)}) collective-permute-start(bf16[384,1024]{1,0:T(8,128)(2,1)} %own), channel_id=1, source_target_pairs={{0,1},{1,0},{2,3},{3,2},{4,5},{5,4},{6,7},{7,6},{8,9},{9,8},{10,11... | collective-permute-start | bytes 2359304 | tf_op jit(solution)/shard_map/ppermute | solution.py:468
  23.7 12.8 %copy-start.2 = (f32[384,1]{1,0:T(8,128)S(1)}, f32[384,1]{1,0:T(8,128)}, u32[]{:S(2)}) copy-start(f32[384,1]{1,0:T(8,128)} %get-tuple-element.48.r_own.refs_3_) | copy-start | bytes 4612
  23.7 12.8 %copy-start.7 = (f32[384,1]{1,0:T(8,128)S(1)}, f32[384,1]{1,0:T(8,128)}, u32[]{:S(2)}) copy-start(f32[384,1]{1,0:T(8,128)} %get-tuple-element.49.r_sib) | copy-start | bytes 4612
  41.4 5.3 %copy-start.1 = (bf16[384,1024]{1,0:T(8,128)(2,1)}, bf16[384,1024]{1,0:T(8,128)(2,1)S(1)}, u32[]{:S(2)}) copy-start(bf16[384,1024]{1,0:T(8,128)(2,1)S(1)} %get-tuple-element.62.refs_0_) | copy-start | bytes 2359300
  41.4 5.3 %copy-start.3 = (bf16[384,1024]{1,0:T(8,128)(2,1)}, bf16[384,1024]{1,0:T(8,128)(2,1)S(1)}, u32[]{:S(2)}) copy-start(bf16[384,1024]{1,0:T(8,128)(2,1)S(1)} %get-tuple-element.63) | copy-start | bytes 2359300
  41.4 5.3 %copy-start.4 = (bf16[128,1024]{1,0:T(8,128)(2,1)}, bf16[128,1024]{1,0:T(8,128)(2,1)S(1)}, u32[]{:S(2)}) copy-start(bf16[128,1024]{1,0:T(8,128)(2,1)S(1)} %get-tuple-element.68) | copy-start | bytes 786436
  41.4 5.3 %copy-start.5 = (bf16[128,1024]{1,0:T(8,128)(2,1)}, bf16[128,1024]{1,0:T(8,128)(2,1)S(1)}, u32[]{:S(2)}) copy-start(bf16[128,1024]{1,0:T(8,128)(2,1)S(1)} %get-tuple-element.67) | copy-start | bytes 786436
  41.4 5.3 %copy-start.6 = (bf16[128,1024]{1,0:T(8,128)(2,1)}, bf16[128,1024]{1,0:T(8,128)(2,1)S(1)}, u32[]{:S(2)}) copy-start(bf16[128,1024]{1,0:T(8,128)(2,1)S(1)} %get-tuple-element.66) | copy-start | bytes 786436
  41.4 6.0 %collective-permute-start.1 = (bf16[1024,512]{1,0:T(8,128)(2,1)S(1)}, bf16[1024,512]{1,0:T(8,128)(2,1)S(1)}, u32[]{:S(2)}, u32[]{:S(2)}) collective-permute-start(bf16[1024,512]{1,0:T(8,128)(2,1)S(1)} %get-tuple-element.60), channel_id=1, source_target_pairs={{0,1},{1,0},{2,3},{3,2},{4,5},{5,4},{6,7},{7,6},{8,9},{9,8},{10,11... | collective-permute-start | bytes 3145736 | tf_op jit(solution)/shard_map/ppermute | solution.py:479
  48.5 21.6 %all-to-all-start.2 = ((bf16[16,16,16,128]{3,2,1,0:T(8,128)(2,1)}), bf16[16,16,16,128]{3,2,1,0:T(8,128)(2,1)S(1)}, u32[]{:S(2)}, u32[]{:S(2)}) async-start(bf16[16,16,16,128]{3,2,1,0:T(8,128)(2,1)} %spread.1), calls=%async_computation.2 | async-start | bytes 2097152 | tf_op jit(solution)/shard_map/all_to_all | solution.py:38
  52.1 13.1 %collective-permute-start.2 = (bf16[384,1024]{1,0:T(8,128)(2,1)}, bf16[384,1024]{1,0:T(8,128)(2,1)S(1)}, u32[]{:S(2)}, u32[]{:S(2)}) collective-permute-start(bf16[384,1024]{1,0:T(8,128)(2,1)} %copy-done.3), channel_id=1, source_target_pairs={{0,1},{1,0},{2,3},{3,2},{4,5},{5,4},{6,7},{7,6},{8,9},{9,8},{10,11... | collective-permute-start | bytes 2359304 | tf_op jit(solution)/shard_map/ppermute | solution.py:486
  54.4 30.5 %collective-permute-start.3 = (bf16[128,1024]{1,0:T(8,128)(2,1)}, bf16[128,1024]{1,0:T(8,128)(2,1)}, u32[]{:S(2)}, u32[]{:S(2)}) collective-permute-start(bf16[128,1024]{1,0:T(8,128)(2,1)} %copy-done.6), channel_id=1, source_target_pairs={{6,0},{0,2},{2,4},{4,6},{7,1},{1,3},{3,5},{5,7},{14,8},{8,10},{10,... | collective-permute-start | bytes 786440 | tf_op jit(solution)/shard_map/ppermute | solution.py:483
  57.9 27.1 %collective-permute-start.4 = (bf16[128,1024]{1,0:T(8,128)(2,1)}, bf16[128,1024]{1,0:T(8,128)(2,1)}, u32[]{:S(2)}, u32[]{:S(2)}) collective-permute-start(bf16[128,1024]{1,0:T(8,128)(2,1)} %copy-done.5), channel_id=1, source_target_pairs={{4,0},{6,2},{0,4},{2,6},{5,1},{7,3},{1,5},{3,7},{12,8},{14,10},{8,... | collective-permute-start | bytes 786440 | tf_op jit(solution)/shard_map/ppermute | solution.py:482
  62.2 22.8 %collective-permute-start.5 = (bf16[128,1024]{1,0:T(8,128)(2,1)}, bf16[128,1024]{1,0:T(8,128)(2,1)}, u32[]{:S(2)}, u32[]{:S(2)}) collective-permute-start(bf16[128,1024]{1,0:T(8,128)(2,1)} %copy-done.4), channel_id=1, source_target_pairs={{2,0},{4,2},{6,4},{0,6},{3,1},{5,3},{7,5},{1,7},{10,8},{12,10},{14... | collective-permute-start | bytes 786440 | tf_op jit(solution)/shard_map/ppermute | solution.py:484
  70.8 25.7 %all-to-all-start.3 = ((bf16[16,16,128]{2,1,0:T(8,128)(2,1)}), bf16[16,16,128]{2,1,0:T(8,128)(2,1)S(1)}, u32[]{:S(2)}, u32[]{:S(2)}) async-start(bf16[16,16,128]{2,1,0:T(8,128)(2,1)} %sum_pieces.1), calls=%async_computation.3 | async-start | bytes 131072 | tf_op jit(solution)/shard_map/all_to_all | solution.py:38

commit v8 on v6

--- a/solution.py
+++ b/solution.py
@@ -172,7 +172,7 @@
         pltpu.make_async_copy(own, passages.at[pl.ds(0, OWN)], sems.at[2]),
         pltpu.make_async_copy(sib, passages.at[pl.ds(OWN, OWN)], sems.at[3]),
     ]
-    for copy in copies:
+    for copy in copies + late:
         copy.start()
     lines = [tiles[k, PIECES * ROWS : LINES, :].astype(F32) for k in range(X)]
     pos_name, pos_rest, names = [
@@ -201,7 +201,7 @@
         pltpu.make_async_copy(q_emb.at[mine], emb_mine, sems.at[4]),
         pltpu.make_async_copy(q_r.at[mine], r_mine, sems.at[5]),
     ]
-    for copy in late + kept:
+    for copy in kept:
         copy.start()
     line = lax.broadcasted_iota(jnp.int32, (ROWS, X * ROWS), 0)
     total = jnp.zeros((1, X * ROWS), F32)

time: 108 us -> 108 us (level)
  no operation moved by 1% of the time
where the time goes in v8:
time: 108 us; the launch traced here: 107 us
  starting transfers between devices  46.6 us (43%)
  Pallas kernels  28.1 us (26%)
  blocking collectives  19.3 us (18%)
  waiting for transfers between devices  11.8 us (11%)
    pallas_call x12, Pallas kernels, call(): pl.pallas_call(kernel, name=name, out_shape=out_shape, in_specs=in_specs,...  28.1 us
    all_to_all x3, starting transfers between devices, exchange(): return lax.all_to_all(value, axis, split_axis=0, concat_axis=0, tiled=True)  22.3 us
    all_to_all x2, blocking collectives, exchange(): return lax.all_to_all(value, axis, split_axis=0, concat_axis=0, tiled=True)  19.3 us
    all_to_all x3, waiting for transfers between devices, exchange(): return lax.all_to_all(value, axis, split_axis=0, concat_axis=0, tiled=True)  8.99 us
    ppermute x1, starting transfers between devices, body(): sibling = lax.ppermute(outgoing, 'c', SWAP)  7.47 us
    ppermute x1, starting transfers between devices, body(): g2 = lax.ppermute(g2, 'x', shift(X - 2))  4.32 us
    ppermute x1, starting transfers between devices, body(): w_there = lax.ppermute(w_there, 'c', SWAP)  3.71 us
    ppermute x1, starting transfers between devices, body(): g1 = lax.ppermute(g1, 'x', shift(X - 1))  3.42 us
  transfers between devices with their start and end apart: 9, of which 4 were waited for; matrix products, arithmetic and copies ran while one was open for 0% of the time, Pallas kernels for 14%

profile of v8, /device:TPU:1, one launch (start us, length us, event | category | flops | bytes accessed | tf_op | source)
XLA Modules:
  0.0 106.8 jit_solution(18325861152175690290)
XLA Ops:
  0.6 0.0 copy-start
  0.6 2.2 %pack.1 = bf16[4,1040,128]{2,1,0:T(8,128)(2,1)} custom-call(bf16[128,1024]{1,0:T(8,128)(2,1)} %queries.1, s32[1,128]{1,0:T(1,128)} %bitcast.4, s32[1,8]{1,0:T(1,128)} %pairs.1), custom_call_target="tpu_custom_call" | custom-call | bytes 1400000 | tf_op jit(solution)/shard_map/pack/pallas_call | solution.py:72
  2.8 4.9 %all-to-all-start = ((bf16[4,1040,128]{2,1,0:T(8,128)(2,1)}), bf16[4,1040,128]{2,1,0:T(8,128)(2,1)S(1)}, u32[]{:S(2)}, u32[]{:S(2)}) async-start(bf16[4,1040,128]{2,1,0:T(8,128)(2,1)} %pack.1), calls=%async_computation | async-start | bytes 2129920 | tf_op jit(solution)/shard_map/all_to_all | solution.py:38
  7.7 0.0 copy-done
  7.7 3.2 %passage_side.2 = (bf16[384,1024]{1,0:T(8,128)(2,1)}, f32[384,1]{1,0:T(8,128)}) custom-call(bf16[384,1024]{1,0:T(8,128)(2,1)} %own, bf16[1024,1024]{1,0:T(8,128)(2,1)S(1)} %copy-done), custom_call_target="tpu_custom_call" | custom-call | flops 1000 | bytes 1000 | tf_op jit(solution)/shard_map/passage_side/pallas_call | solution.py:72
  10.8 7.5 %collective-permute-start = (bf16[384,1024]{1,0:T(8,128)(2,1)}, bf16[384,1024]{1,0:T(8,128)(2,1)}, u32[]{:S(2)}, u32[]{:S(2)}) collective-permute-start(bf16[384,1024]{1,0:T(8,128)(2,1)} %own), channel_id=1, source_target_pairs={{0,1},{1,0},{2,3},{3,2},{4,5},{5,4},{6,7},{7,6},{8,9},{9,8},{10,11... | collective-permute-start | bytes 2359304 | tf_op jit(solution)/shard_map/ppermute | solution.py:464
  18.3 0.1 pad_add_fusion.place
  18.4 2.2 %collective-permute-done.passages.sib = bf16[384,1024]{1,0:T(8,128)(2,1)} collective-permute-done((bf16[384,1024]{1,0:T(8,128)(2,1)}, bf16[384,1024]{1,0:T(8,128)(2,1)}, u32[]{:S(2)}, u32[]{:S(2)}) %collective-permute-start) | collective-permute-done | bytes 786464 | tf_op jit(solution)/shard_map/ppermute | solution.py:464
  20.6 3.2 %passage_side.3 = (bf16[384,1024]{1,0:T(8,128)(2,1)}, f32[384,1]{1,0:T(8,128)}) custom-call(bf16[384,1024]{1,0:T(8,128)(2,1)} %collective-permute-done.passages.sib, bf16[1024,1024]{1,0:T(8,128)(2,1)S(1)} %copy-done), custom_call_target="tpu_custom_call" | custom-call | flops 1000 | bytes 1000 | tf_op jit(solution)/shard_map/passage_side/pallas_call | solution.py:72
  23.7 0.0 all-to-all-done.tiles
  23.7 0.0 copy-start.2
  23.7 0.0 copy-start.7
  23.7 4.3 %score_side.1 = (bf16[512,1024]{1,0:T(8,128)(2,1)S(1)}, f32[512,1]{1,0:T(8,128)S(1)}, f32[768,512]{1,0:T(8,128)S(1)}, f32[4,8,128]{2,1,0:T(8,128)S(1)}, s32[1,51...) custom-call(s32[2]{0:T(128)S(1)} %pad_add_fusion.place, ...), custom_call_target="tpu_custom_call" | custom-call | flops 2000000000 | bytes 8000000 | tf_op jit(solution)/shard_map/score_side/pallas_call | solution.py:72
  28.0 8.5 %all_to_all.25.recv = f32[4,8,128]{2,1,0:T(8,128)S(1)} all-to-all(f32[4,8,128]{2,1,0:T(8,128)S(1)} %get-tuple-element.44), channel_id=1, replica_groups=mesh['z'=16,'y'=4,'x'=4,'c'=2] {'x'}, dimensions={0} | all-to-all | bytes 32768 | tf_op jit(solution)/shard_map/all_to_all | solution.py:38
  36.5 0.0 copy-done.2
  36.5 0.0 copy-done.7
  36.5 4.9 %grad_side.1 = (f32[1,128]{1,0:T(1,128)}, bf16[128,1024]{1,0:T(8,128)(2,1)S(1)}, bf16[128,1024]{1,0:T(8,128)(2,1)S(1)}, bf16[128,1024]{1,0:T(8,128)(2,1)S(1)}, b...) custom-call(s32[2]{0:T(128)S(1)} %pad_add_fusion.place, ...), custom_call_target="tpu_custom_call" | custom-call | flops 3000000000 | bytes 14000000 | tf_op jit(solution)/shard_map/grad_side/pallas_call | solution.py:72
  41.4 0.0 copy-start.1
  41.4 0.0 copy-start.3
  41.4 0.0 copy-start.4
  41.4 0.0 copy-start.5
  41.4 0.0 copy-start.6
  41.4 3.7 %collective-permute-start.1 = (bf16[1024,512]{1,0:T(8,128)(2,1)S(1)}, bf16[1024,512]{1,0:T(8,128)(2,1)S(1)}, u32[]{:S(2)}, u32[]{:S(2)}) collective-permute-start(bf16[1024,512]{1,0:T(8,128)(2,1)S(1)} %get-tuple-element.60), channel_id=1, source_target_pairs={{0,1},{1,0},{2,3},{3,2},{4,5},{5,4},{6,7},{7,6},{8,9},{9,8},{10,11... | collective-permute-start | bytes 3145736 | tf_op jit(solution)/shard_map/ppermute | solution.py:475
  45.1 1.6 %weight_here.1.here = f32[1024,512]{1,0:T(8,128)S(1)} custom-call(bf16[1280,512]{1,0:T(8,128)(2,1)S(1)} %get-tuple-element.59.backs, bf16[512,1024]{1,0:T(8,128)(2,1)S(1)} %get-tuple-element.52.q_rows, bf16[768,1024]{1,0:T(8,128)(2,1)S(1)} %get-tuple-element.53.passages), custom_call_target="tpu_custom_call" | custom-call | flops 1350000000 | bytes 6000000 | tf_op jit(solution)/shard_map/weight_here/pallas_call | solution.py:72
  46.7 0.0 copy-done.1
  46.7 0.0 copy-done.3
  46.7 0.0 copy-done.4
  46.7 0.0 copy-done.5
  46.7 0.0 copy-done.6
  46.7 0.7 collective-permute-done.1.there
  47.4 1.1 spread.1
  48.5 3.7 %all-to-all-start.2 = ((bf16[16,16,16,128]{3,2,1,0:T(8,128)(2,1)}), bf16[16,16,16,128]{3,2,1,0:T(8,128)(2,1)S(1)}, u32[]{:S(2)}, u32[]{:S(2)}) async-start(bf16[16,16,16,128]{3,2,1,0:T(8,128)(2,1)} %spread.1), calls=%async_computation.2 | async-start | bytes 2097152 | tf_op jit(solution)/shard_map/all_to_all | solution.py:38
  52.1 2.3 %collective-permute-start.2 = (bf16[384,1024]{1,0:T(8,128)(2,1)}, bf16[384,1024]{1,0:T(8,128)(2,1)S(1)}, u32[]{:S(2)}, u32[]{:S(2)}) collective-permute-start(bf16[384,1024]{1,0:T(8,128)(2,1)} %copy-done.3), channel_id=1, source_target_pairs={{0,1},{1,0},{2,3},{3,2},{4,5},{5,4},{6,7},{7,6},{8,9},{9,8},{10,11... | collective-permute-start | bytes 2359304 | tf_op jit(solution)/shard_map/ppermute | solution.py:482
  54.4 3.4 %collective-permute-start.3 = (bf16[128,1024]{1,0:T(8,128)(2,1)}, bf16[128,1024]{1,0:T(8,128)(2,1)}, u32[]{:S(2)}, u32[]{:S(2)}) collective-permute-start(bf16[128,1024]{1,0:T(8,128)(2,1)} %copy-done.6), channel_id=1, source_target_pairs={{6,0},{0,2},{2,4},{4,6},{7,1},{1,3},{3,5},{5,7},{14,8},{8,10},{10,... | collective-permute-start | bytes 786440 | tf_op jit(solution)/shard_map/ppermute | solution.py:479
  57.9 4.3 %collective-permute-start.4 = (bf16[128,1024]{1,0:T(8,128)(2,1)}, bf16[128,1024]{1,0:T(8,128)(2,1)}, u32[]{:S(2)}, u32[]{:S(2)}) collective-permute-start(bf16[128,1024]{1,0:T(8,128)(2,1)} %copy-done.5), channel_id=1, source_target_pairs={{4,0},{6,2},{0,4},{2,6},{5,1},{7,3},{1,5},{3,7},{12,8},{14,10},{8,... | collective-permute-start | bytes 786440 | tf_op jit(solution)/shard_map/ppermute | solution.py:478
  62.2 3.1 %collective-permute-start.5 = (bf16[128,1024]{1,0:T(8,128)(2,1)}, bf16[128,1024]{1,0:T(8,128)(2,1)}, u32[]{:S(2)}, u32[]{:S(2)}) collective-permute-start(bf16[128,1024]{1,0:T(8,128)(2,1)} %copy-done.4), channel_id=1, source_target_pairs={{2,0},{4,2},{6,4},{0,6},{3,1},{5,3},{7,5},{1,7},{10,8},{12,10},{14... | collective-permute-start | bytes 786440 | tf_op jit(solution)/shard_map/ppermute | solution.py:480
  65.3 0.0 collective-permute-done.2.refs_1_
  65.3 3.6 %hidden_grad.2 = bf16[384,1024]{1,0:T(8,128)(2,1)} custom-call(bf16[384,1024]{1,0:T(8,128)(2,1)} %copy-done.1, bf16[384,1024]{1,0:T(8,128)(2,1)S(1)} %collective-permute-done.2.refs_1_, bf16[384,1024]{1,0:T(8,128)(2,1)} %get-tuple-element.41.emb_own.refs_2_, f32[384,1]{1,0:T(8,128)} %get-tuple-element.48.r_own.refs_3_, bf16[1024,1024]{1,0:T(8,128)(2,1)S(1)} %copy-done), custom_call_target="tpu_custom_call" | custom-call | flops 805306368 | bytes 5840000 | tf_op jit(solution)/shard_map/hidden_grad/pallas_call | solution.py:72
  68.9 0.3 all-to-all-done.2.pieces
  69.2 0.8 sum_pieces.1
  69.9 13.8 %all-to-all-start.3 = ((bf16[16,16,128]{2,1,0:T(8,128)(2,1)}), bf16[16,16,128]{2,1,0:T(8,128)(2,1)S(1)}, u32[]{:S(2)}, u32[]{:S(2)}) async-start(bf16[16,16,128]{2,1,0:T(8,128)(2,1)} %sum_pieces.1), calls=%async_computation.3 | async-start | bytes 131072 | tf_op jit(solution)/shard_map/all_to_all | solution.py:38
  83.8 0.0 collective-permute-done.3.refs_1_
  83.8 0.0 collective-permute-done.4.refs_2_
  83.8 0.0 collective-permute-done.5.refs_3_
  83.8 2.9 %hidden_grad.3 = bf16[128,1024]{1,0:T(8,128)(2,1)} custom-call(bf16[128,1024]{1,0:T(8,128)(2,1)S(1)} %get-tuple-element.65.refs_0_, bf16[128,1024]{1,0:T(8,128)(2,1)} %collective-permute-done.3.refs_1_, bf16[128,1024]{1,0:T(8,128)(2,1)} %collective-permute-done.4.refs_2_, bf16[128,1024]{1,0:T(8,128)(2,1)} %collective-permute-done.5.refs_3_, ...), custom_call_target="tpu_custom_call" | custom-call | flops 268435456 | bytes 3280000 | tf_op jit(solution)/shard_map/hidden_grad/pallas_call | solution.py:72
  86.7 8.7 %all-to-all-done.3.pieces = bf16[16,16,128]{2,1,0:T(8,128)(2,1)S(1)} async-done(((bf16[16,16,128]{2,1,0:T(8,128)(2,1)}), bf16[16,16,128]{2,1,0:T(8,128)(2,1)S(1)}, u32[]{:S(2)}, u32[]{:S(2)}) %all-to-all-start.3) | async-done | bytes 65568 | tf_op jit(solution)/shard_map/all_to_all | solution.py:38
  95.4 10.8 %all_to_all.26.pieces = f32[8,16,128]{2,1,0:T(8,128)S(1)} all-to-all(f32[8,16,128]{2,1,0:T(8,128)S(1)} %last_sum.1), channel_id=1, replica_groups=mesh['z'=16,'y'=4,'x'=4,'c'=2] {'x','c'}, dimensions={0} | all-to-all | bytes 131072 | tf_op jit(solution)/shard_map/all_to_all | solution.py:38
  106.2 0.6 lay.1
  (1 shorter events, 0.0 us)
Async XLA Ops:
  0.6 7.0 %copy-start = (bf16[1024,1024]{1,0:T(8,128)(2,1)S(1)}, bf16[1024,1024]{1,0:T(8,128)(2,1)}, u32[]{:S(2)}) copy-start(bf16[1024,1024]{1,0:T(8,128)(2,1)} %refs_6_) | copy-start | bytes 6291460
  2.8 20.9 %all-to-all-start = ((bf16[4,1040,128]{2,1,0:T(8,128)(2,1)}), bf16[4,1040,128]{2,1,0:T(8,128)(2,1)S(1)}, u32[]{:S(2)}, u32[]{:S(2)}) async-start(bf16[4,1040,128]{2,1,0:T(8,128)(2,1)} %pack.1), calls=%async_computation | async-start | bytes 2129920 | tf_op jit(solution)/shard_map/all_to_all | solution.py:38
  10.8 9.7 %collective-permute-start = (bf16[384,1024]{1,0:T(8,128)(2,1)}, bf16[384,1024]{1,0:T(8,128)(2,1)}, u32[]{:S(2)}, u32[]{:S(2)}) collective-permute-start(bf16[384,1024]{1,0:T(8,128)(2,1)} %own), channel_id=1, source_target_pairs={{0,1},{1,0},{2,3},{3,2},{4,5},{5,4},{6,7},{7,6},{8,9},{9,8},{10,11... | collective-permute-start | bytes 2359304 | tf_op jit(solution)/shard_map/ppermute | solution.py:464
  23.7 12.8 %copy-start.2 = (f32[384,1]{1,0:T(8,128)S(1)}, f32[384,1]{1,0:T(8,128)}, u32[]{:S(2)}) copy-start(f32[384,1]{1,0:T(8,128)} %get-tuple-element.48.r_own.refs_3_) | copy-start | bytes 4612
  23.7 12.8 %copy-start.7 = (f32[384,1]{1,0:T(8,128)S(1)}, f32[384,1]{1,0:T(8,128)}, u32[]{:S(2)}) copy-start(f32[384,1]{1,0:T(8,128)} %get-tuple-element.49.r_sib) | copy-start | bytes 4612
  41.4 5.3 %copy-start.1 = (bf16[384,1024]{1,0:T(8,128)(2,1)}, bf16[384,1024]{1,0:T(8,128)(2,1)S(1)}, u32[]{:S(2)}) copy-start(bf16[384,1024]{1,0:T(8,128)(2,1)S(1)} %get-tuple-element.62.refs_0_) | copy-start | bytes 2359300
  41.4 5.3 %copy-start.3 = (bf16[384,1024]{1,0:T(8,128)(2,1)}, bf16[384,1024]{1,0:T(8,128)(2,1)S(1)}, u32[]{:S(2)}) copy-start(bf16[384,1024]{1,0:T(8,128)(2,1)S(1)} %get-tuple-element.63) | copy-start | bytes 2359300
  41.4 5.3 %copy-start.4 = (bf16[128,1024]{1,0:T(8,128)(2,1)}, bf16[128,1024]{1,0:T(8,128)(2,1)S(1)}, u32[]{:S(2)}) copy-start(bf16[128,1024]{1,0:T(8,128)(2,1)S(1)} %get-tuple-element.68) | copy-start | bytes 786436
  41.4 5.3 %copy-start.5 = (bf16[128,1024]{1,0:T(8,128)(2,1)}, bf16[128,1024]{1,0:T(8,128)(2,1)S(1)}, u32[]{:S(2)}) copy-start(bf16[128,1024]{1,0:T(8,128)(2,1)S(1)} %get-tuple-element.67) | copy-start | bytes 786436
  41.4 5.3 %copy-start.6 = (bf16[128,1024]{1,0:T(8,128)(2,1)}, bf16[128,1024]{1,0:T(8,128)(2,1)S(1)}, u32[]{:S(2)}) copy-start(bf16[128,1024]{1,0:T(8,128)(2,1)S(1)} %get-tuple-element.66) | copy-start | bytes 786436
  41.4 6.0 %collective-permute-start.1 = (bf16[1024,512]{1,0:T(8,128)(2,1)S(1)}, bf16[1024,512]{1,0:T(8,128)(2,1)S(1)}, u32[]{:S(2)}, u32[]{:S(2)}) collective-permute-start(bf16[1024,512]{1,0:T(8,128)(2,1)S(1)} %get-tuple-element.60), channel_id=1, source_target_pairs={{0,1},{1,0},{2,3},{3,2},{4,5},{5,4},{6,7},{7,6},{8,9},{9,8},{10,11... | collective-permute-start | bytes 3145736 | tf_op jit(solution)/shard_map/ppermute | solution.py:475
  48.5 20.7 %all-to-all-start.2 = ((bf16[16,16,16,128]{3,2,1,0:T(8,128)(2,1)}), bf16[16,16,16,128]{3,2,1,0:T(8,128)(2,1)S(1)}, u32[]{:S(2)}, u32[]{:S(2)}) async-start(bf16[16,16,16,128]{3,2,1,0:T(8,128)(2,1)} %spread.1), calls=%async_computation.2 | async-start | bytes 2097152 | tf_op jit(solution)/shard_map/all_to_all | solution.py:38
  52.1 13.1 %collective-permute-start.2 = (bf16[384,1024]{1,0:T(8,128)(2,1)}, bf16[384,1024]{1,0:T(8,128)(2,1)S(1)}, u32[]{:S(2)}, u32[]{:S(2)}) collective-permute-start(bf16[384,1024]{1,0:T(8,128)(2,1)} %copy-done.3), channel_id=1, source_target_pairs={{0,1},{1,0},{2,3},{3,2},{4,5},{5,4},{6,7},{7,6},{8,9},{9,8},{10,11... | collective-permute-start | bytes 2359304 | tf_op jit(solution)/shard_map/ppermute | solution.py:482
  54.4 29.3 %collective-permute-start.3 = (bf16[128,1024]{1,0:T(8,128)(2,1)}, bf16[128,1024]{1,0:T(8,128)(2,1)}, u32[]{:S(2)}, u32[]{:S(2)}) collective-permute-start(bf16[128,1024]{1,0:T(8,128)(2,1)} %copy-done.6), channel_id=1, source_target_pairs={{6,0},{0,2},{2,4},{4,6},{7,1},{1,3},{3,5},{5,7},{14,8},{8,10},{10,... | collective-permute-start | bytes 786440 | tf_op jit(solution)/shard_map/ppermute | solution.py:479
  57.9 25.9 %collective-permute-start.4 = (bf16[128,1024]{1,0:T(8,128)(2,1)}, bf16[128,1024]{1,0:T(8,128)(2,1)}, u32[]{:S(2)}, u32[]{:S(2)}) collective-permute-start(bf16[128,1024]{1,0:T(8,128)(2,1)} %copy-done.5), channel_id=1, source_target_pairs={{4,0},{6,2},{0,4},{2,6},{5,1},{7,3},{1,5},{3,7},{12,8},{14,10},{8,... | collective-permute-start | bytes 786440 | tf_op jit(solution)/shard_map/ppermute | solution.py:478
  62.2 21.6 %collective-permute-start.5 = (bf16[128,1024]{1,0:T(8,128)(2,1)}, bf16[128,1024]{1,0:T(8,128)(2,1)}, u32[]{:S(2)}, u32[]{:S(2)}) collective-permute-start(bf16[128,1024]{1,0:T(8,128)(2,1)} %copy-done.4), channel_id=1, source_target_pairs={{2,0},{4,2},{6,4},{0,6},{3,1},{5,3},{7,5},{1,7},{10,8},{12,10},{14... | collective-permute-start | bytes 786440 | tf_op jit(solution)/shard_map/ppermute | solution.py:480
  69.9 25.4 %all-to-all-start.3 = ((bf16[16,16,128]{2,1,0:T(8,128)(2,1)}), bf16[16,16,128]{2,1,0:T(8,128)(2,1)S(1)}, u32[]{:S(2)}, u32[]{:S(2)}) async-start(bf16[16,16,128]{2,1,0:T(8,128)(2,1)} %sum_pieces.1), calls=%async_computation.3 | async-start | bytes 131072 | tf_op jit(solution)/shard_map/all_to_all | solution.py:38
